TPU v7x, 32 devices: a whole 2x2x4 slice. The times are simulated.
32 devices in a mesh: dp: 8 (over z, y), seq: 4 (over x, core).
Axes of the slice: x: 2, y: 2, z: 4, core: 2. Of those that a mesh axis runs over, the one named last changes fastest.
Arguments:
- tokens: bfloat16 [8, 1536, 896], P('dp', 'seq'), may hold values from -6 to 6
- doc_lengths: int32 [8, 5], P('dp'), may hold values from 96 to 960, as said below
- cotangent: bfloat16 [8, 1536, 896], P('dp', 'seq'), may hold values from -6 to 6
- norm_one: bfloat16 [896], P('seq'), may hold values from 0.5 to 1.5
- w_qkv: bfloat16 [896, 1152], P('seq'), may hold values from -0.1875 to 0.1875
- b_qkv: bfloat16 [1152], P('seq'), may hold values from -3 to 3
- w_out: bfloat16 [896, 896], P('seq'), may hold values from -1.5 to 1.5
- norm_two: bfloat16 [896], P('seq'), may hold values from 0.5 to 1.5
- w_gate: bfloat16 [896, 4864], P('seq'), may hold values from -0.1875 to 0.1875
- w_up: bfloat16 [896, 4864], P('seq'), may hold values from -0.1875 to 0.1875
- w_down: bfloat16 [4864, 896], P('seq'), may hold values from -0.078125 to 0.078125
Outputs:
- layer_out: bfloat16 [8, 1536, 896], P('dp', 'seq')
- grad_tokens: float32 [8, 1536, 896], P('dp', 'seq')
- grad_norm_one: float32 [896], P('seq')
- grad_w_qkv: float32 [896, 1152], P('seq')
- grad_b_qkv: float32 [1152], P('seq')
- grad_w_out: float32 [896, 896], P('seq')
- grad_norm_two: float32 [896], P('seq')
- grad_w_gate: float32 [896, 4864], P('seq')
- grad_w_up: float32 [896, 4864], P('seq')
- grad_w_down: float32 [4864, 896], P('seq')
Inputs may be any that keep to these rules, and one draw needn't show every extreme that they name: `doc_lengths`: each row packs 5 documents in order: the first two together hold 3 * (96) tokens, each between 96 and 192; the third holds 960; the fourth 384 // 4 and the fifth 384 // 2.
All inputs are finite; a program needn't handle non-finite values.
Results may differ from a plain program's by a relative error of at most 0.02.
Values may be sent and summed in bfloat16 or wider, within the bound.
No kernel may reach another device: no remote copies, remote signals or barrier semaphores. Data moves between devices by JAX's collectives and lax.ppermute only.
A program may use at most 192 MiB of HBM per device.

v0:
```python
import jax
import jax.numpy as jnp
from jax import lax
from jax.sharding import PartitionSpec as P

HEADS = 14
KV_HEADS = 2
HEAD_DIM = 64


EPSILON = 1e-06
ROPE_BASE = 1000000.0


def dot_rows(left, right):
    return lax.dot_general(
        left, right, (((0,), (0,)), ((), ())), preferred_element_type=jnp.float32
    )


def dot_last(left, right):
    return lax.dot_general(
        left, right, (((1,), (1,)), ((), ())), preferred_element_type=jnp.float32
    )


def locate(lengths, where_at):
    starts = jnp.cumsum(lengths) - lengths
    inside = where_at[:, None] >= starts[None, :]
    segment = jnp.sum(inside.astype(jnp.int32), axis=1) - 1
    opening = jnp.max(jnp.where(inside, starts[None, :], 0), axis=1)
    return (segment, where_at - opening)


def angles(places):
    half = HEAD_DIM // 2
    freqs = ROPE_BASE ** (-(jnp.arange(half, dtype=jnp.float32) * 2.0) / HEAD_DIM)
    turned = places.astype(jnp.float32)[:, None] * freqs[None, :]
    return (jnp.cos(turned)[:, None, :], jnp.sin(turned)[:, None, :])


def rotate(values, cosine, sine):
    half = values.shape[-1] // 2
    first = values[..., :half]
    second = values[..., half:]
    return jnp.concatenate(
        [first * cosine - second * sine, second * cosine + first * sine], axis=-1
    )


def unrotate(grads, cosine, sine):
    half = grads.shape[-1] // 2
    first = grads[..., :half]
    second = grads[..., half:]
    return jnp.concatenate(
        [first * cosine + second * sine, second * cosine - first * sine], axis=-1
    )


def norm_back(grad_hidden, normed, scale_rows, gain):
    scaled = grad_hidden * gain
    return scale_rows * (scaled - normed * jnp.mean(scaled * normed, axis=-1, keepdims=True))


def per_device(
    tokens, doc_lengths, cotangent, norm_one, w_qkv, b_qkv, w_out, norm_two, w_gate, w_up, w_down
):
    gain_one, full_qkv, full_bias, full_out, gain_two, full_gate, full_up, full_down = (
        lax.all_gather(norm_one, "seq", axis=0, tiled=True),
        lax.all_gather(w_qkv, "seq", axis=0, tiled=True),
        lax.all_gather(b_qkv, "seq", axis=0, tiled=True),
        lax.all_gather(w_out, "seq", axis=0, tiled=True),
        lax.all_gather(norm_two, "seq", axis=0, tiled=True),
        lax.all_gather(w_gate, "seq", axis=0, tiled=True),
        lax.all_gather(w_up, "seq", axis=0, tiled=True),
        lax.all_gather(w_down, "seq", axis=0, tiled=True),
    )
    inputs = tokens[0].astype(jnp.float32)
    rows = inputs.shape[0]
    length = rows * lax.axis_size("seq")
    index_all = jnp.arange(length, dtype=jnp.int32)
    segment_all, places_all = locate(doc_lengths[0], index_all)
    offset = lax.axis_index("seq") * rows
    index_own = offset + jnp.arange(rows, dtype=jnp.int32)
    segment_own = lax.dynamic_slice_in_dim(segment_all, offset, rows)
    places_own = lax.dynamic_slice_in_dim(places_all, offset, rows)
    allowed = (segment_own[:, None] == segment_all[None, :]) & (
        index_all[None, :] <= index_own[:, None]
    )
    query_width = HEADS * HEAD_DIM
    key_width = KV_HEADS * HEAD_DIM
    group_size = HEADS // KV_HEADS
    scale = HEAD_DIM ** (-0.5)
    gain_one_f = gain_one.astype(jnp.float32)
    scale_one = lax.rsqrt(jnp.mean(inputs * inputs, axis=-1, keepdims=True) + EPSILON)
    normed_one = inputs * scale_one
    hidden_one = (normed_one * gain_one_f).astype(jnp.bfloat16)
    project = jnp.dot(hidden_one, full_qkv, preferred_element_type=jnp.float32) + full_bias.astype(
        jnp.float32
    )
    cosine, sine = angles(places_own)
    queries = rotate(project[:, :query_width].reshape(rows, HEADS, HEAD_DIM), cosine, sine).astype(
        jnp.bfloat16
    )
    keys = rotate(
        project[:, query_width : query_width + key_width].reshape(rows, KV_HEADS, HEAD_DIM),
        cosine,
        sine,
    )
    keys = keys.reshape(rows, key_width).astype(jnp.bfloat16)
    values = project[:, query_width + key_width :].astype(jnp.bfloat16)
    keys_all, values_all = (
        lax.all_gather(keys, "seq", axis=0, tiled=True),
        lax.all_gather(values, "seq", axis=0, tiled=True),
    )
    key_heads = keys_all.reshape(length, KV_HEADS, HEAD_DIM).transpose(1, 0, 2)
    value_heads = values_all.reshape(length, KV_HEADS, HEAD_DIM).transpose(1, 0, 2)
    query_heads = queries.transpose(1, 0, 2)
    group_ids = jnp.arange(HEADS, dtype=jnp.int32) // group_size

    def head_forward(items):
        query, group = items
        key = lax.dynamic_index_in_dim(key_heads, group, 0, keepdims=False)
        value = lax.dynamic_index_in_dim(value_heads, group, 0, keepdims=False)
        scores = jnp.where(allowed, dot_last(query, key) * scale, -1e30)
        top = jnp.max(scores, axis=-1, keepdims=True)
        weights = jnp.exp(scores - top)
        total = jnp.sum(weights, axis=-1, keepdims=True)
        probs = (weights / total).astype(jnp.bfloat16)
        mixed_head = jnp.dot(probs, value, preferred_element_type=jnp.float32).astype(jnp.bfloat16)
        return (mixed_head, (top + jnp.log(total))[:, 0])

    mixed_heads, log_totals = lax.map(head_forward, (query_heads, group_ids))
    mixed = mixed_heads.transpose(1, 0, 2).reshape(rows, query_width)
    residual = inputs + jnp.dot(mixed, full_out, preferred_element_type=jnp.float32)
    gain_two_f = gain_two.astype(jnp.float32)
    scale_two = lax.rsqrt(jnp.mean(residual * residual, axis=-1, keepdims=True) + EPSILON)
    normed_two = residual * scale_two
    hidden_two = (normed_two * gain_two_f).astype(jnp.bfloat16)
    gate = jnp.dot(hidden_two, full_gate, preferred_element_type=jnp.float32)
    upward = jnp.dot(hidden_two, full_up, preferred_element_type=jnp.float32)
    sigma = jax.nn.sigmoid(gate)
    active = gate * sigma
    product = (active * upward).astype(jnp.bfloat16)
    layer_out = (residual + jnp.dot(product, full_down, preferred_element_type=jnp.float32)).astype(
        jnp.bfloat16
    )
    gain_one, full_qkv, full_bias, full_out, gain_two, full_gate, full_up, full_down = (
        lax.all_gather(norm_one, "seq", axis=0, tiled=True),
        lax.all_gather(w_qkv, "seq", axis=0, tiled=True),
        lax.all_gather(b_qkv, "seq", axis=0, tiled=True),
        lax.all_gather(w_out, "seq", axis=0, tiled=True),
        lax.all_gather(norm_two, "seq", axis=0, tiled=True),
        lax.all_gather(w_gate, "seq", axis=0, tiled=True),
        lax.all_gather(w_up, "seq", axis=0, tiled=True),
        lax.all_gather(w_down, "seq", axis=0, tiled=True),
    )
    gain_one_f = gain_one.astype(jnp.float32)
    gain_two_f = gain_two.astype(jnp.float32)
    grad_out_b = cotangent[0]
    grad_out = grad_out_b.astype(jnp.float32)
    grad_down = dot_rows(product, grad_out_b)
    grad_product = dot_last(grad_out_b, full_down)
    grad_gate_b = (grad_product * upward * sigma * (1.0 + gate * (1.0 - sigma))).astype(
        jnp.bfloat16
    )
    grad_up_b = (grad_product * active).astype(jnp.bfloat16)
    grad_gate_w = dot_rows(hidden_two, grad_gate_b)
    grad_up_w = dot_rows(hidden_two, grad_up_b)
    grad_hidden_two = dot_last(grad_gate_b, full_gate) + dot_last(grad_up_b, full_up)
    grad_gain_two = jnp.sum(grad_hidden_two * normed_two, axis=0)
    grad_residual = grad_out + norm_back(grad_hidden_two, normed_two, scale_two, gain_two_f)
    grad_residual_b = grad_residual.astype(jnp.bfloat16)
    grad_out_w = dot_rows(mixed, grad_residual_b)
    grad_mixed = dot_last(grad_residual_b, full_out).astype(jnp.bfloat16)
    grad_heads = grad_mixed.reshape(rows, HEADS, HEAD_DIM).transpose(1, 0, 2)

    def head_backward(items):
        query, grad_head, log_total, group = items
        key = lax.dynamic_index_in_dim(key_heads, group, 0, keepdims=False)
        value = lax.dynamic_index_in_dim(value_heads, group, 0, keepdims=False)
        scores = jnp.where(allowed, dot_last(query, key) * scale, -1e30)
        probs = jnp.exp(scores - log_total[:, None])
        grad_probs = dot_last(grad_head, value)
        centre = jnp.sum(grad_probs * probs, axis=-1, keepdims=True)
        grad_scores = (probs * (grad_probs - centre)).astype(jnp.bfloat16)
        grad_query = jnp.dot(grad_scores, key, preferred_element_type=jnp.float32) * scale
        grad_key = dot_rows(grad_scores, query) * scale
        grad_value = dot_rows(probs.astype(jnp.bfloat16), grad_head)
        return (grad_query, grad_key, grad_value)

    grad_q_heads, grad_k_heads, grad_v_heads = lax.map(
        head_backward, (query_heads, grad_heads, log_totals, group_ids)
    )
    grad_keys = jnp.sum(grad_k_heads.reshape(KV_HEADS, group_size, length, HEAD_DIM), axis=1)
    grad_keys = grad_keys.transpose(1, 0, 2).reshape(length, key_width)
    grad_values = jnp.sum(grad_v_heads.reshape(KV_HEADS, group_size, length, HEAD_DIM), axis=1)
    grad_values = grad_values.transpose(1, 0, 2).reshape(length, key_width)
    grad_keys_own, grad_values_own = (
        lax.psum_scatter(
            grad_keys.astype(jnp.bfloat16), "seq", scatter_dimension=0, tiled=True
        ).astype(jnp.float32),
        lax.psum_scatter(
            grad_values.astype(jnp.bfloat16), "seq", scatter_dimension=0, tiled=True
        ).astype(jnp.float32),
    )
    grad_query_pre = unrotate(grad_q_heads.transpose(1, 0, 2), cosine, sine).reshape(
        rows, query_width
    )
    grad_key_pre = unrotate(grad_keys_own.reshape(rows, KV_HEADS, HEAD_DIM), cosine, sine).reshape(
        rows, key_width
    )
    grad_project = jnp.concatenate([grad_query_pre, grad_key_pre, grad_values_own], axis=-1).astype(
        jnp.bfloat16
    )
    grad_qkv_w = dot_rows(hidden_one, grad_project)
    grad_bias = jnp.sum(grad_project.astype(jnp.float32), axis=0)
    grad_hidden_one = dot_last(grad_project, full_qkv)
    grad_gain_one = jnp.sum(grad_hidden_one * normed_one, axis=0)
    grad_inputs = grad_residual + norm_back(grad_hidden_one, normed_one, scale_one, gain_one_f)
    sliced = (
        lax.psum_scatter(
            grad_gain_one.astype(jnp.bfloat16), "seq", scatter_dimension=0, tiled=True
        ).astype(jnp.float32),
        lax.psum_scatter(
            grad_qkv_w.astype(jnp.bfloat16), "seq", scatter_dimension=0, tiled=True
        ).astype(jnp.float32),
        lax.psum_scatter(
            grad_bias.astype(jnp.bfloat16), "seq", scatter_dimension=0, tiled=True
        ).astype(jnp.float32),
        lax.psum_scatter(
            grad_out_w.astype(jnp.bfloat16), "seq", scatter_dimension=0, tiled=True
        ).astype(jnp.float32),
        lax.psum_scatter(
            grad_gain_two.astype(jnp.bfloat16), "seq", scatter_dimension=0, tiled=True
        ).astype(jnp.float32),
        lax.psum_scatter(
            grad_gate_w.astype(jnp.bfloat16), "seq", scatter_dimension=0, tiled=True
        ).astype(jnp.float32),
        lax.psum_scatter(
            grad_up_w.astype(jnp.bfloat16), "seq", scatter_dimension=0, tiled=True
        ).astype(jnp.float32),
        lax.psum_scatter(
            grad_down.astype(jnp.bfloat16), "seq", scatter_dimension=0, tiled=True
        ).astype(jnp.float32),
    )
    summed = (
        lax.psum(sliced[0].astype(jnp.bfloat16), "dp").astype(jnp.float32),
        lax.psum(sliced[1].astype(jnp.bfloat16), "dp").astype(jnp.float32),
        lax.psum(sliced[2].astype(jnp.bfloat16), "dp").astype(jnp.float32),
        lax.psum(sliced[3].astype(jnp.bfloat16), "dp").astype(jnp.float32),
        lax.psum(sliced[4].astype(jnp.bfloat16), "dp").astype(jnp.float32),
        lax.psum(sliced[5].astype(jnp.bfloat16), "dp").astype(jnp.float32),
        lax.psum(sliced[6].astype(jnp.bfloat16), "dp").astype(jnp.float32),
        lax.psum(sliced[7].astype(jnp.bfloat16), "dp").astype(jnp.float32),
    )
    return (
        layer_out[None],
        grad_inputs[None],
        summed[0],
        summed[1],
        summed[2],
        summed[3],
        summed[4],
        summed[5],
        summed[6],
        summed[7],
    )


def solution(mesh):
    return jax.shard_map(
        per_device,
        mesh=mesh,
        in_specs=(
            P("dp", "seq", None),
            P("dp", None),
            P("dp", "seq", None),
            P("seq"),
            P("seq", None),
            P("seq"),
            P("seq", None),
            P("seq"),
            P("seq", None),
            P("seq", None),
            P("seq", None),
        ),
        out_specs=(
            P("dp", "seq", None),
            P("dp", "seq", None),
            P("seq"),
            P("seq", None),
            P("seq"),
            P("seq", None),
            P("seq"),
            P("seq", None),
            P("seq", None),
            P("seq", None),
        ),
        check_vma=False,
    )
```

profile of v0, /device:TPU:0, one launch (start us, length us, event | category | flops | bytes accessed | tf_op | source)
XLA Modules:
  0.0 1057.6 jit_solution(7982948748047595327)
XLA Ops:
  14.4 8.5 all-reduce.9
  24.5 10.3 all-gather.6.cloned.1.call-done
  34.8 2.8 convolution_add_fusion
  41.3 8.2 all_gather.40
  50.0 8.7 all_gather.41
  60.0 116.8 %while.28 = (s32[]{:T(128)}, bf16[14,384,64]{1,2,0:T(8,128)(2,1)}, f32[14,384]{1,0:T(8,128)}, bf16[14,384,64]{2,1,0:T(8,128)(2,1)}, s32[14]{0:T(128)S(1)}, /*ind...) while((s32[]{:T(128)}, bf16[14,384,64]{1,2,0:T(8,128)(2,1)}, ...), condition=%wide.region_7.8_spmd.clone, body=%wide.region_4.7_spmd.clone.sunk | while | flops 157507200 | bytes 8043703 | solution.py:133
  176.8 2.9 multiply_reduce_fusion.3
  180.9 9.5 fusion.76
  190.5 12.3 %fusion.77 = f32[384,4864]{1,0:T(8,128)} fusion(bf16[384,896]{1,0:T(8,128)(2,1)} %copy-done.13, bf16[896,4864]{1,0:T(8,128)(2,1)} %all-gather.12.cloned.1.call-done), kind=kOutput, calls=%fused_computation.139 | convolution fusion | flops 3347054592 | bytes 16875520 | tf_op jit(solution)/shard_map/dot_general | solution.py:141
  202.7 40.9 %all-gather.14.cloned.1.call-done = bf16[4864,896]{1,0:T(8,128)(2,1)} async-done(((bf16[1216,896]{1,0:T(8,128)(2,1)}), bf16[4864,896]{1,0:T(8,128)(2,1)}) %all-gather.14.cloned.1.call-update) | async-done | bytes 8716304 | tf_op jit(solution)/shard_map/all_gather | solution.py:76
  243.6 13.6 %multiply_convert_fusion.1 = (bf16[384,4864]{1,0:T(8,128)(2,1)S(1)}, bf16[384,4864]{1,0:T(8,128)(2,1)}, bf16[384,4864]{1,0:T(8,128)(2,1)}) fusion(f32[384,4864]{1,0:T(8,128)} %fusion.76, f32[384,4864]{1,0:T(8,128)} %fusion.77, bf16[4864,896]{1,0:T(8,128)(2,1)} %all-gather.14.cloned.1.call-done, bf16[1,384,896]{2,1,0:T(8,128)(2,1)S(1)} %copy-done.10), kind=kOutput, calls=%fused_computation.64 | convolution fusion | flops 3375071232 | bytes 35553280 | tf_op jit(solution)/shard_map/dot_general | solution.py:22
  257.3 11.3 %fusion.78 = f32[384,896]{1,0:T(8,128)S(1)} fusion(bf16[384,4864]{1,0:T(8,128)(2,1)} %get-tuple-element.336, bf16[896,4864]{1,0:T(8,128)(2,1)} %all-gather.10.cloned.1.call-done), kind=kOutput, calls=%fused_computation.140 | convolution fusion | flops 3347054592 | bytes 13828096 | tf_op jit(solution)/shard_map/dot_general | solution.py:22
  268.6 4.8 multiply_reduce_fusion.1
  279.4 164.9 %while.29 = (s32[]{:T(128)}, f32[14,384,64]{1,2,0:T(8,128)}, f32[14,1536,64]{1,2,0:T(8,128)}, f32[14,1536,64]{1,2,0:T(8,128)}, bf16[14,384,64]{2,1,0:T(8,128)(2,...) while((s32[]{:T(128)}, f32[14,384,64]{1,2,0:T(8,128)}, ...), condition=%wide.region_12.13_spmd.clone, body=%wide.region_10.12_spmd.clone.sunk | while | flops 384687744 | bytes 20078292 | solution.py:192
  444.3 3.1 reduce_sum.115
  448.5 3.2 reduce_sum.116
  456.9 12.5 %reduce-scatter.22.cloned.1.call-done = bf16[384,128]{1,0:T(8,128)(2,1)} async-done(((bf16[1536,128]{1,0:T(8,128)(2,1)}), bf16[384,128]{1,0:T(8,128)(2,1)}) %reduce-scatter.22.cloned.1.call-update) | async-done | bytes 98320
  470.4 22.9 %reduce-scatter.24.cloned.1.call-done = bf16[384,128]{1,0:T(8,128)(2,1)} async-done(((bf16[1536,128]{1,0:T(8,128)(2,1)}), bf16[384,128]{1,0:T(8,128)(2,1)}) %reduce-scatter.24.cloned.1.call-update) | async-done | bytes 98320
  495.0 2.8 convolution_convert_fusion.3
  498.9 10.2 convolution_convert_fusion.2
  509.1 10.2 convolution_convert_fusion.1
  520.4 9.6 convolution_convert_fusion
  530.2 28.2 %reduce-scatter.12.cloned.1.call-done = bf16[224,1152]{1,0:T(8,128)(2,1)} async-done(((bf16[896,1152]{1,0:T(8,128)(2,1)}), bf16[224,1152]{1,0:T(8,128)(2,1)}) %reduce-scatter.12.cloned.1.call-update) | async-done | bytes 516112 | tf_op jit(solution)/shard_map/reduce_scatter | solution.py:225
  558.4 76.2 %reduce-scatter.16.cloned.1.call-done = bf16[224,4864]{1,0:T(8,128)(2,1)} async-done(((bf16[896,4864]{1,0:T(8,128)(2,1)}), bf16[224,4864]{1,0:T(8,128)(2,1)}) %reduce-scatter.16.cloned.1.call-update) | async-done | bytes 2179088 | tf_op jit(solution)/shard_map/reduce_scatter | solution.py:237
  634.6 76.4 %reduce-scatter.18.cloned.1.call-done = bf16[224,4864]{1,0:T(8,128)(2,1)} async-done(((bf16[896,4864]{1,0:T(8,128)(2,1)}), bf16[224,4864]{1,0:T(8,128)(2,1)}) %reduce-scatter.18.cloned.1.call-update) | async-done | bytes 2179088 | tf_op jit(solution)/shard_map/reduce_scatter | solution.py:240
  711.0 76.2 %reduce-scatter.20.cloned.1.call-done = bf16[1216,896]{1,0:T(8,128)(2,1)} async-done(((bf16[4864,896]{1,0:T(8,128)(2,1)}), bf16[1216,896]{1,0:T(8,128)(2,1)}) %reduce-scatter.20.cloned.1.call-update) | async-done | bytes 2179088 | tf_op jit(solution)/shard_map/reduce_scatter | solution.py:243
  788.7 9.6 fusion.63
  800.5 6.3 all-reduce.8
  807.1 22.8 %all-reduce.6 = (bf16[224]{0:T(256)(128)(2,1)S(1)}, bf16[288]{0:T(512)(128)(2,1)S(1)}, bf16[224]{0:T(256)(128)(2,1)S(1)}) all-reduce(bf16[224]{0:T(256)(128)(2,1)S(1)} %dynamic-slice.4, bf16[288]{0:T(512)(128)(2,1)S(1)} %dynamic-slice.6, bf16[224]{0:T(256)(128)(2,1)S(1)} %dynamic-slice.8), channel_id=1, replica_groups=mesh['dp'=8,'seq'=4] {'dp'}, use_global_device_ids=true, to_apply=%region_20.21 | all-reduce | flops 736 | bytes 2944 | tf_op jit(solution)/shard_map/psum | solution.py:248
  833.0 206.6 %all-reduce.12.cloned.1.call-done = (bf16[224,1152]{1,0:T(8,128)(2,1)}, bf16[224,896]{1,0:T(8,128)(2,1)}, bf16[224,4864]{1,0:T(8,128)(2,1)}, bf16[224,4864]{1,0:T(8,128)(2,1)}, bf16[1216,896]{1,0:T(8,128)(2,1)}) async-done(((bf16[224,1152]{1,0:T(8,128)(2,1)}, bf16[224,896]{1,0:T(8,128)(2,1)}, bf16[224,4864]{1,0:T(8,128)(2,1)}, bf16[224,4864]{1,0:T(8,128)(2,1)}, bf16[1216,896]{1,0:T(8,128)(2,1)}), ...) | async-done | bytes 7454736 | tf_op jit(solution)/shard_map/psum | solution.py:249
  1039.7 4.1 convert_element_type.185
  1043.8 2.3 convert_element_type.187
  (376 shorter events, 267.9 us)
Async XLA Ops:
  7.2 27.6 %all-gather.6.cloned.1.call-start = ((), (), s32[]{:S(2)}) async-start(), calls=%async_computation.7 | async-start | bytes 2580480 | tf_op jit(solution)/shard_map/all_gather | solution.py:70
  7.9 168.9 %all-gather.8.cloned.1.call-start = ((), (), s32[]{:S(2)}) async-start(), calls=%async_computation.8 | async-start | bytes 2007040 | tf_op jit(solution)/shard_map/all_gather | solution.py:72
  8.7 171.3 %all-gather.10.cloned.1.call-start = ((), (), s32[]{:S(2)}) async-start(), calls=%async_computation.9 | async-start | bytes 10895360 | tf_op jit(solution)/shard_map/all_gather | solution.py:74
  9.4 4.5 copy-start.29
  9.4 4.8 copy-start.24
  9.4 13.5 %copy-start.3 = (bf16[1,384,896]{2,1,0:T(8,128)(2,1)S(1)}, bf16[1,384,896]{2,1,0:T(8,128)(2,1)}, u32[]{:S(2)}) copy-start(bf16[1,384,896]{2,1,0:T(8,128)(2,1)} %param.15) | copy-start | bytes 2064388
  9.5 13.7 %copy-start.30 = (s32[1,5]{1,0:T(1,128)S(1)}, s32[1,5]{1,0:T(1,128)}, u32[]{:S(2)}) copy-start(s32[1,5]{1,0:T(1,128)} %param.16) | copy-start | bytes 64
  9.5 181.0 %all-gather.12.cloned.1.call-start = ((), (), s32[]{:S(2)}) async-start(), calls=%async_computation.10 | async-start | bytes 10895360 | tf_op jit(solution)/shard_map/all_gather | solution.py:75
  10.0 233.6 %all-gather.14.cloned.1.call-start = ((), (), s32[]{:S(2)}) async-start(), calls=%async_computation.11 | async-start | bytes 10895360 | tf_op jit(solution)/shard_map/all_gather | solution.py:76
  10.6 458.8 %reduce-scatter.22.cloned.1.call-start = ((), (), s32[]{:S(2)}) async-start(), calls=%async_computation.17 | async-start | bytes 491520
  23.2 14.4 %copy-start.19 = (f32[384]{0:T(512)}, f32[384]{0:T(512)S(1)}, u32[]{:S(2)}) copy-start(f32[384]{0:T(512)S(1)} %add_rsqrt_fusion.1) | copy-start | bytes 4612
  41.3 18.7 %copy-start.22 = (s32[384]{0:T(512)S(1)}, s32[384]{0:T(512)}, u32[]{:S(2)}) copy-start(s32[384]{0:T(512)} %iota_add_fusion) | copy-start | bytes 4612
  41.3 18.7 %copy-start.23 = (s32[384]{0:T(512)S(1)}, s32[384]{0:T(512)}, u32[]{:S(2)}) copy-start(s32[384]{0:T(512)} %dynamic_slice.41) | copy-start | bytes 4612
  41.3 18.7 %copy-start.31 = (s32[14]{0:T(128)S(1)}, s32[14]{0:T(128)}, u32[]{:S(2)}) copy-start(s32[14]{0:T(128)} %and_select_fusion) | copy-start | bytes 172
  179.7 88.8 %copy-start.1 = (f32[384,896]{1,0:T(8,128)}, f32[384,896]{1,0:T(8,128)S(1)}, u32[]{:S(2)}) copy-start(f32[384,896]{1,0:T(8,128)S(1)} %get-tuple-element.351) | copy-start | bytes 4128772
  190.4 53.2 %copy-start.10 = (bf16[1,384,896]{2,1,0:T(8,128)(2,1)S(1)}, bf16[1,384,896]{2,1,0:T(8,128)(2,1)}, u32[]{:S(2)}) copy-start(bf16[1,384,896]{2,1,0:T(8,128)(2,1)} %param.17) | copy-start | bytes 2064388
  257.3 11.3 %copy-start.32 = (bf16[384,4864]{1,0:T(8,128)(2,1)}, bf16[384,4864]{1,0:T(8,128)(2,1)S(1)}, u32[]{:S(2)}) copy-start(bf16[384,4864]{1,0:T(8,128)(2,1)S(1)} %get-tuple-element.335) | copy-start | bytes 11206660
  257.3 11.3 %copy-start.25 = (bf16[896,4864]{1,0:T(8,128)(2,1)S(1)}, bf16[896,4864]{1,0:T(8,128)(2,1)}, u32[]{:S(2)}) copy-start(bf16[896,4864]{1,0:T(8,128)(2,1)} %all-gather.12.cloned.1.call-done) | copy-start | bytes 26148868
  448.4 44.9 %reduce-scatter.24.cloned.1.call-start = ((), (), s32[]{:S(2)}) async-start(), calls=%async_computation.18 | async-start | bytes 491520
  448.5 4.4 copy-start.12
  452.6 77.5 %reduce-scatter.14.cloned.1.call-start = ((), (), s32[]{:S(2)}) async-start(), calls=%async_computation.13 | async-start | bytes 2007040 | tf_op jit(solution)/shard_map/reduce_scatter | solution.py:231
  455.1 103.3 %reduce-scatter.12.cloned.1.call-start = ((), (), s32[]{:S(2)}) async-start(), calls=%async_computation.12 | async-start | bytes 2580480 | tf_op jit(solution)/shard_map/reduce_scatter | solution.py:225
  455.1 39.9 %copy-start.4 = (bf16[1,384,896]{2,1,0:T(8,128)(2,1)S(1)}, bf16[1,384,896]{2,1,0:T(8,128)(2,1)}, u32[]{:S(2)}) copy-start(bf16[1,384,896]{2,1,0:T(8,128)(2,1)} %param.15) | copy-start | bytes 2064388
  455.2 39.8 %copy-start.20 = (f32[384]{0:T(512)S(1)}, f32[384]{0:T(512)}, u32[]{:S(2)}) copy-start(f32[384]{0:T(512)} %copy-done.19) | copy-start | bytes 4612
  456.9 40.9 %copy-start.5 = (bf16[384,14,64]{0,2,1:T(8,128)(2,1)}, bf16[384,14,64]{0,2,1:T(8,128)(2,1)S(1)}, u32[]{:S(2)}) copy-start(bf16[384,14,64]{0,2,1:T(8,128)(2,1)S(1)} %pad_maximum_fusion.1) | copy-start | bytes 2064388
  497.8 136.8 %reduce-scatter.16.cloned.1.call-start = ((), (), s32[]{:S(2)}) async-start(), calls=%async_computation.14 | async-start | bytes 10895360 | tf_op jit(solution)/shard_map/reduce_scatter | solution.py:237
  509.1 201.9 %reduce-scatter.18.cloned.1.call-start = ((), (), s32[]{:S(2)}) async-start(), calls=%async_computation.15 | async-start | bytes 10895360 | tf_op jit(solution)/shard_map/reduce_scatter | solution.py:240
  519.4 267.9 %reduce-scatter.20.cloned.1.call-start = ((), (), s32[]{:S(2)}) async-start(), calls=%async_computation.16 | async-start | bytes 10895360 | tf_op jit(solution)/shard_map/reduce_scatter | solution.py:243
  530.1 509.6 %all-reduce.12.cloned.1.call-start = ((), (), s32[]{:S(2)}) async-start(), calls=%async_computation.19 | async-start | bytes 14909440 | tf_op jit(solution)/shard_map/psum | solution.py:249
  788.7 9.7 copy-start.6
  788.7 9.7 copy-start.18
  788.7 9.9 copy-start.26
  (15 other events, 33.2 us)
Sparse Core Ops, SparseCore 0:
  9.6 25.1 all-gather.5
  36.4 22.2 all-gather.7
  60.2 60.1 all-gather.9
  121.8 60.1 all-gather.11
  183.4 60.1 all-gather.13
  448.5 20.8 reduce-scatter.21
  472.5 20.8 reduce-scatter.23
  495.9 28.3 reduce-scatter.13
  527.1 31.2 reduce-scatter.11
  560.8 73.7 reduce-scatter.15
  637.2 73.7 reduce-scatter.17
  713.5 73.7 reduce-scatter.19
  792.2 247.4 all-reduce.11
where the time goes:
time: 1070 us; the launch traced here: 1060 us
  waiting for transfers between devices  554 us (52%)
  matrix products  277 us (26%)
  local copies, waits for them, and re-layouts  62.1 us (6%)
  loops' own time  54.9 us (5%)
  blocking collectives  54.5 us (5%)
  other arithmetic  37.2 us (3%)
  between operations  17.6 us (2%)
    psum x1, waiting for transfers between devices, per_device(): lax.psum(sliced[1].astype(jnp.bfloat16), 'dp').astype(jnp.float32)  207 us
    dot_general x47, matrix products, dot_last(): lax.dot_general(left, right, (((1,), (1,)), ((), ())), preferred_element_...  102 us
    dot_general x33, matrix products, dot_rows(): lax.dot_general(left, right, (((0,), (0,)), ((), ())), preferred_element_...  89.8 us
    reduce_scatter x1, waiting for transfers between devices, per_device(): lax.psum_scatter(grad_up_w.astype(jnp.bfloat16), 'seq', scatter_dimension...  76.4 us
    reduce_scatter x1, waiting for transfers between devices, per_device(): lax.psum_scatter(grad_down.astype(jnp.bfloat16), 'seq', scatter_dimension...  76.2 us
    reduce_scatter x1, waiting for transfers between devices, per_device(): lax.psum_scatter(grad_gate_w.astype(jnp.bfloat16), 'seq', scatter_dimensi...  76.2 us
    all_gather x1, waiting for transfers between devices, per_device(): lax.all_gather(w_down, 'seq', axis=0, tiled=True)  40.9 us
    unnamed x15, waiting for transfers between devices  38.7 us
  transfers between devices with their start and end apart: 13, of which 9 were waited for; matrix products, arithmetic and copies ran while one was open for 17% of the time, Pallas kernels for 0%

commit v1 on v0

v1 whole, which is shorter than its diff:
```python
import functools

import jax
import jax.numpy as jnp
from jax import lax
from jax.experimental import pallas as pl
from jax.experimental.pallas import tpu as pltpu
from jax.sharding import PartitionSpec as P

HEADS = 14
KV_HEADS = 2
HEAD_DIM = 64
GROUP = HEADS // KV_HEADS
EPSILON = 1e-06
ROPE_BASE = 1000000.0
SCALE = HEAD_DIM ** (-0.5)
QB = 128
KB = 256
BF16 = jnp.bfloat16
F32 = jnp.float32


def dot_rows(left, right):
    return lax.dot_general(left, right, (((0,), (0,)), ((), ())), preferred_element_type=F32)


def dot_last(left, right):
    return lax.dot_general(left, right, (((1,), (1,)), ((), ())), preferred_element_type=F32)


def dot(left, right):
    return jnp.dot(left, right, preferred_element_type=F32)


def swap(x, axis, mask):
    return lax.ppermute(x, axis, [(i, i ^ mask) for i in range(lax.axis_size(axis))])


def after(x, *deps):
    return lax.optimization_barrier((x, *deps))[0]


def pick(x, index):
    return lax.dynamic_index_in_dim(x, index, 0, keepdims=False)


def bits_down(n):
    bits = []
    b = n // 2
    while b:
        bits.append(b)
        b //= 2
    return bits


def gather_rel(x, axis):
    blocks = {0: x}
    for b in bits_down(lax.axis_size(axis)):
        blocks.update({r ^ b: swap(v, axis, b) for r, v in list(blocks.items())})
    return blocks


def scatter_rel(parts, axis):
    parts = dict(parts)
    for b in reversed(bits_down(lax.axis_size(axis))):
        kept = {}
        for r in [r for r in parts if not r & b]:
            kept[r] = (parts[r].astype(F32) + swap(parts[r ^ b], axis, b).astype(F32)).astype(BF16)
        parts = kept
    return parts[0]


def place(blocks, index):
    rows = blocks[0].shape[0]
    out = jnp.zeros((rows * len(blocks),) + blocks[0].shape[1:], blocks[0].dtype)
    for r, v in blocks.items():
        out = lax.dynamic_update_slice_in_dim(out, v, (index ^ r) * rows, 0)
    return out


def masks(start_ref, first_query, first_key):
    key = first_key + lax.broadcasted_iota(jnp.int32, (KB, QB), 0)
    query = first_query + lax.broadcasted_iota(jnp.int32, (KB, QB), 1)
    fine = (key >= start_ref[...]) & (key <= query)
    bias = jnp.where(fine, 0.0, -1e30).astype(F32)
    return jnp.concatenate([bias] * GROUP, axis=1)


def collect(bounds, blocks, k_ref, v_ref):
    me = bounds[bounds.shape[0] - 1]
    for r, block in enumerate(blocks):
        rows = block.shape[0]
        at = pl.multiple_of((me ^ r) * rows, QB)
        k_ref[pl.ds(at, rows), :] = block[:, : 2 * HEAD_DIM]
        v_ref[pl.ds(at, rows), :] = block[:, 2 * HEAD_DIM :]


def turn_over(source, target):
    for at in range(0, source.shape[0], QB):
        target[:, at : at + QB] = source[at : at + QB, :].astype(F32).T.astype(BF16)


def forward_kernel(group, bounds, pq_ref, cos_ref, sin_ref, start_ref, *rest):
    blocks = rest[:group]
    o_ref, qt_ref, ot_ref, lse_ref, qpad, top, total, acc, k_ref, v_ref, vt_ref = rest[-11:]
    b = pl.program_id(0)

    @pl.when(b == 0)
    def _():
        collect(bounds, blocks, k_ref, v_ref)
        turn_over(v_ref, vt_ref)

    lo, hi, first = bounds[3 * b], bounds[3 * b + 1], bounds[3 * b + 2]
    half = HEAD_DIM // 2
    turned = pq_ref[...].T
    cosine, sine = cos_ref[...], sin_ref[...]
    qpad[...] = jnp.zeros_like(qpad)
    for h in range(HEADS):
        g, i = divmod(h, GROUP)
        u1 = turned[h * HEAD_DIM : h * HEAD_DIM + half]
        u2 = turned[h * HEAD_DIM + half : (h + 1) * HEAD_DIM]
        both = jnp.concatenate([u1 * cosine - u2 * sine, u2 * cosine + u1 * sine], axis=0)
        both = both.astype(BF16) * jnp.asarray(SCALE, BF16)
        qpad[g, g * HEAD_DIM : (g + 1) * HEAD_DIM, i * QB : (i + 1) * QB] = both
        qt_ref[0, g, :, i * QB : (i + 1) * QB] = both
    top[...] = jnp.full_like(top, -1e30)
    total[...] = jnp.zeros_like(total)
    acc[...] = jnp.zeros_like(acc)

    def step(j, _):
        at = pl.multiple_of(j * KB, KB)
        keys = k_ref[pl.ds(at, KB), :]
        bias = masks(start_ref, first, at)
        for g in range(KV_HEADS):
            scores = dot(keys, qpad[g]) + bias
            new_top = jnp.maximum(top[g], jnp.max(scores, axis=0, keepdims=True))
            weights = jnp.exp(scores - new_top)
            fade = jnp.exp(top[g] - new_top)
            total[g] = total[g] * fade + jnp.sum(weights, axis=0, keepdims=True)
            values = vt_ref[g * HEAD_DIM : (g + 1) * HEAD_DIM, pl.ds(at, KB)]
            acc[g] = acc[g] * fade + dot(values, weights.astype(BF16))
            top[g] = new_top
        return 0

    lax.fori_loop(lo, hi, step, 0)
    pieces = []
    for g in range(KV_HEADS):
        mixed = acc[g] / total[g]
        ot_ref[0, g] = mixed.astype(BF16)
        lse_ref[0, g] = top[g] + jnp.log(total[g])
        pieces += [mixed[:, i * QB : (i + 1) * QB] for i in range(GROUP)]
    o_ref[...] = jnp.concatenate(pieces, axis=0).T.astype(BF16)


def backward_kernel(
    group, waits, bounds, qt_ref, ot_ref, lse_ref, do_ref, cos_ref, sin_ref, start_ref, *rest
):
    blocks, rest = rest[:group], rest[group + waits :]
    dq_ref, dkv_refs, rest = rest[0], rest[1 : 1 + group], rest[1 + group :]
    qpad, dopad, qrow, dorow, centre, dqt, dk_acc, dv_acc, k_ref, v_ref, kt_ref = rest
    b = pl.program_id(0)
    lo, hi, first = bounds[3 * b], bounds[3 * b + 1], bounds[3 * b + 2]
    half = HEAD_DIM // 2

    @pl.when(b == 0)
    def _():
        dk_acc[...] = jnp.zeros_like(dk_acc)
        dv_acc[...] = jnp.zeros_like(dv_acc)
        collect(bounds, blocks, k_ref, v_ref)
        turn_over(k_ref, kt_ref)

    qpad[...] = jnp.zeros_like(qpad)
    dopad[...] = jnp.zeros_like(dopad)
    dqt[...] = jnp.zeros_like(dqt)
    grads = do_ref[...].astype(F32)
    turned = grads.T
    lane = lax.broadcasted_iota(jnp.int32, (QB, 2 * HEAD_DIM), 1)
    for h in range(HEADS):
        g, i = divmod(h, GROUP)
        rows = slice(g * HEAD_DIM, (g + 1) * HEAD_DIM)
        cols = slice(i * QB, (i + 1) * QB)
        grad_t = turned[h * HEAD_DIM : (h + 1) * HEAD_DIM]
        dopad[g, rows, cols] = grad_t.astype(BF16)
        centre[g, :, cols] = jnp.sum(grad_t * ot_ref[0, g, :, cols].astype(F32), axis=0, keepdims=True)
        query_t = qt_ref[0, g, :, cols]
        qpad[g, rows, cols] = query_t
        mine = (lane >= g * HEAD_DIM) & (lane < (g + 1) * HEAD_DIM)
        pair = grads[:, (h // 2) * 2 * HEAD_DIM : (h // 2 + 1) * 2 * HEAD_DIM]
        if h % 2 != g:
            pair = pltpu.roll(pair, HEAD_DIM, 1)
        dorow[g, cols, :] = jnp.where(mine, pair, 0.0).astype(BF16)
        wide = qpad[g, :, cols].astype(F32)
        qrow[g, cols, :] = wide.T.astype(BF16)

    def step(j, _):
        at = pl.multiple_of(j * KB, KB)
        keys = k_ref[pl.ds(at, KB), :]
        values = v_ref[pl.ds(at, KB), :]
        bias = masks(start_ref, first, at)
        dk_term = None
        dv_term = None
        for g in range(KV_HEADS):
            probs = jnp.exp(dot(keys, qpad[g]) + bias - lse_ref[0, g])
            grad_probs = dot(values, dopad[g])
            grad_scores = (probs * (grad_probs - centre[g])).astype(BF16)
            dv_g = dot(probs.astype(BF16), dorow[g])
            dk_g = dot(grad_scores, qrow[g])
            dk_term = dk_g if g == 0 else dk_term + dk_g
            dv_term = dv_g if g == 0 else dv_term + dv_g
            turned_keys = kt_ref[g * HEAD_DIM : (g + 1) * HEAD_DIM, pl.ds(at, KB)]
            dqt[g] += dot(turned_keys, grad_scores)
        dk_acc[pl.ds(at, KB), :] += dk_term
        dv_acc[pl.ds(at, KB), :] += dv_term
        return 0

    lax.fori_loop(lo, hi, step, 0)
    cosine, sine = cos_ref[...], sin_ref[...]
    pieces = []
    for h in range(HEADS):
        g, i = divmod(h, GROUP)
        w1 = dqt[g, :half, i * QB : (i + 1) * QB] * SCALE
        w2 = dqt[g, half:, i * QB : (i + 1) * QB] * SCALE
        pieces += [w1 * cosine + w2 * sine, w2 * cosine - w1 * sine]
    dq_ref[...] = jnp.concatenate(pieces, axis=0).T.astype(BF16)

    @pl.when(b == pl.num_programs(0) - 1)
    def _():
        me = bounds[bounds.shape[0] - 1]
        for r, ref in enumerate(dkv_refs):
            rows = ref.shape[0]
            at = pl.multiple_of((me ^ r) * rows, QB)
            ref[:, : 2 * HEAD_DIM] = dk_acc[pl.ds(at, rows), :].astype(BF16)
            ref[:, 2 * HEAD_DIM :] = dv_acc[pl.ds(at, rows), :].astype(BF16)


def whole(shape):
    return pl.BlockSpec(shape, lambda b, *_: (0,) * len(shape))


def attention_forward(bounds, pq, cos_t, sin_t, start, blocks, waits):
    rows = pq.shape[0]
    length = rows * len(blocks)
    count = rows // QB
    width = HEADS * HEAD_DIM
    lanes = GROUP * QB
    return pl.pallas_call(
        functools.partial(forward_kernel, len(blocks)),
        out_shape=(
            jax.ShapeDtypeStruct((rows, width), BF16),
            jax.ShapeDtypeStruct((count, KV_HEADS, HEAD_DIM, lanes), BF16),
            jax.ShapeDtypeStruct((count, KV_HEADS, HEAD_DIM, lanes), BF16),
            jax.ShapeDtypeStruct((count, KV_HEADS, 1, lanes), F32),
        ),
        grid_spec=pltpu.PrefetchScalarGridSpec(
            num_scalar_prefetch=1,
            grid=(count,),
            in_specs=[
                pl.BlockSpec((QB, width), lambda b, *_: (b, 0)),
                pl.BlockSpec((HEAD_DIM // 2, QB), lambda b, *_: (0, b)),
                pl.BlockSpec((HEAD_DIM // 2, QB), lambda b, *_: (0, b)),
                pl.BlockSpec((1, QB), lambda b, *_: (0, b)),
                *[whole((rows, 4 * HEAD_DIM))] * len(blocks),
                *[pl.BlockSpec(memory_space=pl.ANY)] * len(waits),
            ],
            out_specs=[
                pl.BlockSpec((QB, width), lambda b, *_: (b, 0)),
                pl.BlockSpec((1, KV_HEADS, HEAD_DIM, lanes), lambda b, *_: (b, 0, 0, 0)),
                pl.BlockSpec((1, KV_HEADS, HEAD_DIM, lanes), lambda b, *_: (b, 0, 0, 0)),
                pl.BlockSpec((1, KV_HEADS, 1, lanes), lambda b, *_: (b, 0, 0, 0)),
            ],
            scratch_shapes=[
                pltpu.VMEM((KV_HEADS, 2 * HEAD_DIM, lanes), BF16),
                pltpu.VMEM((KV_HEADS, 1, lanes), F32),
                pltpu.VMEM((KV_HEADS, 1, lanes), F32),
                pltpu.VMEM((KV_HEADS, HEAD_DIM, lanes), F32),
                pltpu.VMEM((length, 2 * HEAD_DIM), BF16),
                pltpu.VMEM((length, 2 * HEAD_DIM), BF16),
                pltpu.VMEM((2 * HEAD_DIM, length), BF16),
            ],
        ),
        compiler_params=pltpu.CompilerParams(vmem_limit_bytes=40 << 20),
        cost_estimate=pl.CostEstimate(
            flops=1 << 22, bytes_accessed=1 << 18, transcendentals=0
        ),
        name="attention_forward",
    )(bounds, pq, cos_t, sin_t, start, *blocks, *waits)


def attention_backward(bounds, qt, ot, lse, grad_mixed, cos_t, sin_t, start, blocks, waits):
    rows = grad_mixed.shape[0]
    group = len(blocks)
    length = rows * group
    count = rows // QB
    width = HEADS * HEAD_DIM
    lanes = GROUP * QB
    return pl.pallas_call(
        functools.partial(backward_kernel, group, len(waits)),
        out_shape=(
            jax.ShapeDtypeStruct((rows, width), BF16),
            *[jax.ShapeDtypeStruct((rows, 4 * HEAD_DIM), BF16)] * group,
        ),
        grid_spec=pltpu.PrefetchScalarGridSpec(
            num_scalar_prefetch=1,
            grid=(count,),
            in_specs=[
                pl.BlockSpec((1, KV_HEADS, HEAD_DIM, lanes), lambda b, *_: (b, 0, 0, 0)),
                pl.BlockSpec((1, KV_HEADS, HEAD_DIM, lanes), lambda b, *_: (b, 0, 0, 0)),
                pl.BlockSpec((1, KV_HEADS, 1, lanes), lambda b, *_: (b, 0, 0, 0)),
                pl.BlockSpec((QB, width), lambda b, *_: (b, 0)),
                pl.BlockSpec((HEAD_DIM // 2, QB), lambda b, *_: (0, b)),
                pl.BlockSpec((HEAD_DIM // 2, QB), lambda b, *_: (0, b)),
                pl.BlockSpec((1, QB), lambda b, *_: (0, b)),
                *[whole((rows, 4 * HEAD_DIM))] * group,
                *[pl.BlockSpec(memory_space=pl.ANY)] * len(waits),
            ],
            out_specs=[
                pl.BlockSpec((QB, width), lambda b, *_: (b, 0)),
                *[whole((rows, 4 * HEAD_DIM))] * group,
            ],
            scratch_shapes=[
                pltpu.VMEM((KV_HEADS, 2 * HEAD_DIM, lanes), BF16),
                pltpu.VMEM((KV_HEADS, 2 * HEAD_DIM, lanes), BF16),
                pltpu.VMEM((KV_HEADS, lanes, 2 * HEAD_DIM), BF16),
                pltpu.VMEM((KV_HEADS, lanes, 2 * HEAD_DIM), BF16),
                pltpu.VMEM((KV_HEADS, 1, lanes), F32),
                pltpu.VMEM((KV_HEADS, HEAD_DIM, lanes), F32),
                pltpu.VMEM((length, 2 * HEAD_DIM), F32),
                pltpu.VMEM((length, 2 * HEAD_DIM), F32),
                pltpu.VMEM((length, 2 * HEAD_DIM), BF16),
                pltpu.VMEM((length, 2 * HEAD_DIM), BF16),
                pltpu.VMEM((2 * HEAD_DIM, length), BF16),
            ],
        ),
        compiler_params=pltpu.CompilerParams(vmem_limit_bytes=48 << 20),
        cost_estimate=pl.CostEstimate(
            flops=1 << 22, bytes_accessed=1 << 18, transcendentals=0
        ),
        name="attention_backward",
    )(bounds, qt, ot, lse, grad_mixed, cos_t, sin_t, start, *blocks, *waits)


def project_kernel(offsets, x_ref, gain_ref, bias_ref, cos_ref, sin_ref, *rest):
    pieces = rest[:-6]
    pass_ref, q_ref, kv_ref, hidden_ref, w_ref, passed_ref = rest[-6:]
    passed_ref[...] = pass_ref[...]
    for i, piece in enumerate(pieces):
        count = piece.shape[0]
        w_ref[pl.ds(pl.multiple_of(offsets[i], 16), count), :] = piece[...]
    x = x_ref[...].astype(F32)
    scale = lax.rsqrt(jnp.mean(x * x, axis=-1, keepdims=True) + EPSILON)
    hidden = (x * scale * gain_ref[...]).astype(BF16)
    hidden_ref[...] = hidden
    query_width = HEADS * HEAD_DIM
    key_width = KV_HEADS * HEAD_DIM
    q_ref[...] = dot(hidden, w_ref[:, :query_width]) + bias_ref[:, :query_width]
    kv = dot(hidden, w_ref[:, query_width:]) + bias_ref[:, query_width:]
    keys = kv[:, :key_width]
    lane = lax.broadcasted_iota(jnp.int32, keys.shape, 1) % HEAD_DIM
    half = HEAD_DIM // 2
    other = jnp.where(
        lane < half, pltpu.roll(keys, key_width - half, 1), pltpu.roll(keys, half, 1)
    )
    keys = keys * cos_ref[...] + other * sin_ref[...]
    kv_ref[:, :key_width] = keys.astype(BF16)
    kv_ref[:, key_width:] = kv[:, key_width:].astype(BF16)


def project(offsets, x, gain, bias, cosine, sine, pieces, passed):
    rows, width = x.shape
    total = bias.shape[1]
    query_width = HEADS * HEAD_DIM
    return pl.pallas_call(
        project_kernel,
        out_shape=(
            jax.ShapeDtypeStruct((rows, query_width), F32),
            jax.ShapeDtypeStruct((rows, total - query_width), BF16),
            jax.ShapeDtypeStruct((rows, width), BF16),
            jax.ShapeDtypeStruct((width, total), BF16),
            jax.ShapeDtypeStruct(passed.shape, BF16),
        ),
        grid_spec=pltpu.PrefetchScalarGridSpec(
            num_scalar_prefetch=1,
            grid=(1,),
            in_specs=[whole(v.shape) for v in (x, gain, bias, cosine, sine, *pieces, passed)],
            out_specs=[
                whole((rows, query_width)),
                whole((rows, total - query_width)),
                whole((rows, width)),
                whole((width, total)),
                whole(passed.shape),
            ],
        ),
        compiler_params=pltpu.CompilerParams(vmem_limit_bytes=40 << 20),
        cost_estimate=pl.CostEstimate(
            flops=2 * rows * width * total, bytes_accessed=8 << 20, transcendentals=0
        ),
        name="norm_project_rotate",
    )(offsets, x, gain, bias, cosine, sine, *pieces, passed)


def output_kernel(pieces, offsets, x_ref, mixed_ref, gain_ref, *rest):
    residual_ref, hidden_ref, w_ref = rest[-3:]
    for i, piece in enumerate(rest[:pieces]):
        w_ref[pl.ds(pl.multiple_of(offsets[i], 16), piece.shape[0]), :] = piece[...]
    residual = x_ref[...].astype(F32) + dot(mixed_ref[...], w_ref[...])
    residual_ref[...] = residual
    scale = lax.rsqrt(jnp.mean(residual * residual, axis=-1, keepdims=True) + EPSILON)
    hidden_ref[...] = (residual * scale * gain_ref[...]).astype(BF16)


def output_of(offsets, x, mixed, gain, pieces, waits):
    rows, width = x.shape
    return pl.pallas_call(
        functools.partial(output_kernel, len(pieces)),
        out_shape=(
            jax.ShapeDtypeStruct((rows, width), F32),
            jax.ShapeDtypeStruct((rows, width), BF16),
            jax.ShapeDtypeStruct((width, width), BF16),
        ),
        grid_spec=pltpu.PrefetchScalarGridSpec(
            num_scalar_prefetch=1,
            grid=(1,),
            in_specs=[
                *[whole(v.shape) for v in (x, mixed, gain, *pieces)],
                *[pl.BlockSpec(memory_space=pl.ANY)] * len(waits),
            ],
            out_specs=[whole((rows, width)), whole((rows, width)), whole((width, width))],
        ),
        compiler_params=pltpu.CompilerParams(vmem_limit_bytes=40 << 20),
        cost_estimate=pl.CostEstimate(flops=1 << 22, bytes_accessed=1 << 18, transcendentals=0),
        name="project_add_norm",
    )(offsets, x, mixed, gain, *pieces, *waits)


FB = 256


def feed_kernel(blocks, offsets, *refs):
    hs, dys, refs = refs[:blocks], refs[blocks : 2 * blocks], refs[2 * blocks :]
    count = offsets.shape[0]
    pieces, refs = refs[:count], refs[count:]
    wd_ref, m_ref, d_ref = refs[:3]
    outs, backs = refs[3 : 3 + blocks], refs[3 + blocks : 3 + 2 * blocks]
    out_acc, dh_acc, wg, wu = refs[3 + 2 * blocks :]
    step = pl.program_id(0)
    last = pl.num_programs(0) - 1
    rows = hs[0].shape[0]
    for i, piece in enumerate(pieces):
        at = pl.ds(pl.multiple_of(offsets[i], 16), piece.shape[1])
        wg[at, :] = piece[0]
        wu[at, :] = piece[1]

    @pl.when(step == 0)
    def _():
        out_acc[...] = jnp.zeros_like(out_acc)
        dh_acc[...] = jnp.zeros_like(dh_acc)

    for t in range(blocks):
        at = slice(t * rows, (t + 1) * rows)
        hidden, cot = hs[t][...], dys[t][...]
        gate = dot(hidden, wg[...])
        upward = dot(hidden, wu[...])
        grad_product = dot_last(cot, wd_ref[...])
        sigma = jax.nn.sigmoid(gate)
        active = gate * sigma
        product = (active * upward).astype(BF16)
        grad_gate = (grad_product * upward * (sigma + active * (1.0 - sigma))).astype(BF16)
        grad_up = (grad_product * active).astype(BF16)
        d_ref[0, at], d_ref[1, at] = grad_gate, grad_up
        m_ref[:, at] = (active * upward).T.astype(BF16)
        out_acc[at] += dot(product, wd_ref[...])
        dh_acc[at] += dot_last(grad_gate, wg[...]) + dot_last(grad_up, wu[...])

    @pl.when(step == last)
    def _():
        for t in range(blocks):
            at = slice(t * rows, (t + 1) * rows)
            outs[t][...] = out_acc[at].astype(BF16)
            backs[t][...] = dh_acc[at].astype(BF16)


def feed(offsets, hiddens, cots, pieces, w_down):
    blocks = len(hiddens)
    rows, width = hiddens[0].shape
    inner = w_down.shape[0]
    wide = jax.ShapeDtypeStruct((2, blocks * rows, inner), BF16)
    tall = jax.ShapeDtypeStruct((inner, blocks * rows), BF16)
    narrow = jax.ShapeDtypeStruct((rows, width), BF16)
    return pl.pallas_call(
        functools.partial(feed_kernel, blocks),
        out_shape=(tall, wide) + (narrow,) * (2 * blocks),
        grid_spec=pltpu.PrefetchScalarGridSpec(
            num_scalar_prefetch=1,
            grid=(inner // FB,),
            in_specs=[
                *[whole((rows, width))] * (2 * blocks),
                *[pl.BlockSpec((2, v.shape[1], FB), lambda j, *_: (0, 0, j)) for v in pieces],
                pl.BlockSpec((FB, width), lambda j, *_: (j, 0)),
            ],
            out_specs=[
                pl.BlockSpec((FB, blocks * rows), lambda j, *_: (j, 0)),
                pl.BlockSpec((2, blocks * rows, FB), lambda j, *_: (0, 0, j)),
                *[whole((rows, width))] * (2 * blocks),
            ],
            scratch_shapes=[
                pltpu.VMEM((blocks * rows, width), F32),
                pltpu.VMEM((blocks * rows, width), F32),
                pltpu.VMEM((width, FB), BF16),
                pltpu.VMEM((width, FB), BF16),
            ],
        ),
        compiler_params=pltpu.CompilerParams(vmem_limit_bytes=48 << 20),
        cost_estimate=pl.CostEstimate(
            flops=1 << 22, bytes_accessed=1 << 18, transcendentals=0
        ),
        name="feed_forward_backward",
    )(offsets, *hiddens, *cots, *pieces, w_down)


def down_kernel(parts, per, cut, offsets, *refs):
    ms, dys, outs = refs[:parts], refs[parts : parts + parts * per], refs[-2:]
    for k, out_ref in enumerate(outs):
        rows = out_ref.shape[0]

        @pl.when(pl.program_id(0) == 1 - k)
        def _():
            total = None
            for i, m_ref in enumerate(ms):
                width = m_ref.shape[-1] // per
                for t in range(per):
                    if cut:
                        at = pl.ds(pl.multiple_of(offsets[k], 16), rows)
                        left = m_ref[at, t * width : (t + 1) * width]
                    else:
                        left = m_ref[k, :, t * width : (t + 1) * width]
                    term = dot(left, dys[i * per + t][...])
                    total = term if total is None else total + term
            out_ref[...] = total.astype(BF16)


def grad_down_of(products, cots, offsets, half, waits):
    rows, width = cots[0].shape
    cut = half % 16 == 0
    if not cut:
        products = [
            jnp.stack([lax.dynamic_slice_in_dim(v, offsets[k], half, 0) for k in range(2)]) for v in products
        ]
    out = jax.ShapeDtypeStruct((half, width), BF16)
    return pl.pallas_call(
        functools.partial(down_kernel, len(products), len(cots) // len(products), cut),
        out_shape=(out, out),
        grid_spec=pltpu.PrefetchScalarGridSpec(
            num_scalar_prefetch=1,
            grid=(2,),
            in_specs=[*[whole(v.shape) for v in (*products, *cots)], *[ANY] * len(waits)],
            out_specs=[whole((half, width))] * 2,
        ),
        compiler_params=pltpu.CompilerParams(vmem_limit_bytes=56 << 20),
        cost_estimate=pl.CostEstimate(flops=1 << 22, bytes_accessed=1 << 18, transcendentals=0),
        name="grad_down",
    )(offsets, *products, *cots, *waits)


def gate_up_kernel(parts, blocks, waits, given, which, *refs):
    keeps, sends, refs = refs[:parts], refs[parts : 2 * parts], refs[2 * parts :]
    hs, refs = refs[:blocks], refs[blocks + waits :]
    outs, refs = refs[:2], refs[2:]
    if given:
        (turned,) = hs
    else:
        (turned,) = refs

        @pl.when(pl.program_id(0) == 0)
        def _():
            rows = hs[0].shape[0]
            for t, h in enumerate(hs):
                for at in range(0, rows, QB):
                    place_at = slice(t * rows + at, t * rows + at + QB)
                    turned[:, place_at] = h[at : at + QB, :].astype(F32).T.astype(BF16)

    for out, group in zip(outs, (keeps, sends)):
        total = None
        first = 0
        for v in group:
            term = dot(turned[:, first : first + v.shape[1]], v[0])
            total = term if total is None else total + term
            first += v.shape[1]
        out[...] = total.astype(BF16)


def grad_gate_up_of(grads, hiddens, first, count, which, waits):
    given = len(hiddens) == 1
    width = hiddens[0].shape[0] if given else hiddens[0].shape[1]
    tokens = sum(v.shape[1] for v in grads)
    out = jax.ShapeDtypeStruct((width, count * FB), BF16)
    turned = jax.ShapeDtypeStruct((width, tokens), BF16)
    place_of = pl.BlockSpec((width, FB), lambda j, *_: (0, j))
    keep = [pl.BlockSpec((1, v.shape[1], FB), lambda j, at: (at[0], 0, j + first)) for v in grads]
    send = [pl.BlockSpec((1, v.shape[1], FB), lambda j, at: (1 - at[0], 0, j + first)) for v in grads]
    return pl.pallas_call(
        functools.partial(gate_up_kernel, len(grads), len(hiddens), len(waits), given),
        out_shape=(out, out) if given else (out, out, turned),
        grid_spec=pltpu.PrefetchScalarGridSpec(
            num_scalar_prefetch=1,
            grid=(count,),
            in_specs=[*keep, *send, *[whole(v.shape) for v in hiddens], *[ANY] * len(waits)],
            out_specs=[place_of] * 2 if given else [place_of] * 2 + [whole((width, tokens))],
        ),
        compiler_params=pltpu.CompilerParams(vmem_limit_bytes=56 << 20),
        cost_estimate=pl.CostEstimate(flops=1 << 22, bytes_accessed=1 << 18, transcendentals=0),
        name="grad_gate_up",
    )(which, *grads, *grads, *hiddens, *waits)


def residual_back_kernel(mine_ref, got_ref, cot_ref, residual_ref, gain_ref, w_ref, *rest):
    grad_ref, mixed_ref, gain_out = rest[-3:]
    grad_hidden = mine_ref[...].astype(F32) + got_ref[...].astype(F32)
    residual = residual_ref[...]
    scale = lax.rsqrt(jnp.mean(residual * residual, axis=-1, keepdims=True) + EPSILON)
    normed = residual * scale
    gain_out[...] = jnp.sum(grad_hidden * normed, axis=0, keepdims=True)
    grad = cot_ref[...].astype(F32) + norm_back(grad_hidden, normed, scale, gain_ref[...])
    grad_ref[...] = grad
    mixed_ref[...] = dot_last(grad.astype(BF16), w_ref[...]).astype(BF16)


def single_call(kernel, name, ins, waits, outs, scalars=None):
    scalars = jnp.zeros((1,), jnp.int32) if scalars is None else scalars
    scratch = [v for v in outs if isinstance(v, type(pltpu.VMEM((8, 128), F32)))]
    outs = [v for v in outs if v not in scratch]

    def body(scalar_ref, *refs):
        kernel(scalar_ref, *refs[: len(ins)], *refs[len(ins) + len(waits) :])

    return pl.pallas_call(
        body,
        out_shape=outs,
        grid_spec=pltpu.PrefetchScalarGridSpec(
            num_scalar_prefetch=1,
            grid=(1,),
            in_specs=[*[whole(v.shape) for v in ins], *[ANY] * len(waits)],
            out_specs=[whole(v.shape) for v in outs],
            scratch_shapes=scratch,
        ),
        compiler_params=pltpu.CompilerParams(vmem_limit_bytes=52 << 20),
        cost_estimate=pl.CostEstimate(flops=1 << 22, bytes_accessed=1 << 18, transcendentals=0),
        name=name,
    )(scalars, *ins, *waits)


def project_back_kernel(
    aligned, offsets, x_ref, gain_ref, hidden_ref, dq_ref, mine_ref, got_ref, w_ref, grad_ref, mixed_ref,
    cos_ref, sin_ref, out_ref, gain_out, bias_out, *rest
):
    weights, (dp_ref, dw_ref) = rest[:-2], rest[-2:]
    query_width = HEADS * HEAD_DIM
    key_width = KV_HEADS * HEAD_DIM
    half = HEAD_DIM // 2
    total = w_ref.shape[1]
    dkv = mine_ref[...].astype(F32) + got_ref[...].astype(F32)
    keys = dkv[:, :key_width]
    lane = lax.broadcasted_iota(jnp.int32, keys.shape, 1) % HEAD_DIM
    other = jnp.where(
        lane < half, pltpu.roll(keys, key_width - half, 1), pltpu.roll(keys, half, 1)
    )
    dp_ref[:, :query_width] = dq_ref[...]
    dp_ref[:, query_width : query_width + key_width] = (
        keys * cos_ref[...] - other * sin_ref[...]
    ).astype(BF16)
    dp_ref[:, query_width + key_width :] = dkv[:, key_width:].astype(BF16)
    grads = dp_ref[...]
    bias_out[...] = jnp.sum(grads.astype(F32), axis=0, keepdims=True)
    back = dot_last(grads, w_ref[...])
    x = x_ref[...].astype(F32)
    scale = lax.rsqrt(jnp.mean(x * x, axis=-1, keepdims=True) + EPSILON)
    normed = x * scale
    gain_out[...] = jnp.sum(back * normed, axis=0, keepdims=True)
    out_ref[...] = grad_ref[...] + norm_back(back, normed, scale, gain_ref[...])
    dw_ref[:, :total] = dot(hidden_ref[...].astype(F32).T.astype(BF16), grads).astype(BF16)
    dw_ref[:, total:] = dot(
        mixed_ref[...].astype(F32).T.astype(BF16), grad_ref[...].astype(BF16)
    ).astype(BF16)
    if aligned:
        rows = dw_ref.shape[0] // len(weights)
        for k, ref in enumerate(weights):
            ref[:rows] = dw_ref[pl.ds(pl.multiple_of(offsets[k], 16), rows), :]
            ref[rows:] = jnp.zeros((ref.shape[0] - rows, ref.shape[1]), BF16)
    else:
        weights[0][...] = dw_ref[...]


ANY = pl.BlockSpec(memory_space=pl.ANY)


class Line:
    def __init__(self):
        self.last = []

    def mark(self, x):
        self.last = [x]
        return x


def small_call(kernel, name, scalars, grid, ins, in_specs, out_shape, out_specs, waits):
    count = len(ins)

    def body(scalar_ref, *refs):
        kernel(scalar_ref, refs[:count], refs[count + len(waits) :])

    return pl.pallas_call(
        body,
        out_shape=out_shape,
        grid_spec=pltpu.PrefetchScalarGridSpec(
            num_scalar_prefetch=1,
            grid=grid,
            in_specs=[*in_specs, *[ANY] * len(waits)],
            out_specs=out_specs,
        ),
        compiler_params=pltpu.CompilerParams(vmem_limit_bytes=40 << 20),
        cost_estimate=pl.CostEstimate(flops=1 << 20, bytes_accessed=1 << 18, transcendentals=0),
        name=name,
    )(scalars, *ins, *waits)


def add_split(x, got, lead, mine, waits):
    columns = x.shape[-1]
    x, got = x.reshape(lead, 2, -1, columns), got.reshape(lead, 2, -1, columns)
    rows = x.shape[2]

    def kernel(_, ins, outs):
        for k in range(2):
            total = ins[2 * k][0, 0].astype(F32) + ins[2 * k + 1][0, 0].astype(F32)
            outs[k][0] = total.astype(BF16)

    keep = pl.BlockSpec((1, 1, rows, columns), lambda i, at: (i, at[0], 0, 0))
    send = pl.BlockSpec((1, 1, rows, columns), lambda i, at: (i, 1 - at[0], 0, 0))
    half = jax.ShapeDtypeStruct((lead, rows, columns), BF16)
    out = pl.BlockSpec((1, rows, columns), lambda i, at: (i, 0, 0))
    return small_call(
        kernel, "add_and_split", mine[None], (lead,), (x, got, x, got), (keep, keep, send, send),
        (half, half), (out, out), waits,
    )


def add_ordered(x, got, order, waits):
    shape = (1,) + x.shape[1:]
    got = got.reshape(x.shape)

    def kernel(_, ins, outs):
        for k, out in enumerate(outs):
            out[...] = (ins[2 * k][...].astype(F32) + ins[2 * k + 1][...].astype(F32)).astype(BF16)

    specs = []
    for k in range(order.shape[0]):
        specs += [pl.BlockSpec(shape, lambda i, at, k=k: (at[k], 0, 0))] * 2
    count = order.shape[0]
    return small_call(
        kernel, "add", order, (1,), (x, got) * count, specs,
        (jax.ShapeDtypeStruct(shape, BF16),) * count, (whole(shape),) * count, waits,
    )


def put_ordered(parts, order, waits, dtype=BF16):
    shape = parts[0].shape
    block = shape[-2:]
    lead = parts[0].size // (block[0] * block[1])
    parts = [v.reshape((lead,) + block) for v in parts]
    count = len(parts)

    def kernel(at, ins, outs):
        for k in range(count):
            outs[0][at[k]] = ins[k][...].astype(dtype)

    (out,) = small_call(
        kernel, "place", order, (lead,), parts,
        [pl.BlockSpec((1,) + block, lambda i, at: (i, 0, 0))] * count,
        (jax.ShapeDtypeStruct((count, lead) + block, dtype),),
        (pl.BlockSpec((count, 1) + block, lambda i, at: (0, i, 0, 0)),), waits,
    )
    return out.reshape((count,) + shape)


def steps_of_sum(line, keep, send, lead, order=None, last=None, bits=None):
    index = lax.axis_index("dp")
    depth = lax.axis_size("dp").bit_length() - 1
    masks = [1 << k for k in (range(depth) if bits is None else bits)]
    bits = [((index // mask) & 1).astype(jnp.int32) for mask in masks]
    pair = lambda k: jnp.stack([bits[k], 1 - bits[k]])
    columns = keep.shape[-1]
    for k in range(depth - 1):
        got = swap(send, "dp", masks[k])
        yield None
        keep, send = add_split(keep, got, lead, bits[k + 1], line.last)
        line.mark(keep)
    got = swap(send, "dp", masks[-1])
    yield None
    keep = keep.reshape(lead, -1, columns)
    if order is None:
        (part,) = add_ordered(keep, got, jnp.zeros((1,), jnp.int32), line.last)
        part = line.mark(part[0])
    else:
        parts = add_ordered(keep, got, order, line.last)
        line.mark(parts[0])
        parts = [swap(v, "seq", r) if r else v for r, v in enumerate(parts)]
        yield None
        part = line.mark(put_ordered([v[0] for v in parts], order, line.last))
    for k in reversed(range(1, depth)):
        got = swap(part, "dp", masks[k])
        yield None
        part = line.mark(put_ordered([part, got], pair(k), line.last))
    got = swap(part, "dp", masks[0])
    yield None
    part = put_ordered([part, got], pair(0), line.last, BF16 if last is None else last)
    line.mark(part)
    yield part


def steps_of_scatter(parts, axis):
    parts = dict(parts)
    for b in reversed(bits_down(lax.axis_size(axis))):
        got = {r: swap(parts[r ^ b], axis, b) for r in parts if not r & b}
        yield None
        if len(got) == 1:
            yield parts[0], got[0]
        parts = {r: (parts[r].astype(F32) + v.astype(F32)).astype(BF16) for r, v in got.items()}


def pad_rows(x, multiple):
    extra = -x.shape[0] % multiple
    return jnp.pad(x, ((0, extra), (0, 0))) if extra else x


def locate(lengths, where_at):
    starts = jnp.cumsum(lengths) - lengths
    inside = where_at[:, None] >= starts[None, :]
    return jnp.max(jnp.where(inside, starts[None, :], 0), axis=1)


def norm_back(grad_hidden, normed, scale_rows, gain):
    scaled = grad_hidden * gain
    return scale_rows * (scaled - normed * jnp.mean(scaled * normed, axis=-1, keepdims=True))


def turn_heads(values, cosine, sine):
    rows = values.shape[0]
    values = values.reshape(rows, KV_HEADS, HEAD_DIM)
    half = HEAD_DIM // 2
    first, second = values[..., :half], values[..., half:]
    cosine, sine = cosine[:, None, :], sine[:, None, :]
    turned = jnp.concatenate([first * cosine - second * sine, second * cosine + first * sine], axis=-1)
    return turned.reshape(rows, KV_HEADS * HEAD_DIM)


def swaps(x, axis):
    return {r: swap(x, axis, r) if r else x for r in range(lax.axis_size(axis))}


def windows(total, count, tile=128):
    each = total // count
    firsts = [j * each // tile * tile for j in range(count)]
    width = max(j * each - first + each for j, first in enumerate(firsts))
    return -(-width // FB) * FB, firsts


def join(parts, firsts, total, tile=128):
    runs = []
    for at in range(0, total, tile):
        cover = []
        for i, (first, values) in enumerate(parts):
            for j, begin in enumerate(firsts):
                local = at - begin - first
                if 0 <= local < values.shape[-1]:
                    cover.append((i, j, local))
        if runs and [(i, j, c - runs[-1][1]) for i, j, c in cover] == runs[-1][0]:
            runs[-1][1] += tile
        else:
            runs.append([cover, tile])
    segments = []
    for cover, width in runs:
        segments.append(
            sum(parts[i][1][j, :, c : c + width].astype(F32) for i, j, c in cover)
        )
    return jnp.concatenate(segments, axis=1)


def per_device(
    tokens, doc_lengths, cotangent, norm_one, w_qkv, b_qkv, w_out, norm_two, w_gate, w_up, w_down
):
    group = lax.axis_size("seq")
    me = lax.axis_index("seq")
    inputs = tokens[0].astype(F32)
    rows, width = inputs.shape
    query_width = HEADS * HEAD_DIM
    key_width = KV_HEADS * HEAD_DIM
    slice_d = width // group
    slice_b = b_qkv.shape[0]
    slice_f = w_down.shape[0]
    hidden_units = slice_f * group
    aligned = slice_d % 32 == 0

    small = jnp.concatenate([norm_one, norm_two, b_qkv])[None, :]
    small = place(swaps(small, "seq"), me)
    gain_one = small[:, :slice_d].reshape(1, width).astype(F32)
    gain_two = small[:, slice_d : 2 * slice_d].reshape(1, width).astype(F32)
    bias = small[:, 2 * slice_d :].reshape(1, -1).astype(F32)
    pieces_qkv = gather_rel(w_qkv, "seq")
    order = [me ^ r for r in range(group)]
    if aligned:
        offsets_qkv = jnp.stack([j * slice_d for j in order]).astype(jnp.int32)
        pieces_qkv = [pieces_qkv[r] for r in range(group)]
    else:
        offsets_qkv = jnp.zeros((1,), jnp.int32)
        pieces_qkv = [place(pieces_qkv, me)]

    inner, firsts = windows(hidden_units, group)
    both = jnp.stack([w_gate, w_up])
    both = jnp.pad(both, ((0, 0), (0, 0), (0, max(0, firsts[-1] + inner - hidden_units))))
    both = jnp.stack([both[:, :, at : at + inner] for at in firsts])
    shift = lax.rem(me * slice_f, 128)
    down = lax.dynamic_update_slice_in_dim(jnp.zeros((inner, width), BF16), w_down, shift, 0)

    half_d = slice_d // 2
    fast = (lax.axis_index("dp") & 1).astype(jnp.int32)
    slow = ((lax.axis_index("dp") >> 1) & 1).astype(jnp.int32)
    early = {}
    for r in range(2, group):
        part = lax.dynamic_slice(
            both, (order[r], slow, fast * half_d, 0), (1, 1, half_d, inner)
        )
        early[r] = swap(part.reshape(half_d, inner), "seq", r)

    offset = me * rows
    index = offset + jnp.arange(rows, dtype=jnp.int32)
    start = locate(doc_lengths[0], index)
    places = (index - start).astype(F32)
    half = HEAD_DIM // 2
    freqs = ROPE_BASE ** (-(jnp.arange(half, dtype=F32) * 2.0) / HEAD_DIM)
    angle = places[:, None] * freqs[None, :]
    cosine, sine = jnp.cos(angle), jnp.sin(angle)
    cos_t, sin_t = cosine.T, sine.T
    cos_k = jnp.concatenate([cosine] * (2 * KV_HEADS), axis=1)
    sin_k = jnp.concatenate([-sine, sine] * KV_HEADS, axis=1)
    marks = offset + jnp.arange(rows // QB, dtype=jnp.int32) * QB
    bounds = jnp.stack([start[::QB] // KB, (marks + QB - 1) // KB + 1, marks], axis=1).reshape(-1)
    bounds = jnp.concatenate([bounds, me[None]]).astype(jnp.int32)
    start_row = start.astype(jnp.int32)[None, :]

    queries, kv, hidden_one, full_qkv, w_out = project(
        offsets_qkv, tokens[0], gain_one, bias, cos_k, sin_k, pieces_qkv, w_out
    )
    pieces_out = gather_rel(w_out, "seq")
    pieces_out = [pieces_out[r] for r in range(group)] if aligned else [place(pieces_out, me)]
    (kv,) = single_call(
        lambda _, a, b: b.__setitem__(..., a[...]), "pass_on", (kv,), [early[r] for r in early],
        [jax.ShapeDtypeStruct(kv.shape, BF16)],
    )
    blocks = gather_rel(kv, "seq")
    blocks = [blocks[r] for r in range(group)]
    later = {}
    pieces = [pick(both, order[0]), swap(pick(both, order[1]), "seq", 1)]
    offsets = [order[0] * slice_d, order[1] * slice_d]
    for r in range(2, group):
        later[r] = got = swap(early[r], "dp", 2)
        part = jnp.stack([jnp.where(slow == 0, early[r], got), jnp.where(slow == 0, got, early[r])])
        pieces += [part, swap(part, "dp", 1)]
        at = order[r] * slice_d
        offsets += [at + fast * half_d, at + (1 - fast) * half_d]
    if not aligned:
        full = jnp.zeros((2, width, inner), BF16)
        for piece, at in zip(pieces, offsets):
            full = lax.dynamic_update_slice(full, piece, (0, at, 0))
        pieces, offsets = [full], [0 * me]
    offsets = jnp.stack(offsets).astype(jnp.int32)
    mixed, qt, ot, lse = attention_forward(bounds, queries, cos_t, sin_t, start_row, blocks, [])
    residual, hidden_two, full_out = output_of(
        offsets_qkv, tokens[0], mixed, gain_two, pieces_out, [later[r] for r in later]
    )

    cot = cotangent[0]
    hiddens = gather_rel(hidden_two, "seq")
    cots = gather_rel(after(cot, hiddens[group // 2]), "seq")
    terms_out, terms_back, products, grads = {}, {}, [], []
    for r in range(0, group, 2):
        got = feed(offsets, [hiddens[r], hiddens[r + 1]], [cots[r], cots[r + 1]], pieces, down)
        products.append(got[0])
        grads.append(got[1])
        terms_out[r], terms_out[r + 1], terms_back[r], terms_back[r + 1] = got[2:]
    hiddens = [hiddens[r] for r in range(group)]
    cots = [cots[r] for r in range(group)]
    total = lax.axis_size("dp")
    depth = total.bit_length() - 1
    levels = group.bit_length() - 1
    line = Line()
    count = inner // FB
    cuts = [0, -(-count // 2), count]
    share = 2 * slice_d // total
    order = jnp.stack(order).astype(jnp.int32)
    which = fast.astype(jnp.int32)[None]

    back = steps_of_scatter(terms_back, "seq")
    next(back)
    half_rows = slice_f // 2
    down_at = shift + half_rows * jnp.stack([fast, 1 - fast])
    down_keep, down_send = grad_down_of(products, cots, down_at.astype(jnp.int32), half_rows, [])
    down_steps = steps_of_sum(line, down_keep, down_send, 1, last=F32)
    next(down_steps)
    for _ in range(levels - 1):
        next(back)
    back_mine, back_got = next(back)
    first_keep, first_send, turned = grad_gate_up_of(
        grads, hiddens, 0, cuts[1], which, [down_keep, back_mine]
    )
    second_keep, second_send = grad_gate_up_of(
        grads, [turned], cuts[1], count - cuts[1], slow[None], []
    )
    f32 = lambda *shape: jax.ShapeDtypeStruct(shape, F32)
    bf16 = lambda *shape: jax.ShapeDtypeStruct(shape, BF16)

    grad_residual, grad_mixed, grad_gain_two = single_call(
        lambda _, *refs: residual_back_kernel(*refs), "norm_back",
        (back_mine, back_got, cot, residual, gain_two, full_out), [second_keep],
        [f32(rows, width), bf16(rows, width), f32(1, width)],
    )
    line.mark(grad_mixed)
    next(down_steps)
    first_steps = steps_of_sum(line, first_keep, first_send, group, order)
    next(first_steps)
    second_steps = steps_of_sum(line, second_keep, second_send, group, order, bits=[*range(1, depth), 0])
    next(second_steps)
    dq, *dkv = attention_backward(
        bounds, qt, ot, lse, grad_mixed, cos_t, sin_t, start_row, blocks, line.last
    )
    line.mark(dq)
    dkv_steps = steps_of_scatter(dict(enumerate(dkv)), "seq")
    next(dkv_steps)
    for _ in range(levels - 1):
        next(dkv_steps)
    next(second_steps)
    next(down_steps)
    dkv_mine, dkv_got = next(dkv_steps)
    qkv_width = w_qkv.shape[1]
    joint_width = qkv_width + width
    extra = -slice_d % (8 * total) or 8 * total
    joint_rows = slice_d + extra
    weights = [bf16(joint_rows, joint_width)] * group if aligned else [bf16(width, joint_width)]
    grad_inputs, grad_gain_one, grad_bias, *joint = single_call(
        functools.partial(project_back_kernel, aligned), "project_back",
        (tokens[0], gain_one, hidden_one, dq, dkv_mine, dkv_got, full_qkv, grad_residual, mixed, cos_k, sin_k),
        line.last,
        [f32(rows, width), f32(1, width), f32(1, qkv_width), *weights,
         pltpu.VMEM((rows, qkv_width), BF16), pltpu.VMEM((width, joint_width), BF16)],
        order * slice_d,
    )

    rest = jnp.concatenate(
        [
            grad_gain_one.reshape(group, slice_d),
            grad_gain_two.reshape(group, slice_d),
            grad_bias.reshape(group, slice_b),
        ],
        axis=1,
    ).astype(BF16)
    rest = jnp.pad(rest[:, None, :], ((0, 0), (0, 0), (0, joint_width - rest.shape[1])))
    if not aligned:
        joint = [
            jnp.pad(lax.dynamic_slice_in_dim(joint[0], order[r] * slice_d, slice_d, 0), ((0, extra), (0, 0)))
            for r in range(group)
        ]
    joint = {
        r: lax.dynamic_update_slice_in_dim(v, pick(rest, order[r]), slice_d, 0) for r, v in enumerate(joint)
    }
    line.last = [*line.last, grad_inputs]
    joint_steps = steps_of_scatter(joint, "seq")
    next(joint_steps)
    next(first_steps)
    next(second_steps)
    next(down_steps)
    for _ in range(levels - 1):
        next(joint_steps)
    next(first_steps)
    next(second_steps)
    next(down_steps)
    joint_mine, joint_got = next(joint_steps)
    keep, send = add_split(joint_mine, joint_got, 1, which[0], line.last)
    line.mark(keep)
    joint_steps = steps_of_sum(line, keep[0], send[0], 1, last=F32)
    next(joint_steps)
    next(second_steps)
    next(first_steps)
    out_steps = steps_of_scatter(terms_out, "seq")
    next(out_steps)
    next(second_steps)
    for _ in range(2 * (depth - 3)):
        for steps in (down_steps, first_steps, second_steps, joint_steps):
            next(steps)
    next(first_steps)
    next(joint_steps)
    next(down_steps)
    next(second_steps)
    next(joint_steps)
    next(first_steps)
    for _ in range(levels - 1):
        next(out_steps)
    next(joint_steps)
    down_sum = next(down_steps).reshape(slice_f, width)
    next(first_steps)
    second = next(second_steps)
    next(joint_steps)
    out_mine, out_got = next(out_steps)
    layer_out = (residual + out_mine.astype(F32) + out_got.astype(F32)).astype(BF16)
    next(joint_steps)
    first = next(first_steps)
    joint = next(joint_steps).reshape(joint_rows, joint_width)
    rest = joint[slice_d]
    lows, highs = [], []
    for i, done in enumerate((first, second)):
        columns = done.shape[-1]
        for kept, v in zip((lows, highs), done):
            v = jnp.moveaxis(v, depth - 1, 0).reshape(group, slice_d, columns)
            kept.append((cuts[i] * FB, v))
    gate_sum = join(lows, firsts, hidden_units)
    up_sum = join(highs, firsts, hidden_units)
    return (
        layer_out[None],
        grad_inputs[None],
        rest[:slice_d],
        joint[:slice_d, :qkv_width],
        rest[2 * slice_d : 2 * slice_d + slice_b],
        joint[:slice_d, qkv_width:],
        rest[slice_d : 2 * slice_d],
        gate_sum,
        up_sum,
        down_sum,
    )


def solution(mesh):
    return jax.shard_map(
        per_device,
        mesh=mesh,
        in_specs=(
            P("dp", "seq", None),
            P("dp", None),
            P("dp", "seq", None),
            P("seq"),
            P("seq", None),
            P("seq"),
            P("seq", None),
            P("seq"),
            P("seq", None),
            P("seq", None),
            P("seq", None),
        ),
        out_specs=(
            P("dp", "seq", None),
            P("dp", "seq", None),
            P("seq"),
            P("seq", None),
            P("seq"),
            P("seq", None),
            P("seq"),
            P("seq", None),
            P("seq", None),
            P("seq", None),
        ),
        check_vma=False,
    )
```

time: 1070 us -> 468 us (0.44)
  waiting for transfers between devices: 554 us -> 181 us
  matrix products: 277 us -> 0 us
  Pallas kernels: 0 us -> 133 us
  starting transfers between devices: 0.99 us -> 81.6 us
  loops' own time: 54.9 us -> 0 us
  blocking collectives: 54.5 us -> 0 us
  local copies, waits for them, and re-layouts: 62.1 us -> 39.6 us
  between operations: 17.6 us -> 2.44 us
  other arithmetic: 37.2 us -> 23.9 us
    dot_general x113 -> x0, matrix products: 277 us -> none  [the longest x47 102 us: dot_last(): lax.dot_general(left, right, (((1,), (1,)), ((), ())), preferred_element_...]
    reduce_scatter x5 -> x0, waiting for transfers between devices: 257 us -> none  [the longest x1 76.4 us: per_device(): lax.psum_scatter(grad_up_w.astype(jnp.bfloat16), 'seq', scatter_dimension...]
    psum x1 -> x0, waiting for transfers between devices: 207 us -> none  [per_device(): lax.psum(sliced[1].astype(jnp.bfloat16), 'dp').astype(jnp.float32)]
    ppermute x0 -> x67, waiting for transfers between devices: none -> 181 us  [swap(): lax.ppermute(x, axis, [(i, i ^ mask) for i in range(lax.axis_size(axis))])]
    pallas_call x0 -> x39, Pallas kernels: none -> 133 us  [the longest x2 37 us: feed(): pl.pallas_call(functools.partial(feed_kernel, blocks), out_shape=(tall, w...]
    ppermute x0 -> x67, starting transfers between devices: none -> 81.6 us  [swap(): lax.ppermute(x, axis, [(i, i ^ mask) for i in range(lax.axis_size(axis))])]
    another operation x2 -> x0, loops' own time: 54.9 us -> none  [the longest x1 27.5 us: per_device(): lax.map(head_backward, (query_heads, grad_heads, log_totals, group_ids))]
    all_gather x5 -> x0, waiting for transfers between devices: 51.2 us -> none  [the longest x1 40.9 us: per_device(): lax.all_gather(w_down, 'seq', axis=0, tiled=True)]
  transfers between devices with their start and end apart: 13 -> 67, of which waited for: 9 -> 26; matrix products, arithmetic and copies ran while one was open for 17% -> 8% of each run, Pallas kernels for 0% -> 29%
where the time goes in v1:
time: 468 us; the launch traced here: 462 us
  waiting for transfers between devices  181 us (39%)
  Pallas kernels  133 us (28%)
  starting transfers between devices  81.6 us (17%)
  local copies, waits for them, and re-layouts  39.6 us (8%)
  other arithmetic  23.9 us (5%)
    ppermute x67, waiting for transfers between devices, swap(): lax.ppermute(x, axis, [(i, i ^ mask) for i in range(lax.axis_size(axis))])  181 us
    ppermute x67, starting transfers between devices, swap(): lax.ppermute(x, axis, [(i, i ^ mask) for i in range(lax.axis_size(axis))])  81.6 us
    pallas_call x2, Pallas kernels, feed(): pl.pallas_call(functools.partial(feed_kernel, blocks), out_shape=(tall, w...  37 us
    pallas_call x27, Pallas kernels, small_call(): pl.pallas_call(body, out_shape=out_shape, grid_spec=pltpu.PrefetchScalarG...  31.3 us
    unnamed x146, local copies, waits for them, and re-layouts  23.2 us
    pallas_call x2, Pallas kernels, grad_gate_up_of(): pl.pallas_call(functools.partial(gate_up_kernel, len(grads), len(hiddens)...  16.1 us
    pallas_call x3, Pallas kernels, single_call(): pl.pallas_call(body, out_shape=outs, grid_spec=pltpu.PrefetchScalarGridSp...  13 us
    pallas_call x1, Pallas kernels, grad_down_of(): pl.pallas_call(functools.partial(down_kernel, len(products), len(cots) //...  10.4 us
  transfers between devices with their start and end apart: 67, of which 26 were waited for; matrix products, arithmetic and copies ran while one was open for 8% of the time, Pallas kernels for 29%

profile of v1, /device:TPU:0, one launch (start us, length us, event | category | flops | bytes accessed | tf_op | source)
XLA Modules:
  0.0 461.9 jit_solution(10468691712904709876)
XLA Ops:
  27.3 3.8 norm_project_rotate.1
  37.7 7.0 %collective-permute-done.12.rest_2_ = bf16[224,896]{1,0:T(8,128)(2,1)} collective-permute-done((bf16[224,896]{1,0:T(8,128)(2,1)}, bf16[224,896]{1,0:T(8,128)(2,1)}, u32[]{:S(2)}, u32[]{:S(2)}) %collective-permute-start.12) | collective-permute-done | bytes 401440 | tf_op jit(solution)/shard_map/ppermute | solution.py:36
  51.3 7.9 %attention_forward.1 = (bf16[384,896]{1,0:T(8,128)(2,1)S(1)}, bf16[3,2,64,896]{3,2,1,0:T(8,128)(2,1)S(1)}, bf16[3,2,64,896]{3,2,1,0:T(8,128)(2,1)S(1)}, f32[3,2,1,896]{3,2,1,0:T(1,128)S(1)}) custom-call(s32[10]{0:T(128)S(1)} %pad_add_fusion.2.bounds, f32[384,896]{1,0:T(8,128)S(1)} %get-tuple-element.83.pq_ref, f32[32,384]{1,0:T(8,128)S(1)} %get-tuple-element.193.cos_ref, ...), custom_call_target="tpu_custom_call" | custom-call | flops 4194304 | bytes 262144 | tf_op jit(solution)/shard_map/attention_forward/pallas_call | solution.py:246
  64.3 8.7 %collective-permute-start.17 = (bf16[384,896]{1,0:T(8,128)(2,1)S(1)}, bf16[384,896]{1,0:T(8,128)(2,1)S(1)}, u32[]{:S(2)}, u32[]{:S(2)}) collective-permute-start(bf16[384,896]{1,0:T(8,128)(2,1)S(1)} %get-tuple-element.88.refs_0_.refs_4_), channel_id=1, source_target_pairs={{0,2},{1,3},{2,0},{3,1},{4,6},{5,7},{6,4},{7,5},{8,10},{9,11},{10,... | collective-permute-start | bytes 2064392 | tf_op jit(solution)/shard_map/ppermute | solution.py:36
  75.8 10.6 %collective-permute-done.17.refs_0_.refs_6_ = bf16[384,896]{1,0:T(8,128)(2,1)S(1)} collective-permute-done((bf16[384,896]{1,0:T(8,128)(2,1)S(1)}, bf16[384,896]{1,0:T(8,128)(2,1)S(1)}, u32[]{:S(2)}, u32[]{:S(2)}) %collective-permute-start.17) | collective-permute-done | bytes 688160 | tf_op jit(solution)/shard_map/ppermute | solution.py:36
  92.5 7.9 %collective-permute-done.24.refs_2_.refs_4_ = bf16[384,896]{1,0:T(8,128)(2,1)} collective-permute-done((bf16[384,896]{1,0:T(8,128)(2,1)}, bf16[384,896]{1,0:T(8,128)(2,1)}, u32[]{:S(2)}, u32[]{:S(2)}) %collective-permute-start.24) | collective-permute-done | bytes 688160 | tf_op jit(solution)/shard_map/ppermute | solution.py:36
  105.2 18.4 %feed_forward_backward.2 = (bf16[1280,768]{1,0:T(8,128)(2,1)}, bf16[2,768,1280]{2,1,0:T(8,128)(2,1)}, bf16[384,896]{1,0:T(8,128)(2,1)S(1)}, bf16[384,896]{1,0:T(...) custom-call(s32[6]{0:T(128)S(1)} %stack.165.offsets, ...), custom_call_target="tpu_custom_call" | custom-call | flops 4194304 | bytes 262144 | tf_op jit(solution)/shard_map/feed_forward_backward/pallas_call | solution.py:489
  124.5 18.6 %feed_forward_backward.3 = (bf16[1280,768]{1,0:T(8,128)(2,1)}, bf16[2,768,1280]{2,1,0:T(8,128)(2,1)}, bf16[384,896]{1,0:T(8,128)(2,1)S(1)}, bf16[384,896]{1,0:T(...) custom-call(s32[6]{0:T(128)S(1)} %stack.165.offsets, ...), custom_call_target="tpu_custom_call" | custom-call | flops 4194304 | bytes 262144 | tf_op jit(solution)/shard_map/feed_forward_backward/pallas_call | solution.py:489
  145.1 10.4 %grad_down.1 = (bf16[608,896]{1,0:T(8,128)(2,1)}, bf16[608,896]{1,0:T(8,128)(2,1)}) custom-call(s32[2]{0:T(128)} %get-tuple-element.156.offsets, bf16[1280,768]{1,0:T(8,128)(2,1)} %get-tuple-element.105.refs_0_, bf16[1280,768]{1,0:T(8,128)(2,1)} %get-tuple-element.106.refs_1_, bf16[384,896]{1,0:T(8,128)(2,1)} %bitcast.20.refs_2_, ...), custom_call_target="tpu_custom_call" | custom-call | flops 4194304 | bytes 262144 | tf_op jit(solution)/shard_map/grad_down/pallas_call | solution.py:549
  158.1 9.4 %grad_gate_up.2 = (bf16[896,768]{1,0:T(8,128)(2,1)}, bf16[896,768]{1,0:T(8,128)(2,1)}, bf16[896,1536]{1,0:T(8,128)(2,1)}) custom-call(s32[1]{0:T(128)} %bitcast.32.which.scalar_ref, bf16[2,768,1280]{2,1,0:T(8,128)(2,1)} %get-tuple-element.103.refs_0_.refs_2_, bf16[2,768,1280]{2,1,0:T(8,128)(2,1)} %get-tuple-element.104.refs_1_.refs_3_, ...), custom_call_target="tpu_custom_call" | custom-call | flops 4194304 | bytes 262144 | tf_op jit(solution)/shard_map/grad_gate_up/pallas_call | solution.py:600
  167.5 6.7 %grad_gate_up.3 = (bf16[896,512]{1,0:T(8,128)(2,1)}, bf16[896,512]{1,0:T(8,128)(2,1)}) custom-call(s32[1]{0:T(128)} %bitcast.31.which, bf16[2,768,1280]{2,1,0:T(8,128)(2,1)} %get-tuple-element.103.refs_0_.refs_2_, bf16[2,768,1280]{2,1,0:T(8,128)(2,1)} %get-tuple-element.104.refs_1_.refs_3_, bf16[2,768,1280]{2,1,0:T(8,128)(2,1)} %get-tuple-element.103.refs_0_.refs_2_, ...), custom_call_target="tpu_custom_call" | custom-call | flops 4194304 | bytes 262144 | tf_op jit(solution)/shard_map/grad_gate_up/pallas_call | solution.py:600
  177.1 16.8 %collective-permute-done.30.refs_1_ = bf16[384,896]{1,0:T(8,128)(2,1)} collective-permute-done((bf16[384,896]{1,0:T(8,128)(2,1)}, bf16[384,896]{1,0:T(8,128)(2,1)}, u32[]{:S(2)}, u32[]{:S(2)}) %collective-permute-start.30) | collective-permute-done | bytes 688160 | tf_op jit(solution)/shard_map/ppermute | solution.py:36
  193.9 4.3 norm_back.1
  199.9 10.4 %attention_backward.1 = (bf16[384,896]{1,0:T(8,128)(2,1)S(1)}, bf16[384,256]{1,0:T(8,128)(2,1)S(1)}, bf16[384,256]{1,0:T(8,128)(2,1)}, bf16[384,256]{1,0:T(8,128)(2,1)S(1)}, bf16[384,256]{1,0:T(8,128)(2,1)}) custom-call(s32[10]{0:T(128)S(1)} %copy-done.62, bf16[3,2,64,896]{3,2,1,0:T(8,128)(2,1)S(1)} %copy-done.34, bf16[3,2,64,896]{3,2,1,0:T(8,128)(2,1)S(1)} %copy-done.36, ...), custom_call_target="tpu_custom_call" | custom-call | flops 4194304 | bytes 262144 | tf_op jit(solution)/shard_map/attention_backward/pallas_call | solution.py:296
  217.5 9.1 %collective-permute-start.34 = (bf16[384,256]{1,0:T(8,128)(2,1)S(1)}, bf16[384,256]{1,0:T(8,128)(2,1)S(1)}, u32[]{:S(2)}, u32[]{:S(2)}) collective-permute-start(bf16[384,256]{1,0:T(8,128)(2,1)S(1)} %add_convert_fusion.7), channel_id=1, source_target_pairs={{0,2},{1,3},{2,0},{3,1},{4,6},{5,7},{6,4},{7,5},{8,10},{9,11},{10,... | collective-permute-start | bytes 589832 | tf_op jit(solution)/shard_map/ppermute | solution.py:36
  231.7 8.7 %project_back.1 = (f32[384,896]{1,0:T(8,128)}, f32[1,896]{1,0:T(1,128)S(1)}, f32[1,1152]{1,0:T(1,128)S(1)}, bf16[256,2048]{1,0:T(8,128)(2,1)}, bf16[256,2048]{1,...) custom-call(s32[4]{0:T(128)S(1)} %get-tuple-element.158.scalar_ref, ...), custom_call_target="tpu_custom_call" | custom-call | flops 4194304 | bytes 262144 | tf_op jit(solution)/shard_map/project_back/pallas_call | solution.py:635
  249.0 3.5 add_and_split.12
  258.4 5.9 %collective-permute-start.39 = (bf16[256,2048]{1,0:T(8,128)(2,1)}, bf16[256,2048]{1,0:T(8,128)(2,1)S(1)}, u32[]{:S(2)}, u32[]{:S(2)}) collective-permute-start(bf16[256,2048]{1,0:T(8,128)(2,1)} %add_convert_fusion), channel_id=1, source_target_pairs={{0,2},{1,3},{2,0},{3,1},{4,6},{5,7},{6,4},{7,5},{8,10},{9,11},{10,... | collective-permute-start | bytes 3145736 | tf_op jit(solution)/shard_map/ppermute | solution.py:36
  264.3 8.2 %collective-permute-done.41 = bf16[4,112,512]{2,1,0:T(8,128)(2,1)} collective-permute-done((bf16[4,112,512]{2,1,0:T(8,128)(2,1)}, bf16[4,112,512]{2,1,0:T(8,128)(2,1)}, u32[]{:S(2)}, u32[]{:S(2)}) %collective-permute-start.41) | collective-permute-done | bytes 458784 | tf_op jit(solution)/shard_map/ppermute | solution.py:36
  282.1 3.8 collective-permute-done.45
  290.4 12.2 %collective-permute-done.43 = bf16[152,896]{1,0:T(8,128)(2,1)S(1)} collective-permute-done((bf16[152,896]{1,0:T(8,128)(2,1)S(1)}, bf16[152,896]{1,0:T(8,128)(2,1)S(1)}, u32[]{:S(2)}, u32[]{:S(2)}) %collective-permute-start.43) | collective-permute-done | bytes 272416 | tf_op jit(solution)/shard_map/ppermute | solution.py:36
  307.4 5.2 %collective-permute-start.49 = (bf16[1,56,512]{2,1,0:T(8,128)(2,1)S(1)}, bf16[1,56,512]{2,1,0:T(8,128)(2,1)S(1)}, u32[]{:S(2)}, u32[]{:S(2)}) collective-permute-start(bf16[1,56,512]{2,1,0:T(8,128)(2,1)S(1)} %get-tuple-element.146), channel_id=1, source_target_pairs={{0,2},{1,3},{2,0},{3,1},{4,6},{5,7},{6,4},{7,5},{8,10},{9,11},{10,... | collective-permute-start | bytes 172040 | tf_op jit(solution)/shard_map/ppermute | solution.py:36
  318.6 5.5 %collective-permute-done.54.refs_1_ = bf16[4,56,512]{2,1,0:T(8,128)(2,1)S(1)} collective-permute-done((bf16[4,56,512]{2,1,0:T(8,128)(2,1)S(1)}, bf16[4,56,512]{2,1,0:T(8,128)(2,1)S(1)}, u32[]{:S(2)}, u32[]{:S(2)}) %collective-permute-start.54) | collective-permute-done | bytes 229408 | tf_op jit(solution)/shard_map/ppermute | solution.py:36
  324.2 5.7 %collective-permute-start.52 = (bf16[1,56,768]{2,1,0:T(8,128)(2,1)S(1)}, bf16[1,56,768]{2,1,0:T(8,128)(2,1)S(1)}, u32[]{:S(2)}, u32[]{:S(2)}) collective-permute-start(bf16[1,56,768]{2,1,0:T(8,128)(2,1)S(1)} %get-tuple-element.150), channel_id=1, source_target_pairs={{0,2},{1,3},{2,0},{3,1},{4,6},{5,7},{6,4},{7,5},{8,10},{9,11},{10,... | collective-permute-start | bytes 258056 | tf_op jit(solution)/shard_map/ppermute | solution.py:36
  340.4 22.2 %collective-permute-done.56 = bf16[2,4,56,512]{3,2,1,0:T(8,128)(2,1)S(1)} collective-permute-done((bf16[2,4,56,512]{3,2,1,0:T(8,128)(2,1)S(1)}, bf16[2,4,56,512]{3,2,1,0:T(8,128)(2,1)S(1)}, u32[]{:S(2)}, u32[]{:S(2)}) %collective-permute-start.56) | collective-permute-done | bytes 458784 | tf_op jit(solution)/shard_map/ppermute | solution.py:36
  363.7 5.1 %collective-permute-done.59.refs_1_ = bf16[4,56,768]{2,1,0:T(8,128)(2,1)S(1)} collective-permute-done((bf16[4,56,768]{2,1,0:T(8,128)(2,1)S(1)}, bf16[4,56,768]{2,1,0:T(8,128)(2,1)S(1)}, u32[]{:S(2)}, u32[]{:S(2)}) %collective-permute-start.59) | collective-permute-done | bytes 344096 | tf_op jit(solution)/shard_map/ppermute | solution.py:36
  373.1 14.1 %collective-permute-done.58.refs_1_ = bf16[1,32,2048]{2,1,0:T(8,128)(2,1)S(1)} collective-permute-done((bf16[1,32,2048]{2,1,0:T(8,128)(2,1)S(1)}, bf16[1,32,2048]{2,1,0:T(8,128)(2,1)S(1)}, u32[]{:S(2)}, u32[]{:S(2)}) %collective-permute-start.58) | collective-permute-done | bytes 131104 | tf_op jit(solution)/shard_map/ppermute | solution.py:36
  392.2 13.7 %collective-permute-done.62 = bf16[2,4,56,768]{3,2,1,0:T(8,128)(2,1)S(1)} collective-permute-done((bf16[2,4,56,768]{3,2,1,0:T(8,128)(2,1)S(1)}, bf16[2,4,56,768]{3,2,1,0:T(8,128)(2,1)S(1)}, u32[]{:S(2)}, u32[]{:S(2)}) %collective-permute-start.62) | collective-permute-done | bytes 688160 | tf_op jit(solution)/shard_map/ppermute | solution.py:36
  411.8 6.8 %collective-permute-done.60 = bf16[32,2048]{1,0:T(8,128)(2,1)S(1)} collective-permute-done((bf16[32,2048]{1,0:T(8,128)(2,1)S(1)}, bf16[32,2048]{1,0:T(8,128)(2,1)S(1)}, u32[]{:S(2)}, u32[]{:S(2)}) %collective-permute-start.60) | collective-permute-done | bytes 131104 | tf_op jit(solution)/shard_map/ppermute | solution.py:36
  420.4 7.0 %collective-permute-done.64.refs_1_ = bf16[2,32,2048]{2,1,0:T(8,128)(2,1)S(1)} collective-permute-done((bf16[2,32,2048]{2,1,0:T(8,128)(2,1)S(1)}, bf16[2,32,2048]{2,1,0:T(8,128)(2,1)S(1)}, u32[]{:S(2)}, u32[]{:S(2)}) %collective-permute-start.64) | collective-permute-done | bytes 262176 | tf_op jit(solution)/shard_map/ppermute | solution.py:36
  429.0 13.1 %collective-permute-done.66 = bf16[2,2,4,56,768]{4,3,2,1,0:T(8,128)(2,1)S(1)} collective-permute-done((bf16[2,2,4,56,768]{4,3,2,1,0:T(8,128)(2,1)S(1)}, bf16[2,2,4,56,768]{4,3,2,1,0:T(8,128)(2,1)S(1)}, u32[]{:S(2)}, u32[]{:S(2)}) %collective-permute-start.66) | collective-permute-done | bytes 1376288 | tf_op jit(solution)/shard_map/ppermute | solution.py:36
  443.4 9.1 %collective-permute-done.65 = bf16[2,2,32,2048]{3,2,1,0:T(8,128)(2,1)S(1)} collective-permute-done((bf16[2,2,32,2048]{3,2,1,0:T(8,128)(2,1)S(1)}, bf16[2,2,32,2048]{3,2,1,0:T(8,128)(2,1)S(1)}, u32[]{:S(2)}, u32[]{:S(2)}) %collective-permute-start.65) | collective-permute-done | bytes 524320 | tf_op jit(solution)/shard_map/ppermute | solution.py:36
  (386 shorter events, 159.7 us)
Async XLA Ops:
  1.9 19.8 %collective-permute-start.1 = (bf16[1,736]{1,0:T(2,128)(2,1)S(1)}, bf16[1,736]{1,0:T(2,128)(2,1)S(1)}, u32[]{:S(2)}, u32[]{:S(2)}) collective-permute-start(bf16[1,736]{1,0:T(2,128)(2,1)S(1)} %broadcast_in_dim.58), channel_id=1, source_target_pairs={{0,2},{1,3},{2,0},{3,1},{4,6},{5,7},{6,4},{7,5},{8,10},{9,11},{10,... | collective-permute-start | bytes 4424 | tf_op jit(solution)/shard_map/ppermute | solution.py:36
  37.7 23.3 %collective-permute-start.11 = (bf16[224,896]{1,0:T(8,128)(2,1)}, bf16[224,896]{1,0:T(8,128)(2,1)}, u32[]{:S(2)}, u32[]{:S(2)}) collective-permute-start(bf16[224,896]{1,0:T(8,128)(2,1)} %get-tuple-element.86.rest_0_), channel_id=1, source_target_pairs={{0,1},{1,0},{2,3},{3,2},{4,5},{5,4},{6,7},{7,6},{8,9},{9,8},{10,11... | collective-permute-start | bytes 1204232 | tf_op jit(solution)/shard_map/ppermute | solution.py:36
  50.3 39.8 %collective-permute-start.19 = (bf16[2,224,1280]{2,1,0:T(8,128)(2,1)}, bf16[2,224,1280]{2,1,0:T(8,128)(2,1)S(1)}, u32[]{:S(2)}, u32[]{:S(2)}) collective-permute-start(bf16[2,224,1280]{2,1,0:T(8,128)(2,1)} %get-tuple-element.160), channel_id=1, source_target_pairs={{0,1},{1,0},{2,3},{3,2},{4,5},{5,4},{6,7},{7,6},{8,9},{9,8},{10,11... | collective-permute-start | bytes 3440648 | tf_op jit(solution)/shard_map/ppermute | solution.py:36
  64.3 22.1 %collective-permute-start.17 = (bf16[384,896]{1,0:T(8,128)(2,1)S(1)}, bf16[384,896]{1,0:T(8,128)(2,1)S(1)}, u32[]{:S(2)}, u32[]{:S(2)}) collective-permute-start(bf16[384,896]{1,0:T(8,128)(2,1)S(1)} %get-tuple-element.88.refs_0_.refs_4_), channel_id=1, source_target_pairs={{0,2},{1,3},{2,0},{3,1},{4,6},{5,7},{6,4},{7,5},{8,10},{9,11},{10,... | collective-permute-start | bytes 2064392 | tf_op jit(solution)/shard_map/ppermute | solution.py:36
  92.5 32.1 %collective-permute-start.23 = (bf16[384,896]{1,0:T(8,128)(2,1)S(1)}, bf16[384,896]{1,0:T(8,128)(2,1)}, u32[]{:S(2)}, u32[]{:S(2)}) collective-permute-start(bf16[384,896]{1,0:T(8,128)(2,1)S(1)} %collective-permute-done.17.refs_0_.refs_6_), channel_id=1, source_target_pairs={{0,1},{1,0},{2,3},{3,2},{4,5},{5,4},{6,7},{7,6},{8,9},{9,8},{10,11... | collective-permute-start | bytes 2064392 | tf_op jit(solution)/shard_map/ppermute | solution.py:36
  100.4 24.2 %collective-permute-start.25 = (bf16[384,896]{1,0:T(8,128)(2,1)}, bf16[384,896]{1,0:T(8,128)(2,1)}, u32[]{:S(2)}, u32[]{:S(2)}) collective-permute-start(bf16[384,896]{1,0:T(8,128)(2,1)} %collective-permute-done.24.refs_2_.refs_4_), channel_id=1, source_target_pairs={{0,1},{1,0},{2,3},{3,2},{4,5},{5,4},{6,7},{7,6},{8,9},{9,8},{10,11... | collective-permute-start | bytes 2064392 | tf_op jit(solution)/shard_map/ppermute | solution.py:36
  124.5 32.6 %collective-permute-start.28 = (bf16[384,896]{1,0:T(8,128)(2,1)S(1)}, bf16[384,896]{1,0:T(8,128)(2,1)S(1)}, u32[]{:S(2)}, u32[]{:S(2)}) collective-permute-start(bf16[384,896]{1,0:T(8,128)(2,1)S(1)} %get-tuple-element.99), channel_id=1, source_target_pairs={{0,1},{1,0},{2,3},{3,2},{4,5},{5,4},{6,7},{7,6},{8,9},{9,8},{10,11... | collective-permute-start | bytes 2064392 | tf_op jit(solution)/shard_map/ppermute | solution.py:36
  144.0 31.7 %collective-permute-start.29 = (bf16[384,896]{1,0:T(8,128)(2,1)S(1)}, bf16[384,896]{1,0:T(8,128)(2,1)S(1)}, u32[]{:S(2)}, u32[]{:S(2)}) collective-permute-start(bf16[384,896]{1,0:T(8,128)(2,1)S(1)} %get-tuple-element.101), channel_id=1, source_target_pairs={{0,1},{1,0},{2,3},{3,2},{4,5},{5,4},{6,7},{7,6},{8,9},{9,8},{10,11... | collective-permute-start | bytes 2064392 | tf_op jit(solution)/shard_map/ppermute | solution.py:36
  155.6 42.6 %collective-permute-start.31 = (bf16[608,896]{1,0:T(8,128)(2,1)}, bf16[608,896]{1,0:T(8,128)(2,1)S(1)}, u32[]{:S(2)}, u32[]{:S(2)}) collective-permute-start(bf16[608,896]{1,0:T(8,128)(2,1)} %get-tuple-element.111), channel_id=1, source_target_pairs={{0,4},{4,0},{8,12},{12,8},{16,20},{20,16},{24,28},{28,24},{1,5},{5... | collective-permute-start | bytes 3268616 | tf_op jit(solution)/shard_map/ppermute | solution.py:36
  174.2 38.9 %collective-permute-start.36 = (bf16[896,512]{1,0:T(8,128)(2,1)}, bf16[896,512]{1,0:T(8,128)(2,1)}, u32[]{:S(2)}, u32[]{:S(2)}) collective-permute-start(bf16[896,512]{1,0:T(8,128)(2,1)} %get-tuple-element.121), channel_id=1, source_target_pairs={{0,8},{4,12},{8,0},{12,4},{16,24},{20,28},{24,16},{28,20},{1,9},{5... | collective-permute-start | bytes 2752520 | tf_op jit(solution)/shard_map/ppermute | solution.py:36
  211.7 35.0 %collective-permute-start.42 = (bf16[896,768]{1,0:T(8,128)(2,1)}, bf16[896,768]{1,0:T(8,128)(2,1)}, u32[]{:S(2)}, u32[]{:S(2)}) collective-permute-start(bf16[896,768]{1,0:T(8,128)(2,1)} %get-tuple-element.135), channel_id=1, source_target_pairs={{0,4},{4,0},{8,12},{12,8},{16,20},{20,16},{24,28},{28,24},{1,5},{5... | collective-permute-start | bytes 4128776 | tf_op jit(solution)/shard_map/ppermute | solution.py:36
  242.2 30.3 %collective-permute-start.41 = (bf16[4,112,512]{2,1,0:T(8,128)(2,1)}, bf16[4,112,512]{2,1,0:T(8,128)(2,1)}, u32[]{:S(2)}, u32[]{:S(2)}) collective-permute-start(bf16[4,112,512]{2,1,0:T(8,128)(2,1)} %get-tuple-element.133), channel_id=1, source_target_pairs={{0,16},{4,20},{8,24},{12,28},{16,0},{20,4},{24,8},{28,12},{1,17},{... | collective-permute-start | bytes 1376264 | tf_op jit(solution)/shard_map/ppermute | solution.py:36
  246.2 57.1 %collective-permute-start.37 = (bf16[256,2048]{1,0:T(8,128)(2,1)}, bf16[256,2048]{1,0:T(8,128)(2,1)}, u32[]{:S(2)}, u32[]{:S(2)}) collective-permute-start(bf16[256,2048]{1,0:T(8,128)(2,1)} %dynamic_update_slice.33), channel_id=1, source_target_pairs={{0,1},{1,0},{2,3},{3,2},{4,5},{5,4},{6,7},{7,6},{8,9},{9,8},{10,11... | collective-permute-start | bytes 3145736 | tf_op jit(solution)/shard_map/ppermute | solution.py:36
  246.4 31.6 %collective-permute-start.40 = (bf16[1,152,896]{2,1,0:T(8,128)(2,1)}, bf16[1,152,896]{2,1,0:T(8,128)(2,1)}, u32[]{:S(2)}, u32[]{:S(2)}) collective-permute-start(bf16[1,152,896]{2,1,0:T(8,128)(2,1)} %get-tuple-element.132), channel_id=1, source_target_pairs={{0,16},{4,20},{8,24},{12,28},{16,0},{20,4},{24,8},{28,12},{1,17},{... | collective-permute-start | bytes 817160 | tf_op jit(solution)/shard_map/ppermute | solution.py:36
  252.5 33.5 %collective-permute-start.45 = (bf16[4,112,768]{2,1,0:T(8,128)(2,1)}, bf16[4,112,768]{2,1,0:T(8,128)(2,1)}, u32[]{:S(2)}, u32[]{:S(2)}) collective-permute-start(bf16[4,112,768]{2,1,0:T(8,128)(2,1)} %get-tuple-element.139), channel_id=1, source_target_pairs={{0,8},{4,12},{8,0},{12,4},{16,24},{20,28},{24,16},{28,20},{1,9},{5... | collective-permute-start | bytes 2064392 | tf_op jit(solution)/shard_map/ppermute | solution.py:36
  258.4 46.4 %collective-permute-start.39 = (bf16[256,2048]{1,0:T(8,128)(2,1)}, bf16[256,2048]{1,0:T(8,128)(2,1)S(1)}, u32[]{:S(2)}, u32[]{:S(2)}) collective-permute-start(bf16[256,2048]{1,0:T(8,128)(2,1)} %add_convert_fusion), channel_id=1, source_target_pairs={{0,2},{1,3},{2,0},{3,1},{4,6},{5,7},{6,4},{7,5},{8,10},{9,11},{10,... | collective-permute-start | bytes 3145736 | tf_op jit(solution)/shard_map/ppermute | solution.py:36
  279.0 23.6 %collective-permute-start.43 = (bf16[152,896]{1,0:T(8,128)(2,1)S(1)}, bf16[152,896]{1,0:T(8,128)(2,1)S(1)}, u32[]{:S(2)}, u32[]{:S(2)}) collective-permute-start(bf16[152,896]{1,0:T(8,128)(2,1)S(1)} %bitcast.237), channel_id=1, source_target_pairs={{0,16},{4,20},{8,24},{12,28},{16,0},{20,4},{24,8},{28,12},{1,17},{... | collective-permute-start | bytes 817160 | tf_op jit(solution)/shard_map/ppermute | solution.py:36
  288.1 29.4 %collective-permute-start.47 = (bf16[4,56,768]{2,1,0:T(8,128)(2,1)S(1)}, bf16[4,56,768]{2,1,0:T(8,128)(2,1)S(1)}, u32[]{:S(2)}, u32[]{:S(2)}) collective-permute-start(bf16[4,56,768]{2,1,0:T(8,128)(2,1)S(1)} %get-tuple-element.144), channel_id=1, source_target_pairs={{0,16},{4,20},{8,24},{12,28},{16,0},{20,4},{24,8},{28,12},{1,17},{... | collective-permute-start | bytes 1032200 | tf_op jit(solution)/shard_map/ppermute | solution.py:36
  290.3 22.2 %collective-permute-start.48 = (bf16[1,56,512]{2,1,0:T(8,128)(2,1)S(1)}, bf16[1,56,512]{2,1,0:T(8,128)(2,1)S(1)}, u32[]{:S(2)}, u32[]{:S(2)}) collective-permute-start(bf16[1,56,512]{2,1,0:T(8,128)(2,1)S(1)} %get-tuple-element.145), channel_id=1, source_target_pairs={{0,1},{1,0},{2,3},{3,2},{4,5},{5,4},{6,7},{7,6},{8,9},{9,8},{10,11... | collective-permute-start | bytes 172040 | tf_op jit(solution)/shard_map/ppermute | solution.py:36
  303.1 32.2 %collective-permute-start.57 = (bf16[2,152,896]{2,1,0:T(8,128)(2,1)S(1)}, bf16[2,152,896]{2,1,0:T(8,128)(2,1)S(1)}, u32[]{:S(2)}, u32[]{:S(2)}) collective-permute-start(bf16[2,152,896]{2,1,0:T(8,128)(2,1)S(1)} %bitcast.221), channel_id=1, source_target_pairs={{0,8},{4,12},{8,0},{12,4},{16,24},{20,28},{24,16},{28,20},{1,9},{5... | collective-permute-start | bytes 1634312 | tf_op jit(solution)/shard_map/ppermute | solution.py:36
  305.8 29.3 %collective-permute-start.46 = (bf16[128,2048]{1,0:T(8,128)(2,1)}, bf16[128,2048]{1,0:T(8,128)(2,1)S(1)}, u32[]{:S(2)}, u32[]{:S(2)}) collective-permute-start(bf16[128,2048]{1,0:T(8,128)(2,1)} %bitcast.61), channel_id=1, source_target_pairs={{0,4},{4,0},{8,12},{12,8},{16,20},{20,16},{24,28},{28,24},{1,5},{5... | collective-permute-start | bytes 1572872 | tf_op jit(solution)/shard_map/ppermute | solution.py:36
  317.4 52.1 %collective-permute-start.26 = (bf16[384,896]{1,0:T(8,128)(2,1)}, bf16[384,896]{1,0:T(8,128)(2,1)}, u32[]{:S(2)}, u32[]{:S(2)}) collective-permute-start(bf16[384,896]{1,0:T(8,128)(2,1)} %get-tuple-element.93), channel_id=1, source_target_pairs={{0,1},{1,0},{2,3},{3,2},{4,5},{5,4},{6,7},{7,6},{8,9},{9,8},{10,11... | collective-permute-start | bytes 2064392 | tf_op jit(solution)/shard_map/ppermute | solution.py:36
  332.6 30.0 %collective-permute-start.56 = (bf16[2,4,56,512]{3,2,1,0:T(8,128)(2,1)S(1)}, bf16[2,4,56,512]{3,2,1,0:T(8,128)(2,1)S(1)}, u32[]{:S(2)}, u32[]{:S(2)}) collective-permute-start(bf16[2,4,56,512]{3,2,1,0:T(8,128)(2,1)S(1)} %place.16.refs_4_), channel_id=1, source_target_pairs={{0,16},{4,20},{8,24},{12,28},{16,0},{20,4},{24,8},{28,12},{1,17},{... | collective-permute-start | bytes 1376264 | tf_op jit(solution)/shard_map/ppermute | solution.py:36
  336.1 53.1 %collective-permute-start.63 = (bf16[2,2,152,896]{3,2,1,0:T(8,128)(2,1)S(1)}, bf16[2,2,152,896]{3,2,1,0:T(8,128)(2,1)S(1)}, u32[]{:S(2)}, u32[]{:S(2)}) collective-permute-start(bf16[2,2,152,896]{3,2,1,0:T(8,128)(2,1)S(1)} %place.18.refs_2_), channel_id=1, source_target_pairs={{0,4},{4,0},{8,12},{12,8},{16,20},{20,16},{24,28},{28,24},{1,5},{5... | collective-permute-start | bytes 3268616 | tf_op jit(solution)/shard_map/ppermute | solution.py:36
  337.7 31.1 %collective-permute-start.59 = (bf16[4,56,768]{2,1,0:T(8,128)(2,1)S(1)}, bf16[4,56,768]{2,1,0:T(8,128)(2,1)S(1)}, u32[]{:S(2)}, u32[]{:S(2)}) collective-permute-start(bf16[4,56,768]{2,1,0:T(8,128)(2,1)S(1)} %bitcast.235), channel_id=1, source_target_pairs={{0,16},{4,20},{8,24},{12,28},{16,0},{20,4},{24,8},{28,12},{1,17},{... | collective-permute-start | bytes 1032200 | tf_op jit(solution)/shard_map/ppermute | solution.py:36
  339.5 24.0 %collective-permute-start.55 = (bf16[1,64,2048]{2,1,0:T(8,128)(2,1)S(1)}, bf16[1,64,2048]{2,1,0:T(8,128)(2,1)S(1)}, u32[]{:S(2)}, u32[]{:S(2)}) collective-permute-start(bf16[1,64,2048]{2,1,0:T(8,128)(2,1)S(1)} %get-tuple-element.153), channel_id=1, source_target_pairs={{0,8},{4,12},{8,0},{12,4},{16,24},{20,28},{24,16},{28,20},{1,9},{5... | collective-permute-start | bytes 786440 | tf_op jit(solution)/shard_map/ppermute | solution.py:36
  362.6 56.5 %collective-permute-start.22 = (bf16[384,896]{1,0:T(8,128)(2,1)S(1)}, bf16[384,896]{1,0:T(8,128)(2,1)S(1)}, u32[]{:S(2)}, u32[]{:S(2)}) collective-permute-start(bf16[384,896]{1,0:T(8,128)(2,1)S(1)} %copy-done.64), channel_id=1, source_target_pairs={{0,1},{1,0},{2,3},{3,2},{4,5},{5,4},{6,7},{7,6},{8,9},{9,8},{10,11... | collective-permute-start | bytes 2064392 | tf_op jit(solution)/shard_map/ppermute | solution.py:36
  363.5 47.1 %collective-permute-start.61 = (bf16[2,2,4,56,512]{4,3,2,1,0:T(8,128)(2,1)S(1)}, bf16[2,2,4,56,512]{4,3,2,1,0:T(8,128)(2,1)S(1)}, u32[]{:S(2)}, u32[]{:S(2)}) collective-permute-start(bf16[2,2,4,56,512]{4,3,2,1,0:T(8,128)(2,1)S(1)} %bitcast.204), channel_id=1, source_target_pairs={{0,8},{4,12},{8,0},{12,4},{16,24},{20,28},{24,16},{28,20},{1,9},{5... | collective-permute-start | bytes 2752520 | tf_op jit(solution)/shard_map/ppermute | solution.py:36
  369.5 36.4 %collective-permute-start.62 = (bf16[2,4,56,768]{3,2,1,0:T(8,128)(2,1)S(1)}, bf16[2,4,56,768]{3,2,1,0:T(8,128)(2,1)S(1)}, u32[]{:S(2)}, u32[]{:S(2)}) collective-permute-start(bf16[2,4,56,768]{3,2,1,0:T(8,128)(2,1)S(1)} %place.20.refs_2_), channel_id=1, source_target_pairs={{0,8},{4,12},{8,0},{12,4},{16,24},{20,28},{24,16},{28,20},{1,9},{5... | collective-permute-start | bytes 2064392 | tf_op jit(solution)/shard_map/ppermute | solution.py:36
  387.1 32.1 %collective-permute-start.27 = (bf16[384,896]{1,0:T(8,128)(2,1)S(1)}, bf16[384,896]{1,0:T(8,128)(2,1)S(1)}, u32[]{:S(2)}, u32[]{:S(2)}) collective-permute-start(bf16[384,896]{1,0:T(8,128)(2,1)S(1)} %add_convert_fusion.5), channel_id=1, source_target_pairs={{0,2},{1,3},{2,0},{3,1},{4,6},{5,7},{6,4},{7,5},{8,10},{9,11},{10,... | collective-permute-start | bytes 2064392 | tf_op jit(solution)/shard_map/ppermute | solution.py:36
  409.0 33.1 %collective-permute-start.66 = (bf16[2,2,4,56,768]{4,3,2,1,0:T(8,128)(2,1)S(1)}, bf16[2,2,4,56,768]{4,3,2,1,0:T(8,128)(2,1)S(1)}, u32[]{:S(2)}, u32[]{:S(2)}) collective-permute-start(bf16[2,2,4,56,768]{4,3,2,1,0:T(8,128)(2,1)S(1)} %bitcast.194), channel_id=1, source_target_pairs={{0,4},{4,0},{8,12},{12,8},{16,20},{20,16},{24,28},{28,24},{1,5},{5... | collective-permute-start | bytes 4128776 | tf_op jit(solution)/shard_map/ppermute | solution.py:36
  428.1 24.4 %collective-permute-start.65 = (bf16[2,2,32,2048]{3,2,1,0:T(8,128)(2,1)S(1)}, bf16[2,2,32,2048]{3,2,1,0:T(8,128)(2,1)S(1)}, u32[]{:S(2)}, u32[]{:S(2)}) collective-permute-start(bf16[2,2,32,2048]{3,2,1,0:T(8,128)(2,1)S(1)} %place.25.refs_2_), channel_id=1, source_target_pairs={{0,4},{4,0},{8,12},{12,8},{16,20},{20,16},{24,28},{28,24},{1,5},{5... | collective-permute-start | bytes 1572872 | tf_op jit(solution)/shard_map/ppermute | solution.py:36
  (108 other events, 1113.7 us)

commit v2 on v1

--- a/solution.py
+++ b/solution.py
@@ -561,55 +561,59 @@
     )(offsets, *products, *cots, *waits)
 
 
-def gate_up_kernel(parts, blocks, waits, given, which, *refs):
-    keeps, sends, refs = refs[:parts], refs[parts : 2 * parts], refs[2 * parts :]
-    hs, refs = refs[:blocks], refs[blocks + waits :]
-    outs, refs = refs[:2], refs[2:]
-    if given:
-        (turned,) = hs
-    else:
-        (turned,) = refs
-
-        @pl.when(pl.program_id(0) == 0)
-        def _():
-            rows = hs[0].shape[0]
-            for t, h in enumerate(hs):
-                for at in range(0, rows, QB):
-                    place_at = slice(t * rows + at, t * rows + at + QB)
-                    turned[:, place_at] = h[at : at + QB, :].astype(F32).T.astype(BF16)
-
-    for out, group in zip(outs, (keeps, sends)):
-        total = None
+def gate_up_kernel(parts, blocks, total, *refs):
+    grads, hs, (out, turned) = refs[:parts], refs[parts : parts + blocks], refs[-2:]
+    groups, share = out.shape[1:3]
+    each = turned.shape[0] // groups
+
+    @pl.when(pl.program_id(0) == 0)
+    def _():
+        rows = hs[0].shape[0]
+        for t, h in enumerate(hs):
+            for at in range(0, rows, QB):
+                place_at = slice(t * rows + at, t * rows + at + QB)
+                turned[:, place_at] = h[at : at + QB, :].astype(F32).T.astype(BF16)
+
+    for i in range(2):
+        result = None
         first = 0
-        for v in group:
-            term = dot(turned[:, first : first + v.shape[1]], v[0])
-            total = term if total is None else total + term
+        for v in grads:
+            term = dot(turned[:, first : first + v.shape[1]], v[i])
+            result = term if result is None else result + term
             first += v.shape[1]
-        out[...] = total.astype(BF16)
-
-
-def grad_gate_up_of(grads, hiddens, first, count, which, waits):
-    given = len(hiddens) == 1
-    width = hiddens[0].shape[0] if given else hiddens[0].shape[1]
+        for k in range(total // 2):
+            for j in range(groups):
+                at = j * each + turned_bits(k, total // 2) * share
+                out[2 * k + i, j] = result[at : at + share].astype(BF16)
+
+
+def turned_bits(k, count):
+    out = 0
+    while count > 1:
+        out, k, count = out * 2 + k % 2, k // 2, count // 2
+    return out
+
+
+def grad_gate_up_of(grads, hiddens, groups, total, waits):
+    width = hiddens[0].shape[1]
     tokens = sum(v.shape[1] for v in grads)
-    out = jax.ShapeDtypeStruct((width, count * FB), BF16)
-    turned = jax.ShapeDtypeStruct((width, tokens), BF16)
-    place_of = pl.BlockSpec((width, FB), lambda j, *_: (0, j))
-    keep = [pl.BlockSpec((1, v.shape[1], FB), lambda j, at: (at[0], 0, j + first)) for v in grads]
-    send = [pl.BlockSpec((1, v.shape[1], FB), lambda j, at: (1 - at[0], 0, j + first)) for v in grads]
+    inner = grads[0].shape[2]
+    share = 2 * width // (groups * total)
     return pl.pallas_call(
-        functools.partial(gate_up_kernel, len(grads), len(hiddens), len(waits), given),
-        out_shape=(out, out) if given else (out, out, turned),
-        grid_spec=pltpu.PrefetchScalarGridSpec(
-            num_scalar_prefetch=1,
-            grid=(count,),
-            in_specs=[*keep, *send, *[whole(v.shape) for v in hiddens], *[ANY] * len(waits)],
-            out_specs=[place_of] * 2 if given else [place_of] * 2 + [whole((width, tokens))],
-        ),
+        functools.partial(gate_up_kernel, len(grads), len(hiddens), total),
+        out_shape=jax.ShapeDtypeStruct((total, groups, share, inner), BF16),
+        grid=(inner // FB,),
+        in_specs=[
+            *[pl.BlockSpec((2, v.shape[1], FB), lambda j: (0, 0, j)) for v in grads],
+            *[whole(v.shape) for v in hiddens],
+            *[ANY] * len(waits),
+        ],
+        out_specs=pl.BlockSpec((total, groups, share, FB), lambda j: (0, 0, 0, j)),
+        scratch_shapes=[pltpu.VMEM((width, tokens), BF16)],
         compiler_params=pltpu.CompilerParams(vmem_limit_bytes=56 << 20),
         cost_estimate=pl.CostEstimate(flops=1 << 22, bytes_accessed=1 << 18, transcendentals=0),
         name="grad_gate_up",
-    )(which, *grads, *grads, *hiddens, *waits)
+    )(*grads, *hiddens, *waits)
 
 
 def residual_back_kernel(mine_ref, got_ref, cot_ref, residual_ref, gain_ref, w_ref, *rest):
@@ -780,39 +784,36 @@
     return out.reshape((count,) + shape)
 
 
-def steps_of_sum(line, keep, send, lead, order=None, last=None, bits=None):
+def steps_of_sum(line, keep, send):
     index = lax.axis_index("dp")
     depth = lax.axis_size("dp").bit_length() - 1
-    masks = [1 << k for k in (range(depth) if bits is None else bits)]
-    bits = [((index // mask) & 1).astype(jnp.int32) for mask in masks]
-    pair = lambda k: jnp.stack([bits[k], 1 - bits[k]])
+    bits = [((index >> k) & 1).astype(jnp.int32) for k in range(depth)]
     columns = keep.shape[-1]
     for k in range(depth - 1):
-        got = swap(send, "dp", masks[k])
+        got = swap(send, "dp", 1 << k)
         yield None
-        keep, send = add_split(keep, got, lead, bits[k + 1], line.last)
+        keep, send = add_split(keep, got, 1, bits[k + 1], line.last)
         line.mark(keep)
-    got = swap(send, "dp", masks[-1])
+    got = swap(send, "dp", 1 << (depth - 1))
     yield None
-    keep = keep.reshape(lead, -1, columns)
-    if order is None:
-        (part,) = add_ordered(keep, got, jnp.zeros((1,), jnp.int32), line.last)
-        part = line.mark(part[0])
-    else:
-        parts = add_ordered(keep, got, order, line.last)
-        line.mark(parts[0])
-        parts = [swap(v, "seq", r) if r else v for r, v in enumerate(parts)]
+    part = line.mark(add(keep.reshape(1, -1, columns), got, line.last))
+    yield from steps_of_gather(line, part, reversed(range(depth)))
+
+
+def steps_of_gather(line, part, order):
+    index = lax.axis_index("dp")
+    order = list(order)
+    for k in order:
+        bit = ((index >> k) & 1).astype(jnp.int32)
+        got = swap(part, "dp", 1 << k)
         yield None
-        part = line.mark(put_ordered([v[0] for v in parts], order, line.last))
-    for k in reversed(range(1, depth)):
-        got = swap(part, "dp", masks[k])
-        yield None
-        part = line.mark(put_ordered([part, got], pair(k), line.last))
-    got = swap(part, "dp", masks[0])
-    yield None
-    part = put_ordered([part, got], pair(0), line.last, BF16 if last is None else last)
-    line.mark(part)
-    yield part
+        if k == order[-1]:
+            yield jnp.where(bit == 0, part, got), jnp.where(bit == 0, got, part)
+        part = line.mark(put_ordered([part, got], jnp.stack([bit, 1 - bit]), line.last))
+
+
+def add(x, got, waits):
+    return add_ordered(x, got, jnp.zeros((1,), jnp.int32), waits)[0]
 
 
 def steps_of_scatter(parts, axis):
@@ -960,8 +961,8 @@
     pieces = [pick(both, order[0]), swap(pick(both, order[1]), "seq", 1)]
     offsets = [order[0] * slice_d, order[1] * slice_d]
     for r in range(2, group):
-        later[r] = got = swap(early[r], "dp", 2)
-        part = jnp.stack([jnp.where(slow == 0, early[r], got), jnp.where(slow == 0, got, early[r])])
+        got = swap(early[r], "dp", 2)
+        later[r] = part = put_ordered([early[r], got], jnp.stack([slow, 1 - slow]), [])
         pieces += [part, swap(part, "dp", 1)]
         at = order[r] * slice_d
         offsets += [at + fast * half_d, at + (1 - fast) * half_d]
@@ -997,36 +998,34 @@
     order = jnp.stack(order).astype(jnp.int32)
     which = fast.astype(jnp.int32)[None]
 
-    back = steps_of_scatter(terms_back, "seq")
-    next(back)
+    for b in reversed(bits_down(group)):
+        got = {r: swap(terms_back[r ^ b], "seq", b) for r in terms_back if not r & b}
+        if b < group // 2:
+            terms_back = {
+                r: (terms_back[r].astype(F32) + v.astype(F32)).astype(BF16) for r, v in got.items()
+            }
+    back_mine, back_send, back_got = terms_back[0], terms_back[group // 2], got[0]
+    grad_gu = grad_gate_up_of(grads, hiddens, group, total, [])
     half_rows = slice_f // 2
     down_at = shift + half_rows * jnp.stack([fast, 1 - fast])
-    down_keep, down_send = grad_down_of(products, cots, down_at.astype(jnp.int32), half_rows, [])
-    down_steps = steps_of_sum(line, down_keep, down_send, 1, last=F32)
+    down_keep, down_send = grad_down_of(
+        products, cots, down_at.astype(jnp.int32), half_rows, [grad_gu, back_send]
+    )
+    grad_gu = lax.psum_scatter(
+        grad_gu.reshape(total * group * share, inner), "dp", scatter_dimension=0, tiled=True
+    ).reshape(group, share, inner)
+    down_steps = steps_of_sum(line, down_keep, down_send)
     next(down_steps)
-    for _ in range(levels - 1):
-        next(back)
-    back_mine, back_got = next(back)
-    first_keep, first_send, turned = grad_gate_up_of(
-        grads, hiddens, 0, cuts[1], which, [down_keep, back_mine]
-    )
-    second_keep, second_send = grad_gate_up_of(
-        grads, [turned], cuts[1], count - cuts[1], slow[None], []
-    )
     f32 = lambda *shape: jax.ShapeDtypeStruct(shape, F32)
     bf16 = lambda *shape: jax.ShapeDtypeStruct(shape, BF16)
 
     grad_residual, grad_mixed, grad_gain_two = single_call(
         lambda _, *refs: residual_back_kernel(*refs), "norm_back",
-        (back_mine, back_got, cot, residual, gain_two, full_out), [second_keep],
+        (back_mine, back_got, cot, residual, gain_two, full_out), [down_keep],
         [f32(rows, width), bf16(rows, width), f32(1, width)],
     )
     line.mark(grad_mixed)
     next(down_steps)
-    first_steps = steps_of_sum(line, first_keep, first_send, group, order)
-    next(first_steps)
-    second_steps = steps_of_sum(line, second_keep, second_send, group, order, bits=[*range(1, depth), 0])
-    next(second_steps)
     dq, *dkv = attention_backward(
         bounds, qt, ot, lse, grad_mixed, cos_t, sin_t, start_row, blocks, line.last
     )
@@ -1035,8 +1034,6 @@
     next(dkv_steps)
     for _ in range(levels - 1):
         next(dkv_steps)
-    next(second_steps)
-    next(down_steps)
     dkv_mine, dkv_got = next(dkv_steps)
     qkv_width = w_qkv.shape[1]
     joint_width = qkv_width + width
@@ -1070,54 +1067,62 @@
         r: lax.dynamic_update_slice_in_dim(v, pick(rest, order[r]), slice_d, 0) for r, v in enumerate(joint)
     }
     line.last = [*line.last, grad_inputs]
-    joint_steps = steps_of_scatter(joint, "seq")
-    next(joint_steps)
+    line.mark(grad_inputs)
+    for b in reversed(bits_down(group)):
+        got = {r: swap(joint[r ^ b], "seq", b) for r in joint if not r & b}
+        if b == group // 2:
+            next(down_steps)
+            for _ in range(2 * (depth - 3)):
+                next(down_steps)
+        joint = {r: line.mark(add(joint[r][None], v, line.last))[0] for r, v in got.items()}
+    joint = lax.all_to_all(joint[0], "dp", 0, 0, tiled=True)
+    next(down_steps)
+    next(down_steps)
+    moved = [pick(grad_gu, order[r]) for r in range(group)]
+    moved = [swap(v, "seq", r) if r else v for r, v in enumerate(moved)]
+    columns = inner // 2
+    parts = [
+        line.mark(put_ordered([v[:, at : at + columns] for v in moved], order, line.last))
+        for at in (0, columns)
+    ]
+    first_steps = steps_of_gather(line, parts[0], reversed(range(depth)))
     next(first_steps)
+    second_steps = steps_of_gather(line, parts[1], [0, *reversed(range(1, depth))])
     next(second_steps)
     next(down_steps)
-    for _ in range(levels - 1):
-        next(joint_steps)
-    next(first_steps)
-    next(second_steps)
-    next(down_steps)
-    joint_mine, joint_got = next(joint_steps)
-    keep, send = add_split(joint_mine, joint_got, 1, which[0], line.last)
-    line.mark(keep)
-    joint_steps = steps_of_sum(line, keep[0], send[0], 1, last=F32)
-    next(joint_steps)
-    next(second_steps)
-    next(first_steps)
     out_steps = steps_of_scatter(terms_out, "seq")
     next(out_steps)
     next(second_steps)
-    for _ in range(2 * (depth - 3)):
-        for steps in (down_steps, first_steps, second_steps, joint_steps):
-            next(steps)
     next(first_steps)
-    next(joint_steps)
-    next(down_steps)
-    next(second_steps)
-    next(joint_steps)
-    next(first_steps)
+    shape = (total, joint_rows // total, joint_width)
+
+    def spread(_, x, out):
+        out[...] = jnp.broadcast_to(jnp.sum(x[...].astype(F32), axis=0).astype(BF16)[None], shape)
+
+    (joint,) = single_call(spread, "sum_and_spread", (joint.reshape(shape),), line.last, [bf16(*shape)])
+    line.mark(joint)
+    joint = lax.all_to_all(joint.reshape(joint_rows, joint_width), "dp", 0, 0, tiled=True)
     for _ in range(levels - 1):
         next(out_steps)
-    next(joint_steps)
-    down_sum = next(down_steps).reshape(slice_f, width)
+    for _ in range(depth - 3):
+        next(first_steps)
+        next(second_steps)
+    low, high = next(down_steps)
+    down_sum = jnp.concatenate([low.reshape(-1, width), high.reshape(-1, width)]).astype(F32)
     next(first_steps)
-    second = next(second_steps)
-    next(joint_steps)
+    next(second_steps)
     out_mine, out_got = next(out_steps)
     layer_out = (residual + out_mine.astype(F32) + out_got.astype(F32)).astype(BF16)
-    next(joint_steps)
+    joint = joint.astype(F32)
+    second = jnp.stack(next(second_steps))
     first = next(first_steps)
-    joint = next(joint_steps).reshape(joint_rows, joint_width)
+    second = jnp.moveaxis(second, depth - 1, 0)
     rest = joint[slice_d]
     lows, highs = [], []
     for i, done in enumerate((first, second)):
-        columns = done.shape[-1]
         for kept, v in zip((lows, highs), done):
             v = jnp.moveaxis(v, depth - 1, 0).reshape(group, slice_d, columns)
-            kept.append((cuts[i] * FB, v))
+            kept.append((i * columns, v))
     gate_sum = join(lows, firsts, hidden_units)
     up_sum = join(highs, firsts, hidden_units)
     return (

time: 468 us -> 450 us (0.962)
  Pallas kernels: 133 us -> 115 us
  waiting for transfers between devices: 181 us -> 168 us
  between operations: 2.44 us -> 15.4 us
  starting transfers between devices: 81.6 us -> 75.5 us
  other arithmetic: 23.9 us -> 29.2 us
    ppermute x67 -> x52, starting transfers between devices: 81.6 us -> 64.3 us  [swap(): lax.ppermute(x, axis, [(i, i ^ mask) for i in range(lax.axis_size(axis))])]
    pallas_call x27 -> x16, Pallas kernels: 31.3 us -> 17.1 us  [small_call(): pl.pallas_call(body, out_shape=out_shape, grid_spec=pltpu.PrefetchScalarG...]
    ppermute x67 -> x52, waiting for transfers between devices: 181 us -> 168 us  [swap(): lax.ppermute(x, axis, [(i, i ^ mask) for i in range(lax.axis_size(axis))])]
    all_to_all x0 -> x2, starting transfers between devices: none -> 11.2 us  [the longest x1 6.32 us: per_device(): joint = lax.all_to_all(joint[0], 'dp', 0, 0, tiled=True)]
    convert_element_type x7 -> x3, other arithmetic: 9.88 us -> 2.23 us  [steps_of_scatter(): (parts[r].astype(F32) + v.astype(F32)).astype(BF16)]
    unnamed x18, other arithmetic: 0.59 us -> 7.43 us
    pallas_call x2 -> x1, Pallas kernels: 16.1 us -> 12.4 us  [grad_gate_up_of(): pl.pallas_call(functools.partial(gate_up_kernel, len(grads), len(hiddens)...]
    unnamed x146 -> x132, local copies, waits for them, and re-layouts: 23.2 us -> 25.7 us
  transfers between devices with their start and end apart: 67 -> 55, of which waited for: 26 -> 26; matrix products, arithmetic and copies ran while one was open for 8% -> 9% of each run, Pallas kernels for 29% -> 18%
where the time goes in v2:
time: 450 us; the launch traced here: 444 us
  waiting for transfers between devices  168 us (37%)
  Pallas kernels  115 us (26%)
  starting transfers between devices  75.5 us (17%)
  local copies, waits for them, and re-layouts  41.2 us (9%)
  other arithmetic  29.2 us (6%)
  between operations  15.4 us (3%)
    ppermute x52, waiting for transfers between devices, swap(): lax.ppermute(x, axis, [(i, i ^ mask) for i in range(lax.axis_size(axis))])  168 us
    ppermute x52, starting transfers between devices, swap(): lax.ppermute(x, axis, [(i, i ^ mask) for i in range(lax.axis_size(axis))])  64.3 us
    pallas_call x2, Pallas kernels, feed(): pl.pallas_call(functools.partial(feed_kernel, blocks), out_shape=(tall, w...  37.2 us
    unnamed x132, local copies, waits for them, and re-layouts  25.7 us
    pallas_call x16, Pallas kernels, small_call(): pl.pallas_call(body, out_shape=out_shape, grid_spec=pltpu.PrefetchScalarG...  17.1 us
    pallas_call x4, Pallas kernels, single_call(): pl.pallas_call(body, out_shape=outs, grid_spec=pltpu.PrefetchScalarGridSp...  15.4 us
    pallas_call x1, Pallas kernels, grad_gate_up_of(): pl.pallas_call(functools.partial(gate_up_kernel, len(grads), len(hiddens)...  12.4 us
    pallas_call x1, Pallas kernels, grad_down_of(): pl.pallas_call(functools.partial(down_kernel, len(products), len(cots) //...  10.2 us
  transfers between devices with their start and end apart: 55, of which 26 were waited for; matrix products, arithmetic and copies ran while one was open for 9% of the time, Pallas kernels for 18%

profile of v2, /device:TPU:0, one launch (start us, length us, event | category | flops | bytes accessed | tf_op | source)
XLA Modules:
  0.0 444.1 jit_solution(8667583693151769170)
XLA Ops:
  19.8 5.8 %collective-permute-done.4.rest_2_ = bf16[224,1152]{1,0:T(8,128)(2,1)} collective-permute-done((bf16[224,1152]{1,0:T(8,128)(2,1)}, bf16[224,1152]{1,0:T(8,128)(2,1)}, u32[]{:S(2)}, u32[]{:S(2)}) %collective-permute-start.4) | collective-permute-done | bytes 516128 | tf_op jit(solution)/shard_map/ppermute | solution.py:36
  29.2 3.9 norm_project_rotate.1
  45.4 5.9 %collective-permute-done.12.rest_2_ = bf16[224,896]{1,0:T(8,128)(2,1)} collective-permute-done((bf16[224,896]{1,0:T(8,128)(2,1)}, bf16[224,896]{1,0:T(8,128)(2,1)}, u32[]{:S(2)}, u32[]{:S(2)}) %collective-permute-start.12) | collective-permute-done | bytes 401440 | tf_op jit(solution)/shard_map/ppermute | solution.py:36
  55.9 4.8 %collective-permute-done.14 = bf16[112,1280]{1,0:T(8,128)(2,1)S(1)} collective-permute-done((bf16[112,1280]{1,0:T(8,128)(2,1)S(1)}, bf16[112,1280]{1,0:T(8,128)(2,1)S(1)}, u32[]{:S(2)}, u32[]{:S(2)}) %collective-permute-start.14) | collective-permute-done | bytes 286752 | tf_op jit(solution)/shard_map/ppermute | solution.py:36
  61.4 7.2 %attention_forward.1 = (bf16[384,896]{1,0:T(8,128)(2,1)S(1)}, bf16[3,2,64,896]{3,2,1,0:T(8,128)(2,1)S(1)}, bf16[3,2,64,896]{3,2,1,0:T(8,128)(2,1)S(1)}, f32[3,2,1,896]{3,2,1,0:T(1,128)S(1)}) custom-call(s32[10]{0:T(128)S(1)} %pad_add_fusion.2.bounds, f32[384,896]{1,0:T(8,128)S(1)} %copy-done.18, f32[32,384]{1,0:T(8,128)S(1)} %get-tuple-element.149.cos_ref, ...), custom_call_target="tpu_custom_call" | custom-call | flops 4194304 | bytes 262144 | tf_op jit(solution)/shard_map/attention_forward/pallas_call | solution.py:246
  72.8 8.7 %collective-permute-start.17 = (bf16[384,896]{1,0:T(8,128)(2,1)S(1)}, bf16[384,896]{1,0:T(8,128)(2,1)}, u32[]{:S(2)}, u32[]{:S(2)}) collective-permute-start(bf16[384,896]{1,0:T(8,128)(2,1)S(1)} %get-tuple-element.61.refs_0_.refs_2_), channel_id=1, source_target_pairs={{0,2},{1,3},{2,0},{3,1},{4,6},{5,7},{6,4},{7,5},{8,10},{9,11},{10,... | collective-permute-start | bytes 2064392 | tf_op jit(solution)/shard_map/ppermute | solution.py:36
  83.5 11.3 %collective-permute-done.17.refs_0_.refs_4_ = bf16[384,896]{1,0:T(8,128)(2,1)} collective-permute-done((bf16[384,896]{1,0:T(8,128)(2,1)S(1)}, bf16[384,896]{1,0:T(8,128)(2,1)}, u32[]{:S(2)}, u32[]{:S(2)}) %collective-permute-start.17) | collective-permute-done | bytes 688160 | tf_op jit(solution)/shard_map/ppermute | solution.py:36
  99.8 4.8 %collective-permute-done.21.refs_9_ = bf16[2,112,1280]{2,1,0:T(8,128)(2,1)S(1)} collective-permute-done((bf16[2,112,1280]{2,1,0:T(8,128)(2,1)S(1)}, bf16[2,112,1280]{2,1,0:T(8,128)(2,1)S(1)}, u32[]{:S(2)}, u32[]{:S(2)}) %collective-permute-start.21) | collective-permute-done | bytes 573472 | tf_op jit(solution)/shard_map/ppermute | solution.py:36
  111.6 18.6 %feed_forward_backward.2 = (bf16[1280,768]{1,0:T(8,128)(2,1)}, bf16[2,768,1280]{2,1,0:T(8,128)(2,1)}, bf16[384,896]{1,0:T(8,128)(2,1)S(1)}, bf16[384,896]{1,0:T(...) custom-call(s32[6]{0:T(128)S(1)} %stack.157.offsets, ...), custom_call_target="tpu_custom_call" | custom-call | flops 4194304 | bytes 262144 | tf_op jit(solution)/shard_map/feed_forward_backward/pallas_call | solution.py:489
  131.9 18.6 %feed_forward_backward.3 = (bf16[1280,768]{1,0:T(8,128)(2,1)}, bf16[2,768,1280]{2,1,0:T(8,128)(2,1)}, bf16[384,896]{1,0:T(8,128)(2,1)S(1)}, bf16[384,896]{1,0:T(...) custom-call(s32[6]{0:T(128)S(1)} %stack.157.offsets, ...), custom_call_target="tpu_custom_call" | custom-call | flops 4194304 | bytes 262144 | tf_op jit(solution)/shard_map/feed_forward_backward/pallas_call | solution.py:489
  153.1 12.4 %grad_gate_up.1.refs_6_ = bf16[8,4,56,1280]{3,2,1,0:T(8,128)(2,1)} custom-call(bf16[2,768,1280]{2,1,0:T(8,128)(2,1)} %get-tuple-element.78.refs_0_, bf16[2,768,1280]{2,1,0:T(8,128)(2,1)} %get-tuple-element.79.refs_1_, bf16[384,896]{1,0:T(8,128)(2,1)} %copy-done.5, bf16[384,896]{1,0:T(8,128)(2,1)} %collective-permute-done.16.refs_1_.refs_3_, ...), custom_call_target="tpu_custom_call" | custom-call | flops 4194304 | bytes 262144 | tf_op jit(solution)/shard_map/grad_gate_up/pallas_call | solution.py:602
  169.9 10.2 %grad_down.1 = (bf16[608,896]{1,0:T(8,128)(2,1)}, bf16[608,896]{1,0:T(8,128)(2,1)}) custom-call(s32[2]{0:T(128)} %fusion.9.offsets, bf16[1280,768]{1,0:T(8,128)(2,1)} %get-tuple-element.76.refs_0_, bf16[1280,768]{1,0:T(8,128)(2,1)} %get-tuple-element.77.refs_1_, bf16[384,896]{1,0:T(8,128)(2,1)} %bitcast.28.refs_2_, ...), custom_call_target="tpu_custom_call" | custom-call | flops 4194304 | bytes 262144 | tf_op jit(solution)/shard_map/grad_down/pallas_call | solution.py:549
  184.0 15.5 %collective-permute-done.30.refs_1_ = bf16[384,896]{1,0:T(8,128)(2,1)S(1)} collective-permute-done((bf16[384,896]{1,0:T(8,128)(2,1)S(1)}, bf16[384,896]{1,0:T(8,128)(2,1)S(1)}, u32[]{:S(2)}, u32[]{:S(2)}) %collective-permute-start.30) | collective-permute-done | bytes 688160 | tf_op jit(solution)/shard_map/ppermute | solution.py:36
  200.4 4.3 norm_back.1
  204.7 8.1 %collective-permute-done.31 = bf16[608,896]{1,0:T(8,128)(2,1)S(1)} collective-permute-done((bf16[608,896]{1,0:T(8,128)(2,1)}, bf16[608,896]{1,0:T(8,128)(2,1)S(1)}, u32[]{:S(2)}, u32[]{:S(2)}) %collective-permute-start.31) | collective-permute-done | bytes 1089568 | tf_op jit(solution)/shard_map/ppermute | solution.py:36
  214.6 8.6 %attention_backward.1 = (bf16[384,896]{1,0:T(8,128)(2,1)S(1)}, bf16[384,256]{1,0:T(8,128)(2,1)S(1)}, bf16[384,256]{1,0:T(8,128)(2,1)S(1)}, bf16[384,256]{1,0:T(8,128)(2,1)S(1)}, bf16[384,256]{1,0:T(8,128)(2,1)S(1)}) custom-call(s32[10]{0:T(128)S(1)} %pad_add_fusion.2.bounds, bf16[3,2,64,896]{3,2,1,0:T(8,128)(2,1)S(1)} %copy-done.28, ...), custom_call_target="tpu_custom_call" | custom-call | flops 4194304 | bytes 262144 | tf_op jit(solution)/shard_map/attention_backward/pallas_call | solution.py:296
  226.2 9.4 %collective-permute-start.34 = (bf16[384,256]{1,0:T(8,128)(2,1)S(1)}, bf16[384,256]{1,0:T(8,128)(2,1)S(1)}, u32[]{:S(2)}, u32[]{:S(2)}) collective-permute-start(bf16[384,256]{1,0:T(8,128)(2,1)S(1)} %add_convert_fusion.5), channel_id=1, source_target_pairs={{0,2},{1,3},{2,0},{3,1},{4,6},{5,7},{6,4},{7,5},{8,10},{9,11},{10,... | collective-permute-start | bytes 589832 | tf_op jit(solution)/shard_map/ppermute | solution.py:36
  235.7 5.1 %collective-permute-done.34.refs_5_ = bf16[384,256]{1,0:T(8,128)(2,1)S(1)} collective-permute-done((bf16[384,256]{1,0:T(8,128)(2,1)S(1)}, bf16[384,256]{1,0:T(8,128)(2,1)S(1)}, u32[]{:S(2)}, u32[]{:S(2)}) %collective-permute-start.34) | collective-permute-done | bytes 196640 | tf_op jit(solution)/shard_map/ppermute | solution.py:36
  240.8 8.7 %project_back.1 = (f32[384,896]{1,0:T(8,128)}, f32[1,896]{1,0:T(1,128)S(1)}, f32[1,1152]{1,0:T(1,128)S(1)}, bf16[256,2048]{1,0:T(8,128)(2,1)}, bf16[256,2048]{1,...) custom-call(s32[4]{0:T(128)S(1)} %get-tuple-element.102.scalar_ref, ...), custom_call_target="tpu_custom_call" | custom-call | flops 4194304 | bytes 262144 | tf_op jit(solution)/shard_map/project_back/pallas_call | solution.py:639
  265.3 12.5 %collective-permute-done.38 = bf16[1,304,896]{2,1,0:T(8,128)(2,1)S(1)} collective-permute-done((bf16[1,304,896]{2,1,0:T(8,128)(2,1)}, bf16[1,304,896]{2,1,0:T(8,128)(2,1)S(1)}, u32[]{:S(2)}, u32[]{:S(2)}) %collective-permute-start.38) | collective-permute-done | bytes 544800 | tf_op jit(solution)/shard_map/ppermute | solution.py:36
  280.9 5.7 %collective-permute-done.37 = bf16[256,2048]{1,0:T(8,128)(2,1)} collective-permute-done((bf16[256,2048]{1,0:T(8,128)(2,1)S(1)}, bf16[256,2048]{1,0:T(8,128)(2,1)}, u32[]{:S(2)}, u32[]{:S(2)}) %collective-permute-start.37) | collective-permute-done | bytes 1048608 | tf_op jit(solution)/shard_map/ppermute | solution.py:36
  289.1 3.5 collective-permute-done.42.refs_1_
  293.3 6.3 %all-to-all-start = ((bf16[8,32,2048]{2,1,0:T(8,128)(2,1)}), bf16[8,32,2048]{2,1,0:T(8,128)(2,1)}, u32[]{:S(2)}, u32[]{:S(2)}) async-start(bf16[8,32,2048]{2,1,0:T(8,128)(2,1)} %bitcast.51), calls=%async_computation | async-start | bytes 2097152 | tf_op jit(solution)/shard_map/all_to_all | solution.py:1078
  299.7 12.5 %collective-permute-done.43.refs_1_ = bf16[1,152,896]{2,1,0:T(8,128)(2,1)S(1)} collective-permute-done((bf16[1,152,896]{2,1,0:T(8,128)(2,1)S(1)}, bf16[1,152,896]{2,1,0:T(8,128)(2,1)S(1)}, u32[]{:S(2)}, u32[]{:S(2)}) %collective-permute-start.43) | collective-permute-done | bytes 272416 | tf_op jit(solution)/shard_map/ppermute | solution.py:36
  314.6 5.5 %collective-permute-done.41 = bf16[56,1280]{1,0:T(8,128)(2,1)S(1)} collective-permute-done((bf16[56,1280]{1,0:T(8,128)(2,1)S(1)}, bf16[56,1280]{1,0:T(8,128)(2,1)S(1)}, u32[]{:S(2)}, u32[]{:S(2)}) %collective-permute-start.41) | collective-permute-done | bytes 143392 | tf_op jit(solution)/shard_map/ppermute | solution.py:36
  322.1 3.7 collective-permute-start.44
  326.4 4.3 collective-permute-start.45
  330.7 7.7 %collective-permute-done.46 = bf16[2,1,152,896]{3,2,0,1:T(8,128)(2,1)S(1)} collective-permute-done((bf16[2,1,152,896]{3,2,0,1:T(8,128)(2,1)S(1)}, bf16[2,1,152,896]{3,2,0,1:T(8,128)(2,1)S(1)}, u32[]{:S(2)}, u32[]{:S(2)}) %collective-permute-start.46) | collective-permute-done | bytes 544800 | tf_op jit(solution)/shard_map/ppermute | solution.py:36
  348.4 20.3 %collective-permute-done.47 = bf16[2,4,56,640]{3,2,1,0:T(8,128)(2,1)S(1)} collective-permute-done((bf16[2,4,56,640]{3,2,1,0:T(8,128)(2,1)S(1)}, bf16[2,4,56,640]{3,2,1,0:T(8,128)(2,1)S(1)}, u32[]{:S(2)}, u32[]{:S(2)}) %collective-permute-start.47) | collective-permute-done | bytes 573472 | tf_op jit(solution)/shard_map/ppermute | solution.py:36
  372.2 5.6 %place.19 = bf16[2,8,56,640]{3,2,1,0:T(8,128)(2,1)} custom-call(s32[2]{0:T(128)S(1)} %pad_add_fusion.5.scalar_ref, bf16[8,56,640]{2,1,0:T(8,128)(2,1)S(1)} %bitcast.219, bf16[8,56,640]{2,1,0:T(8,128)(2,1)} %bitcast.85.refs_1_, bf16[2,2,4,56,640]{4,3,2,1,0:T(8,128)(2,1)S(1)} %bitcast.201), custom_call_target="tpu_custom_call" | custom-call | flops 1048576 | bytes 262144 | tf_op jit(solution)/shard_map/place/pallas_call | solution.py:714
  380.7 4.9 %all-to-all-start.1 = ((bf16[8,32,2048]{2,1,0:T(8,128)(2,1)}), bf16[8,32,2048]{2,1,0:T(8,128)(2,1)S(1)}, u32[]{:S(2)}, u32[]{:S(2)}) async-start(bf16[8,32,2048]{2,1,0:T(8,128)(2,1)} %sum_and_spread.1.refs_2_), calls=%async_computation.2 | async-start | bytes 2097152 | tf_op jit(solution)/shard_map/all_to_all | solution.py:1104
  391.5 26.1 %collective-permute-done.50 = bf16[2,2,4,56,640]{4,3,2,1,0:T(8,128)(2,1)} collective-permute-done((bf16[2,2,4,56,640]{4,3,2,1,0:T(8,128)(2,1)}, bf16[2,2,4,56,640]{4,3,2,1,0:T(8,128)(2,1)}, u32[]{:S(2)}, u32[]{:S(2)}) %collective-permute-start.50) | collective-permute-done | bytes 1146912 | tf_op jit(solution)/shard_map/ppermute | solution.py:36
  (343 shorter events, 138.2 us)
Async XLA Ops:
  7.2 305.6 %reduce-scatter.2.cloned.1.call-start = ((), (), s32[]{:S(2)}) async-start(), calls=%async_computation.3 | async-start | bytes 5160960 | tf_op jit(solution)/shard_map/reduce_scatter | solution.py:1014
  8.0 20.8 %collective-permute-start.2 = (bf16[1,736]{1,0:T(2,128)(2,1)S(1)}, bf16[1,736]{1,0:T(2,128)(2,1)S(1)}, u32[]{:S(2)}, u32[]{:S(2)}) collective-permute-start(bf16[1,736]{1,0:T(2,128)(2,1)S(1)} %broadcast_in_dim.50), channel_id=1, source_target_pairs={{0,3},{1,2},{2,1},{3,0},{4,7},{5,6},{6,5},{7,4},{8,11},{9,10},{10,... | collective-permute-start | bytes 4424 | tf_op jit(solution)/shard_map/ppermute | solution.py:36
  10.4 18.0 %collective-permute-start.1 = (bf16[1,736]{1,0:T(2,128)(2,1)S(1)}, bf16[1,736]{1,0:T(2,128)(2,1)S(1)}, u32[]{:S(2)}, u32[]{:S(2)}) collective-permute-start(bf16[1,736]{1,0:T(2,128)(2,1)S(1)} %broadcast_in_dim.50), channel_id=1, source_target_pairs={{0,2},{1,3},{2,0},{3,1},{4,6},{5,7},{6,4},{7,5},{8,10},{9,11},{10,... | collective-permute-start | bytes 4424 | tf_op jit(solution)/shard_map/ppermute | solution.py:36
  11.1 15.3 %collective-permute-start = (bf16[1,736]{1,0:T(2,128)(2,1)S(1)}, bf16[1,736]{1,0:T(2,128)(2,1)S(1)}, u32[]{:S(2)}, u32[]{:S(2)}) collective-permute-start(bf16[1,736]{1,0:T(2,128)(2,1)S(1)} %broadcast_in_dim.50), channel_id=1, source_target_pairs={{0,1},{1,0},{2,3},{3,2},{4,5},{5,4},{6,7},{7,6},{8,9},{9,8},{10,11... | collective-permute-start | bytes 4424 | tf_op jit(solution)/shard_map/ppermute | solution.py:36
  11.1 18.0 %collective-permute-start.3 = (bf16[224,1152]{1,0:T(8,128)(2,1)}, bf16[224,1152]{1,0:T(8,128)(2,1)S(1)}, u32[]{:S(2)}, u32[]{:S(2)}) collective-permute-start(bf16[224,1152]{1,0:T(8,128)(2,1)} %rest_0_.1), channel_id=1, source_target_pairs={{0,1},{1,0},{2,3},{3,2},{4,5},{5,4},{6,7},{7,6},{8,9},{9,8},{10,11... | collective-permute-start | bytes 1548296 | tf_op jit(solution)/shard_map/ppermute | solution.py:36
  40.9 28.7 %collective-permute-start.11 = (bf16[224,896]{1,0:T(8,128)(2,1)}, bf16[224,896]{1,0:T(8,128)(2,1)}, u32[]{:S(2)}, u32[]{:S(2)}) collective-permute-start(bf16[224,896]{1,0:T(8,128)(2,1)} %get-tuple-element.59.rest_0_), channel_id=1, source_target_pairs={{0,1},{1,0},{2,3},{3,2},{4,5},{5,4},{6,7},{7,6},{8,9},{9,8},{10,11... | collective-permute-start | bytes 1204232 | tf_op jit(solution)/shard_map/ppermute | solution.py:36
  51.3 18.3 %collective-permute-start.13 = (bf16[224,896]{1,0:T(8,128)(2,1)}, bf16[224,896]{1,0:T(8,128)(2,1)}, u32[]{:S(2)}, u32[]{:S(2)}) collective-permute-start(bf16[224,896]{1,0:T(8,128)(2,1)} %collective-permute-done.12.rest_2_), channel_id=1, source_target_pairs={{0,1},{1,0},{2,3},{3,2},{4,5},{5,4},{6,7},{7,6},{8,9},{9,8},{10,11... | collective-permute-start | bytes 1204232 | tf_op jit(solution)/shard_map/ppermute | solution.py:36
  72.8 22.0 %collective-permute-start.17 = (bf16[384,896]{1,0:T(8,128)(2,1)S(1)}, bf16[384,896]{1,0:T(8,128)(2,1)}, u32[]{:S(2)}, u32[]{:S(2)}) collective-permute-start(bf16[384,896]{1,0:T(8,128)(2,1)S(1)} %get-tuple-element.61.refs_0_.refs_2_), channel_id=1, source_target_pairs={{0,2},{1,3},{2,0},{3,1},{4,6},{5,7},{6,4},{7,5},{8,10},{9,11},{10,... | collective-permute-start | bytes 2064392 | tf_op jit(solution)/shard_map/ppermute | solution.py:36
  81.4 17.5 %collective-permute-start.20 = (bf16[2,112,1280]{2,1,0:T(8,128)(2,1)S(1)}, bf16[2,112,1280]{2,1,0:T(8,128)(2,1)S(1)}, u32[]{:S(2)}, u32[]{:S(2)}) collective-permute-start(bf16[2,112,1280]{2,1,0:T(8,128)(2,1)S(1)} %bitcast.213), channel_id=1, source_target_pairs={{0,4},{4,0},{8,12},{12,8},{16,20},{20,16},{24,28},{28,24},{1,5},{5... | collective-permute-start | bytes 1720328 | tf_op jit(solution)/shard_map/ppermute | solution.py:36
  83.0 21.6 %collective-permute-start.21 = (bf16[2,112,1280]{2,1,0:T(8,128)(2,1)S(1)}, bf16[2,112,1280]{2,1,0:T(8,128)(2,1)S(1)}, u32[]{:S(2)}, u32[]{:S(2)}) collective-permute-start(bf16[2,112,1280]{2,1,0:T(8,128)(2,1)S(1)} %bitcast.209), channel_id=1, source_target_pairs={{0,4},{4,0},{8,12},{12,8},{16,20},{20,16},{24,28},{28,24},{1,5},{5... | collective-permute-start | bytes 1720328 | tf_op jit(solution)/shard_map/ppermute | solution.py:36
  105.4 26.5 %collective-permute-start.23 = (bf16[384,896]{1,0:T(8,128)(2,1)}, bf16[384,896]{1,0:T(8,128)(2,1)}, u32[]{:S(2)}, u32[]{:S(2)}) collective-permute-start(bf16[384,896]{1,0:T(8,128)(2,1)} %collective-permute-done.17.refs_0_.refs_4_), channel_id=1, source_target_pairs={{0,1},{1,0},{2,3},{3,2},{4,5},{5,4},{6,7},{7,6},{8,9},{9,8},{10,11... | collective-permute-start | bytes 2064392 | tf_op jit(solution)/shard_map/ppermute | solution.py:36
  108.2 23.8 %collective-permute-start.25 = (bf16[384,896]{1,0:T(8,128)(2,1)}, bf16[384,896]{1,0:T(8,128)(2,1)}, u32[]{:S(2)}, u32[]{:S(2)}) collective-permute-start(bf16[384,896]{1,0:T(8,128)(2,1)} %collective-permute-done.24.refs_2_.refs_4_), channel_id=1, source_target_pairs={{0,1},{1,0},{2,3},{3,2},{4,5},{5,4},{6,7},{7,6},{8,9},{9,8},{10,11... | collective-permute-start | bytes 2064392 | tf_op jit(solution)/shard_map/ppermute | solution.py:36
  180.1 32.7 %collective-permute-start.31 = (bf16[608,896]{1,0:T(8,128)(2,1)}, bf16[608,896]{1,0:T(8,128)(2,1)S(1)}, u32[]{:S(2)}, u32[]{:S(2)}) collective-permute-start(bf16[608,896]{1,0:T(8,128)(2,1)} %get-tuple-element.82), channel_id=1, source_target_pairs={{0,4},{4,0},{8,12},{12,8},{16,20},{20,16},{24,28},{28,24},{1,5},{5... | collective-permute-start | bytes 3268616 | tf_op jit(solution)/shard_map/ppermute | solution.py:36
  181.7 17.8 %collective-permute-start.30 = (bf16[384,896]{1,0:T(8,128)(2,1)S(1)}, bf16[384,896]{1,0:T(8,128)(2,1)S(1)}, u32[]{:S(2)}, u32[]{:S(2)}) collective-permute-start(bf16[384,896]{1,0:T(8,128)(2,1)S(1)} %copy-done.58), channel_id=1, source_target_pairs={{0,2},{1,3},{2,0},{3,1},{4,6},{5,7},{6,4},{7,5},{8,10},{9,11},{10,... | collective-permute-start | bytes 2064392 | tf_op jit(solution)/shard_map/ppermute | solution.py:36
  226.2 14.6 %collective-permute-start.34 = (bf16[384,256]{1,0:T(8,128)(2,1)S(1)}, bf16[384,256]{1,0:T(8,128)(2,1)S(1)}, u32[]{:S(2)}, u32[]{:S(2)}) collective-permute-start(bf16[384,256]{1,0:T(8,128)(2,1)S(1)} %add_convert_fusion.5), channel_id=1, source_target_pairs={{0,2},{1,3},{2,0},{3,1},{4,6},{5,7},{6,4},{7,5},{8,10},{9,11},{10,... | collective-permute-start | bytes 589832 | tf_op jit(solution)/shard_map/ppermute | solution.py:36
  261.3 25.3 %collective-permute-start.37 = (bf16[256,2048]{1,0:T(8,128)(2,1)S(1)}, bf16[256,2048]{1,0:T(8,128)(2,1)}, u32[]{:S(2)}, u32[]{:S(2)}) collective-permute-start(bf16[256,2048]{1,0:T(8,128)(2,1)S(1)} %bitcast.227), channel_id=1, source_target_pairs={{0,2},{1,3},{2,0},{3,1},{4,6},{5,7},{6,4},{7,5},{8,10},{9,11},{10,... | collective-permute-start | bytes 3145736 | tf_op jit(solution)/shard_map/ppermute | solution.py:36
  263.1 14.6 %collective-permute-start.38 = (bf16[1,304,896]{2,1,0:T(8,128)(2,1)}, bf16[1,304,896]{2,1,0:T(8,128)(2,1)S(1)}, u32[]{:S(2)}, u32[]{:S(2)}) collective-permute-start(bf16[1,304,896]{2,1,0:T(8,128)(2,1)} %get-tuple-element.99), channel_id=1, source_target_pairs={{0,8},{4,12},{8,0},{12,4},{16,24},{20,28},{24,16},{28,20},{1,9},{5... | collective-permute-start | bytes 1634312 | tf_op jit(solution)/shard_map/ppermute | solution.py:36
  277.9 14.7 %collective-permute-start.42 = (bf16[1,152,896]{2,1,0:T(8,128)(2,1)S(1)}, bf16[1,152,896]{2,1,0:T(8,128)(2,1)S(1)}, u32[]{:S(2)}, u32[]{:S(2)}) collective-permute-start(bf16[1,152,896]{2,1,0:T(8,128)(2,1)S(1)} %get-tuple-element.101), channel_id=1, source_target_pairs={{0,16},{4,20},{8,24},{12,28},{16,0},{20,4},{24,8},{28,12},{1,17},{... | collective-permute-start | bytes 817160 | tf_op jit(solution)/shard_map/ppermute | solution.py:36
  292.6 19.5 %collective-permute-start.43 = (bf16[1,152,896]{2,1,0:T(8,128)(2,1)S(1)}, bf16[1,152,896]{2,1,0:T(8,128)(2,1)S(1)}, u32[]{:S(2)}, u32[]{:S(2)}) collective-permute-start(bf16[1,152,896]{2,1,0:T(8,128)(2,1)S(1)} %add.281.refs_0_.refs_2_), channel_id=1, source_target_pairs={{0,16},{4,20},{8,24},{12,28},{16,0},{20,4},{24,8},{28,12},{1,17},{... | collective-permute-start | bytes 817160 | tf_op jit(solution)/shard_map/ppermute | solution.py:36
  292.8 85.0 %collective-permute-start.22 = (bf16[384,896]{1,0:T(8,128)(2,1)}, bf16[384,896]{1,0:T(8,128)(2,1)}, u32[]{:S(2)}, u32[]{:S(2)}) collective-permute-start(bf16[384,896]{1,0:T(8,128)(2,1)} %get-tuple-element.64), channel_id=1, source_target_pairs={{0,1},{1,0},{2,3},{3,2},{4,5},{5,4},{6,7},{7,6},{8,9},{9,8},{10,11... | collective-permute-start | bytes 2064392 | tf_op jit(solution)/shard_map/ppermute | solution.py:36
  292.8 47.8 %collective-permute-start.26 = (bf16[384,896]{1,0:T(8,128)(2,1)S(1)}, bf16[384,896]{1,0:T(8,128)(2,1)}, u32[]{:S(2)}, u32[]{:S(2)}) collective-permute-start(bf16[384,896]{1,0:T(8,128)(2,1)S(1)} %copy-done.50), channel_id=1, source_target_pairs={{0,1},{1,0},{2,3},{3,2},{4,5},{5,4},{6,7},{7,6},{8,9},{9,8},{10,11... | collective-permute-start | bytes 2064392 | tf_op jit(solution)/shard_map/ppermute | solution.py:36
  293.3 52.7 %all-to-all-start = ((bf16[8,32,2048]{2,1,0:T(8,128)(2,1)}), bf16[8,32,2048]{2,1,0:T(8,128)(2,1)}, u32[]{:S(2)}, u32[]{:S(2)}) async-start(bf16[8,32,2048]{2,1,0:T(8,128)(2,1)} %bitcast.51), calls=%async_computation | async-start | bytes 2097152 | tf_op jit(solution)/shard_map/all_to_all | solution.py:1078
  312.7 25.6 %collective-permute-start.46 = (bf16[2,1,152,896]{3,2,0,1:T(8,128)(2,1)S(1)}, bf16[2,1,152,896]{3,2,0,1:T(8,128)(2,1)S(1)}, u32[]{:S(2)}, u32[]{:S(2)}) collective-permute-start(bf16[2,1,152,896]{3,2,0,1:T(8,128)(2,1)S(1)} %bitcast.223), channel_id=1, source_target_pairs={{0,8},{4,12},{8,0},{12,4},{16,24},{20,28},{24,16},{28,20},{1,9},{5... | collective-permute-start | bytes 1634312 | tf_op jit(solution)/shard_map/ppermute | solution.py:36
  322.1 21.5 %collective-permute-start.44 = (bf16[4,56,640]{2,1,0:T(8,128)(2,1)S(1)}, bf16[4,56,640]{2,1,0:T(8,128)(2,1)S(1)}, u32[]{:S(2)}, u32[]{:S(2)}) collective-permute-start(bf16[4,56,640]{2,1,0:T(8,128)(2,1)S(1)} %bitcast.231), channel_id=1, source_target_pairs={{0,16},{4,20},{8,24},{12,28},{16,0},{20,4},{24,8},{28,12},{1,17},{... | collective-permute-start | bytes 860168 | tf_op jit(solution)/shard_map/ppermute | solution.py:36
  326.4 16.5 %collective-permute-start.45 = (bf16[4,56,640]{2,1,0:T(8,128)(2,1)S(1)}, bf16[4,56,640]{2,1,0:T(8,128)(2,1)S(1)}, u32[]{:S(2)}, u32[]{:S(2)}) collective-permute-start(bf16[4,56,640]{2,1,0:T(8,128)(2,1)S(1)} %bitcast.228), channel_id=1, source_target_pairs={{0,4},{4,0},{8,12},{12,8},{16,20},{20,16},{24,28},{28,24},{1,5},{5... | collective-permute-start | bytes 860168 | tf_op jit(solution)/shard_map/ppermute | solution.py:36
  339.1 48.5 %collective-permute-start.51 = (bf16[2,2,1,152,896]{4,3,2,1,0:T(8,128)(2,1)S(1)}, bf16[2,2,1,152,896]{4,3,2,1,0:T(8,128)(2,1)}, u32[]{:S(2)}, u32[]{:S(2)}) collective-permute-start(bf16[2,2,1,152,896]{4,3,2,1,0:T(8,128)(2,1)S(1)} %bitcast.204), channel_id=1, source_target_pairs={{0,4},{4,0},{8,12},{12,8},{16,20},{20,16},{24,28},{28,24},{1,5},{5... | collective-permute-start | bytes 3268616 | tf_op jit(solution)/shard_map/ppermute | solution.py:36
  342.8 35.0 %collective-permute-start.27 = (bf16[384,896]{1,0:T(8,128)(2,1)}, bf16[384,896]{1,0:T(8,128)(2,1)}, u32[]{:S(2)}, u32[]{:S(2)}) collective-permute-start(bf16[384,896]{1,0:T(8,128)(2,1)} %add_convert_fusion.3), channel_id=1, source_target_pairs={{0,2},{1,3},{2,0},{3,1},{4,6},{5,7},{6,4},{7,5},{8,10},{9,11},{10,... | collective-permute-start | bytes 2064392 | tf_op jit(solution)/shard_map/ppermute | solution.py:36
  344.4 24.3 %collective-permute-start.47 = (bf16[2,4,56,640]{3,2,1,0:T(8,128)(2,1)S(1)}, bf16[2,4,56,640]{3,2,1,0:T(8,128)(2,1)S(1)}, u32[]{:S(2)}, u32[]{:S(2)}) collective-permute-start(bf16[2,4,56,640]{3,2,1,0:T(8,128)(2,1)S(1)} %place.17.refs_1_), channel_id=1, source_target_pairs={{0,8},{4,12},{8,0},{12,4},{16,24},{20,28},{24,16},{28,20},{1,9},{5... | collective-permute-start | bytes 1720328 | tf_op jit(solution)/shard_map/ppermute | solution.py:36
  344.4 27.7 %collective-permute-start.49 = (bf16[2,4,56,640]{3,2,1,0:T(8,128)(2,1)S(1)}, bf16[2,4,56,640]{3,2,1,0:T(8,128)(2,1)}, u32[]{:S(2)}, u32[]{:S(2)}) collective-permute-start(bf16[2,4,56,640]{3,2,1,0:T(8,128)(2,1)S(1)} %place.16.refs_2_), channel_id=1, source_target_pairs={{0,16},{4,20},{8,24},{12,28},{16,0},{20,4},{24,8},{28,12},{1,17},{... | collective-permute-start | bytes 1720328 | tf_op jit(solution)/shard_map/ppermute | solution.py:36
  377.8 39.8 %collective-permute-start.50 = (bf16[2,2,4,56,640]{4,3,2,1,0:T(8,128)(2,1)}, bf16[2,2,4,56,640]{4,3,2,1,0:T(8,128)(2,1)}, u32[]{:S(2)}, u32[]{:S(2)}) collective-permute-start(bf16[2,2,4,56,640]{4,3,2,1,0:T(8,128)(2,1)} %bitcast.86), channel_id=1, source_target_pairs={{0,8},{4,12},{8,0},{12,4},{16,24},{20,28},{24,16},{28,20},{1,9},{5... | collective-permute-start | bytes 3440648 | tf_op jit(solution)/shard_map/ppermute | solution.py:36
  380.7 52.7 %all-to-all-start.1 = ((bf16[8,32,2048]{2,1,0:T(8,128)(2,1)}), bf16[8,32,2048]{2,1,0:T(8,128)(2,1)S(1)}, u32[]{:S(2)}, u32[]{:S(2)}) async-start(bf16[8,32,2048]{2,1,0:T(8,128)(2,1)} %sum_and_spread.1.refs_2_), calls=%async_computation.2 | async-start | bytes 2097152 | tf_op jit(solution)/shard_map/all_to_all | solution.py:1104
  385.6 36.9 %collective-permute-start.48 = (bf16[2,2,4,56,640]{4,3,2,1,0:T(8,128)(2,1)S(1)}, bf16[2,2,4,56,640]{4,3,2,1,0:T(8,128)(2,1)S(1)}, u32[]{:S(2)}, u32[]{:S(2)}) collective-permute-start(bf16[2,2,4,56,640]{4,3,2,1,0:T(8,128)(2,1)S(1)} %bitcast.202), channel_id=1, source_target_pairs={{0,4},{4,0},{8,12},{12,8},{16,20},{20,16},{24,28},{28,24},{1,5},{5... | collective-permute-start | bytes 3440648 | tf_op jit(solution)/shard_map/ppermute | solution.py:36
  (89 other events, 796.3 us)
Sparse Core Ops, SparseCore 0:
  165.6 96.6 reduce-scatter.1

commit v3 on v2

--- a/solution.py
+++ b/solution.py
@@ -1025,11 +1025,11 @@
         [f32(rows, width), bf16(rows, width), f32(1, width)],
     )
     line.mark(grad_mixed)
-    next(down_steps)
     dq, *dkv = attention_backward(
         bounds, qt, ot, lse, grad_mixed, cos_t, sin_t, start_row, blocks, line.last
     )
     line.mark(dq)
+    next(down_steps)
     dkv_steps = steps_of_scatter(dict(enumerate(dkv)), "seq")
     next(dkv_steps)
     for _ in range(levels - 1):
@@ -1076,8 +1076,6 @@
                 next(down_steps)
         joint = {r: line.mark(add(joint[r][None], v, line.last))[0] for r, v in got.items()}
     joint = lax.all_to_all(joint[0], "dp", 0, 0, tiled=True)
-    next(down_steps)
-    next(down_steps)
     moved = [pick(grad_gu, order[r]) for r in range(group)]
     moved = [swap(v, "seq", r) if r else v for r, v in enumerate(moved)]
     columns = inner // 2
@@ -1094,6 +1092,8 @@
     next(out_steps)
     next(second_steps)
     next(first_steps)
+    next(down_steps)
+    next(down_steps)
     shape = (total, joint_rows // total, joint_width)
 
     def spread(_, x, out):

time: 450 us -> 465 us (1.033)
  waiting for transfers between devices: 168 us -> 183 us
  starting transfers between devices: 75.5 us -> 70.1 us
    ppermute x52, waiting for transfers between devices: 168 us -> 183 us  [swap(): lax.ppermute(x, axis, [(i, i ^ mask) for i in range(lax.axis_size(axis))])]
    unnamed x132 -> x130, local copies, waits for them, and re-layouts: 25.7 us -> 24.2 us
  transfers between devices with their start and end apart: 55 -> 55, of which waited for: 26 -> 24; matrix products, arithmetic and copies ran while one was open for 9% -> 9% of each run, Pallas kernels for 18% -> 18%
where the time goes in v3:
time: 465 us; the launch traced here: 459 us
  waiting for transfers between devices  183 us (39%)
  Pallas kernels  119 us (26%)
  starting transfers between devices  70.1 us (15%)
  local copies, waits for them, and re-layouts  42.3 us (9%)
  other arithmetic  29.4 us (6%)
  between operations  15.3 us (3%)
    ppermute x52, waiting for transfers between devices, swap(): lax.ppermute(x, axis, [(i, i ^ mask) for i in range(lax.axis_size(axis))])  183 us
    ppermute x52, starting transfers between devices, swap(): lax.ppermute(x, axis, [(i, i ^ mask) for i in range(lax.axis_size(axis))])  61.6 us
    pallas_call x2, Pallas kernels, feed(): pl.pallas_call(functools.partial(feed_kernel, blocks), out_shape=(tall, w...  37.2 us
    unnamed x130, local copies, waits for them, and re-layouts  24.2 us
    pallas_call x16, Pallas kernels, small_call(): pl.pallas_call(body, out_shape=out_shape, grid_spec=pltpu.PrefetchScalarG...  19.4 us
    pallas_call x4, Pallas kernels, single_call(): pl.pallas_call(body, out_shape=outs, grid_spec=pltpu.PrefetchScalarGridSp...  15.7 us
    pallas_call x1, Pallas kernels, grad_gate_up_of(): pl.pallas_call(functools.partial(gate_up_kernel, len(grads), len(hiddens)...  12.4 us
    pallas_call x1, Pallas kernels, grad_down_of(): pl.pallas_call(functools.partial(down_kernel, len(products), len(cots) //...  10.5 us
  transfers between devices with their start and end apart: 55, of which 24 were waited for; matrix products, arithmetic and copies ran while one was open for 9% of the time, Pallas kernels for 18%

profile of v3, /device:TPU:0, one launch (start us, length us, event | category | flops | bytes accessed | tf_op | source)
XLA Modules:
  0.0 459.0 jit_solution(14457520504336159330)
XLA Ops:
  20.3 5.8 %collective-permute-done.4.rest_2_ = bf16[224,1152]{1,0:T(8,128)(2,1)} collective-permute-done((bf16[224,1152]{1,0:T(8,128)(2,1)}, bf16[224,1152]{1,0:T(8,128)(2,1)}, u32[]{:S(2)}, u32[]{:S(2)}) %collective-permute-start.4) | collective-permute-done | bytes 516128 | tf_op jit(solution)/shard_map/ppermute | solution.py:36
  31.8 3.9 norm_project_rotate.1
  45.7 6.7 %collective-permute-done.12.rest_2_ = bf16[224,896]{1,0:T(8,128)(2,1)S(1)} collective-permute-done((bf16[224,896]{1,0:T(8,128)(2,1)}, bf16[224,896]{1,0:T(8,128)(2,1)S(1)}, u32[]{:S(2)}, u32[]{:S(2)}) %collective-permute-start.12) | collective-permute-done | bytes 401440 | tf_op jit(solution)/shard_map/ppermute | solution.py:36
  58.1 3.8 collective-permute-done.14
  65.2 7.2 %attention_forward.1 = (bf16[384,896]{1,0:T(8,128)(2,1)S(1)}, bf16[3,2,64,896]{3,2,1,0:T(8,128)(2,1)S(1)}, bf16[3,2,64,896]{3,2,1,0:T(8,128)(2,1)S(1)}, f32[3,2,1,896]{3,2,1,0:T(1,128)S(1)}) custom-call(s32[10]{0:T(128)S(1)} %pad_add_fusion.2.bounds, f32[384,896]{1,0:T(8,128)S(1)} %copy-done.22, f32[32,384]{1,0:T(8,128)S(1)} %get-tuple-element.149.cos_ref, ...), custom_call_target="tpu_custom_call" | custom-call | flops 4194304 | bytes 262144 | tf_op jit(solution)/shard_map/attention_forward/pallas_call | solution.py:246
  74.2 3.0 project_add_norm.1
  77.2 8.7 %collective-permute-start.17 = (bf16[384,896]{1,0:T(8,128)(2,1)S(1)}, bf16[384,896]{1,0:T(8,128)(2,1)S(1)}, u32[]{:S(2)}, u32[]{:S(2)}) collective-permute-start(bf16[384,896]{1,0:T(8,128)(2,1)S(1)} %get-tuple-element.61.refs_0_.refs_2_), channel_id=1, source_target_pairs={{0,2},{1,3},{2,0},{3,1},{4,6},{5,7},{6,4},{7,5},{8,10},{9,11},{10,... | collective-permute-start | bytes 2064392 | tf_op jit(solution)/shard_map/ppermute | solution.py:36
  87.9 11.3 %collective-permute-done.17.refs_0_.refs_4_ = bf16[384,896]{1,0:T(8,128)(2,1)S(1)} collective-permute-done((bf16[384,896]{1,0:T(8,128)(2,1)S(1)}, bf16[384,896]{1,0:T(8,128)(2,1)S(1)}, u32[]{:S(2)}, u32[]{:S(2)}) %collective-permute-start.17) | collective-permute-done | bytes 688160 | tf_op jit(solution)/shard_map/ppermute | solution.py:36
  104.3 4.7 %collective-permute-done.21.refs_9_ = bf16[2,112,1280]{2,1,0:T(8,128)(2,1)S(1)} collective-permute-done((bf16[2,112,1280]{2,1,0:T(8,128)(2,1)S(1)}, bf16[2,112,1280]{2,1,0:T(8,128)(2,1)S(1)}, u32[]{:S(2)}, u32[]{:S(2)}) %collective-permute-start.21) | collective-permute-done | bytes 573472 | tf_op jit(solution)/shard_map/ppermute | solution.py:36
  109.9 2.7 collective-permute-done.24.refs_2_.refs_4_
  116.3 18.8 %feed_forward_backward.2 = (bf16[1280,768]{1,0:T(8,128)(2,1)}, bf16[2,768,1280]{2,1,0:T(8,128)(2,1)}, bf16[384,896]{1,0:T(8,128)(2,1)S(1)}, bf16[384,896]{1,0:T(...) custom-call(s32[6]{0:T(128)S(1)} %stack.157.offsets, ...), custom_call_target="tpu_custom_call" | custom-call | flops 4194304 | bytes 262144 | tf_op jit(solution)/shard_map/feed_forward_backward/pallas_call | solution.py:489
  136.0 18.3 %feed_forward_backward.3 = (bf16[1280,768]{1,0:T(8,128)(2,1)}, bf16[2,768,1280]{2,1,0:T(8,128)(2,1)}, bf16[384,896]{1,0:T(8,128)(2,1)S(1)}, bf16[384,896]{1,0:T(...) custom-call(s32[6]{0:T(128)S(1)} %stack.157.offsets, ...), custom_call_target="tpu_custom_call" | custom-call | flops 4194304 | bytes 262144 | tf_op jit(solution)/shard_map/feed_forward_backward/pallas_call | solution.py:489
  156.9 12.4 %grad_gate_up.1.refs_6_ = bf16[8,4,56,1280]{3,2,1,0:T(8,128)(2,1)} custom-call(bf16[2,768,1280]{2,1,0:T(8,128)(2,1)} %get-tuple-element.78.refs_0_, bf16[2,768,1280]{2,1,0:T(8,128)(2,1)} %get-tuple-element.79.refs_1_, bf16[384,896]{1,0:T(8,128)(2,1)} %copy-done.6, bf16[384,896]{1,0:T(8,128)(2,1)} %collective-permute-done.16.refs_1_.refs_3_, ...), custom_call_target="tpu_custom_call" | custom-call | flops 4194304 | bytes 262144 | tf_op jit(solution)/shard_map/grad_gate_up/pallas_call | solution.py:602
  176.1 10.5 %grad_down.1 = (bf16[608,896]{1,0:T(8,128)(2,1)}, bf16[608,896]{1,0:T(8,128)(2,1)}) custom-call(s32[2]{0:T(128)} %fusion.9.offsets, bf16[1280,768]{1,0:T(8,128)(2,1)} %get-tuple-element.76.refs_0_, bf16[1280,768]{1,0:T(8,128)(2,1)} %get-tuple-element.77.refs_1_, bf16[384,896]{1,0:T(8,128)(2,1)} %bitcast.28.refs_2_, bf16[384,896]{1,0:T(8,128)(2,1)} %copy-done.57, ...), custom_call_target="tpu_custom_call" | custom-call | flops 4194304 | bytes 262144 | tf_op jit(solution)/shard_map/grad_down/pallas_call | solution.py:549
  188.3 3.2 collective-permute-done.30.refs_1_
  192.4 4.4 norm_back.1
  196.9 9.2 %attention_backward.1 = (bf16[384,896]{1,0:T(8,128)(2,1)S(1)}, bf16[384,256]{1,0:T(8,128)(2,1)S(1)}, bf16[384,256]{1,0:T(8,128)(2,1)S(1)}, bf16[384,256]{1,0:T(8,128)(2,1)S(1)}, bf16[384,256]{1,0:T(8,128)(2,1)}) custom-call(s32[10]{0:T(128)S(1)} %pad_add_fusion.2.bounds, bf16[3,2,64,896]{3,2,1,0:T(8,128)(2,1)S(1)} %copy-done.35, ...), custom_call_target="tpu_custom_call" | custom-call | flops 4194304 | bytes 262144 | tf_op jit(solution)/shard_map/attention_backward/pallas_call | solution.py:296
  209.7 9.3 %collective-permute-start.33 = (bf16[384,256]{1,0:T(8,128)(2,1)S(1)}, bf16[384,256]{1,0:T(8,128)(2,1)S(1)}, u32[]{:S(2)}, u32[]{:S(2)}) collective-permute-start(bf16[384,256]{1,0:T(8,128)(2,1)S(1)} %add_convert_fusion.5), channel_id=1, source_target_pairs={{0,2},{1,3},{2,0},{3,1},{4,6},{5,7},{6,4},{7,5},{8,10},{9,11},{10,... | collective-permute-start | bytes 589832 | tf_op jit(solution)/shard_map/ppermute | solution.py:36
  221.4 2.8 collective-permute-done.33.refs_5_
  224.2 8.9 %project_back.1 = (f32[384,896]{1,0:T(8,128)}, f32[1,896]{1,0:T(1,128)S(1)}, f32[1,1152]{1,0:T(1,128)S(1)}, bf16[256,2048]{1,0:T(8,128)(2,1)}, bf16[256,2048]{1,...) custom-call(s32[4]{0:T(128)S(1)} %get-tuple-element.102.scalar_ref, bf16[384,896]{1,0:T(8,128)(2,1)} %bitcast.214, ...), custom_call_target="tpu_custom_call" | custom-call | flops 4194304 | bytes 262144 | tf_op jit(solution)/shard_map/project_back/pallas_call | solution.py:639
  248.3 29.7 %collective-permute-done.38 = bf16[1,304,896]{2,1,0:T(8,128)(2,1)S(1)} collective-permute-done((bf16[1,304,896]{2,1,0:T(8,128)(2,1)}, bf16[1,304,896]{2,1,0:T(8,128)(2,1)S(1)}, u32[]{:S(2)}, u32[]{:S(2)}) %collective-permute-start.38) | collective-permute-done | bytes 544800 | tf_op jit(solution)/shard_map/ppermute | solution.py:36
  281.8 4.6 all-to-all-start
  289.5 4.2 collective-permute-done.42
  293.7 3.1 collective-permute-done.41
  303.3 11.0 %collective-permute-done.45.refs_1_ = bf16[4,56,640]{2,1,0:T(8,128)(2,1)S(1)} collective-permute-done((bf16[4,56,640]{2,1,0:T(8,128)(2,1)S(1)}, bf16[4,56,640]{2,1,0:T(8,128)(2,1)S(1)}, u32[]{:S(2)}, u32[]{:S(2)}) %collective-permute-start.45) | collective-permute-done | bytes 286752 | tf_op jit(solution)/shard_map/ppermute | solution.py:36
  315.0 19.7 %collective-permute-done.44.refs_1_ = bf16[4,56,640]{2,1,0:T(8,128)(2,1)S(1)} collective-permute-done((bf16[4,56,640]{2,1,0:T(8,128)(2,1)S(1)}, bf16[4,56,640]{2,1,0:T(8,128)(2,1)S(1)}, u32[]{:S(2)}, u32[]{:S(2)}) %collective-permute-start.44) | collective-permute-done | bytes 286752 | tf_op jit(solution)/shard_map/ppermute | solution.py:36
  335.4 5.0 %collective-permute-done.43.refs_1_ = bf16[1,152,896]{2,1,0:T(8,128)(2,1)S(1)} collective-permute-done((bf16[1,152,896]{2,1,0:T(8,128)(2,1)S(1)}, bf16[1,152,896]{2,1,0:T(8,128)(2,1)S(1)}, u32[]{:S(2)}, u32[]{:S(2)}) %collective-permute-start.43) | collective-permute-done | bytes 272416 | tf_op jit(solution)/shard_map/ppermute | solution.py:36
  341.2 14.2 %collective-permute-done.46 = bf16[2,1,152,896]{3,2,0,1:T(8,128)(2,1)S(1)} collective-permute-done((bf16[2,1,152,896]{3,2,0,1:T(8,128)(2,1)S(1)}, bf16[2,1,152,896]{3,2,0,1:T(8,128)(2,1)S(1)}, u32[]{:S(2)}, u32[]{:S(2)}) %collective-permute-start.46) | collective-permute-done | bytes 544800 | tf_op jit(solution)/shard_map/ppermute | solution.py:36
  366.5 20.3 %collective-permute-done.47 = bf16[2,4,56,640]{3,2,1,0:T(8,128)(2,1)S(1)} collective-permute-done((bf16[2,4,56,640]{3,2,1,0:T(8,128)(2,1)S(1)}, bf16[2,4,56,640]{3,2,1,0:T(8,128)(2,1)S(1)}, u32[]{:S(2)}, u32[]{:S(2)}) %collective-permute-start.47) | collective-permute-done | bytes 573472 | tf_op jit(solution)/shard_map/ppermute | solution.py:36
  389.0 5.6 %place.19 = bf16[2,8,56,640]{3,2,1,0:T(8,128)(2,1)} custom-call(s32[2]{0:T(128)S(1)} %pad_add_fusion.5.scalar_ref, bf16[8,56,640]{2,1,0:T(8,128)(2,1)S(1)} %bitcast.218, bf16[8,56,640]{2,1,0:T(8,128)(2,1)} %bitcast.85.refs_1_, bf16[2,2,4,56,640]{4,3,2,1,0:T(8,128)(2,1)S(1)} %bitcast.201), custom_call_target="tpu_custom_call" | custom-call | flops 1048576 | bytes 262144 | tf_op jit(solution)/shard_map/place/pallas_call | solution.py:714
  397.4 3.9 all-to-all-start.1
  407.5 25.8 %collective-permute-done.50 = bf16[2,2,4,56,640]{4,3,2,1,0:T(8,128)(2,1)} collective-permute-done((bf16[2,2,4,56,640]{4,3,2,1,0:T(8,128)(2,1)}, bf16[2,2,4,56,640]{4,3,2,1,0:T(8,128)(2,1)}, u32[]{:S(2)}, u32[]{:S(2)}) %collective-permute-start.50) | collective-permute-done | bytes 1146912 | tf_op jit(solution)/shard_map/ppermute | solution.py:36
  (341 shorter events, 140.8 us)
Async XLA Ops:
  7.2 279.2 %reduce-scatter.2.cloned.1.call-start = ((), (), s32[]{:S(2)}) async-start(), calls=%async_computation.3 | async-start | bytes 5160960 | tf_op jit(solution)/shard_map/reduce_scatter | solution.py:1014
  8.6 22.0 %collective-permute-start.2 = (bf16[1,736]{1,0:T(2,128)(2,1)}, bf16[1,736]{1,0:T(2,128)(2,1)}, u32[]{:S(2)}, u32[]{:S(2)}) collective-permute-start(bf16[1,736]{1,0:T(2,128)(2,1)} %broadcast_in_dim.50), channel_id=1, source_target_pairs={{0,3},{1,2},{2,1},{3,0},{4,7},{5,6},{6,5},{7,4},{8,11},{9,10},{10,... | collective-permute-start | bytes 4424 | tf_op jit(solution)/shard_map/ppermute | solution.py:36
  11.0 18.6 %collective-permute-start.1 = (bf16[1,736]{1,0:T(2,128)(2,1)}, bf16[1,736]{1,0:T(2,128)(2,1)}, u32[]{:S(2)}, u32[]{:S(2)}) collective-permute-start(bf16[1,736]{1,0:T(2,128)(2,1)} %broadcast_in_dim.50), channel_id=1, source_target_pairs={{0,2},{1,3},{2,0},{3,1},{4,6},{5,7},{6,4},{7,5},{8,10},{9,11},{10,... | collective-permute-start | bytes 4424 | tf_op jit(solution)/shard_map/ppermute | solution.py:36
  11.6 16.0 %collective-permute-start = (bf16[1,736]{1,0:T(2,128)(2,1)}, bf16[1,736]{1,0:T(2,128)(2,1)S(1)}, u32[]{:S(2)}, u32[]{:S(2)}) collective-permute-start(bf16[1,736]{1,0:T(2,128)(2,1)} %broadcast_in_dim.50), channel_id=1, source_target_pairs={{0,1},{1,0},{2,3},{3,2},{4,5},{5,4},{6,7},{7,6},{8,9},{9,8},{10,11... | collective-permute-start | bytes 4424 | tf_op jit(solution)/shard_map/ppermute | solution.py:36
  11.6 20.0 %collective-permute-start.3 = (bf16[224,1152]{1,0:T(8,128)(2,1)}, bf16[224,1152]{1,0:T(8,128)(2,1)S(1)}, u32[]{:S(2)}, u32[]{:S(2)}) collective-permute-start(bf16[224,1152]{1,0:T(8,128)(2,1)} %rest_0_.1), channel_id=1, source_target_pairs={{0,1},{1,0},{2,3},{3,2},{4,5},{5,4},{6,7},{7,6},{8,9},{9,8},{10,11... | collective-permute-start | bytes 1548296 | tf_op jit(solution)/shard_map/ppermute | solution.py:36
  42.7 31.4 %collective-permute-start.11 = (bf16[224,896]{1,0:T(8,128)(2,1)}, bf16[224,896]{1,0:T(8,128)(2,1)}, u32[]{:S(2)}, u32[]{:S(2)}) collective-permute-start(bf16[224,896]{1,0:T(8,128)(2,1)} %get-tuple-element.59.rest_0_), channel_id=1, source_target_pairs={{0,1},{1,0},{2,3},{3,2},{4,5},{5,4},{6,7},{7,6},{8,9},{9,8},{10,11... | collective-permute-start | bytes 1204232 | tf_op jit(solution)/shard_map/ppermute | solution.py:36
  52.4 21.8 %collective-permute-start.13 = (bf16[224,896]{1,0:T(8,128)(2,1)S(1)}, bf16[224,896]{1,0:T(8,128)(2,1)}, u32[]{:S(2)}, u32[]{:S(2)}) collective-permute-start(bf16[224,896]{1,0:T(8,128)(2,1)S(1)} %collective-permute-done.12.rest_2_), channel_id=1, source_target_pairs={{0,1},{1,0},{2,3},{3,2},{4,5},{5,4},{6,7},{7,6},{8,9},{9,8},{10,11... | collective-permute-start | bytes 1204232 | tf_op jit(solution)/shard_map/ppermute | solution.py:36
  77.2 22.0 %collective-permute-start.17 = (bf16[384,896]{1,0:T(8,128)(2,1)S(1)}, bf16[384,896]{1,0:T(8,128)(2,1)S(1)}, u32[]{:S(2)}, u32[]{:S(2)}) collective-permute-start(bf16[384,896]{1,0:T(8,128)(2,1)S(1)} %get-tuple-element.61.refs_0_.refs_2_), channel_id=1, source_target_pairs={{0,2},{1,3},{2,0},{3,1},{4,6},{5,7},{6,4},{7,5},{8,10},{9,11},{10,... | collective-permute-start | bytes 2064392 | tf_op jit(solution)/shard_map/ppermute | solution.py:36
  85.9 17.5 %collective-permute-start.20 = (bf16[2,112,1280]{2,1,0:T(8,128)(2,1)S(1)}, bf16[2,112,1280]{2,1,0:T(8,128)(2,1)S(1)}, u32[]{:S(2)}, u32[]{:S(2)}) collective-permute-start(bf16[2,112,1280]{2,1,0:T(8,128)(2,1)S(1)} %bitcast.211), channel_id=1, source_target_pairs={{0,4},{4,0},{8,12},{12,8},{16,20},{20,16},{24,28},{28,24},{1,5},{5... | collective-permute-start | bytes 1720328 | tf_op jit(solution)/shard_map/ppermute | solution.py:36
  87.4 21.6 %collective-permute-start.21 = (bf16[2,112,1280]{2,1,0:T(8,128)(2,1)S(1)}, bf16[2,112,1280]{2,1,0:T(8,128)(2,1)S(1)}, u32[]{:S(2)}, u32[]{:S(2)}) collective-permute-start(bf16[2,112,1280]{2,1,0:T(8,128)(2,1)S(1)} %bitcast.207), channel_id=1, source_target_pairs={{0,4},{4,0},{8,12},{12,8},{16,20},{20,16},{24,28},{28,24},{1,5},{5... | collective-permute-start | bytes 1720328 | tf_op jit(solution)/shard_map/ppermute | solution.py:36
  109.9 26.1 %collective-permute-start.23 = (bf16[384,896]{1,0:T(8,128)(2,1)S(1)}, bf16[384,896]{1,0:T(8,128)(2,1)}, u32[]{:S(2)}, u32[]{:S(2)}) collective-permute-start(bf16[384,896]{1,0:T(8,128)(2,1)S(1)} %collective-permute-done.17.refs_0_.refs_4_), channel_id=1, source_target_pairs={{0,1},{1,0},{2,3},{3,2},{4,5},{5,4},{6,7},{7,6},{8,9},{9,8},{10,11... | collective-permute-start | bytes 2064392 | tf_op jit(solution)/shard_map/ppermute | solution.py:36
  112.6 23.4 %collective-permute-start.25 = (bf16[384,896]{1,0:T(8,128)(2,1)}, bf16[384,896]{1,0:T(8,128)(2,1)}, u32[]{:S(2)}, u32[]{:S(2)}) collective-permute-start(bf16[384,896]{1,0:T(8,128)(2,1)} %collective-permute-done.24.refs_2_.refs_4_), channel_id=1, source_target_pairs={{0,1},{1,0},{2,3},{3,2},{4,5},{5,4},{6,7},{7,6},{8,9},{9,8},{10,11... | collective-permute-start | bytes 2064392 | tf_op jit(solution)/shard_map/ppermute | solution.py:36
  170.9 17.3 %collective-permute-start.28 = (bf16[384,896]{1,0:T(8,128)(2,1)}, bf16[384,896]{1,0:T(8,128)(2,1)S(1)}, u32[]{:S(2)}, u32[]{:S(2)}) collective-permute-start(bf16[384,896]{1,0:T(8,128)(2,1)} %get-tuple-element.72), channel_id=1, source_target_pairs={{0,1},{1,0},{2,3},{3,2},{4,5},{5,4},{6,7},{7,6},{8,9},{9,8},{10,11... | collective-permute-start | bytes 2064392 | tf_op jit(solution)/shard_map/ppermute | solution.py:36
  173.8 17.8 %collective-permute-start.30 = (bf16[384,896]{1,0:T(8,128)(2,1)S(1)}, bf16[384,896]{1,0:T(8,128)(2,1)S(1)}, u32[]{:S(2)}, u32[]{:S(2)}) collective-permute-start(bf16[384,896]{1,0:T(8,128)(2,1)S(1)} %add_convert_fusion.refs_7_), channel_id=1, source_target_pairs={{0,2},{1,3},{2,0},{3,1},{4,6},{5,7},{6,4},{7,5},{8,10},{9,11},{10,... | collective-permute-start | bytes 2064392 | tf_op jit(solution)/shard_map/ppermute | solution.py:36
  186.7 33.8 %collective-permute-start.34 = (bf16[608,896]{1,0:T(8,128)(2,1)}, bf16[608,896]{1,0:T(8,128)(2,1)S(1)}, u32[]{:S(2)}, u32[]{:S(2)}) collective-permute-start(bf16[608,896]{1,0:T(8,128)(2,1)} %get-tuple-element.89), channel_id=1, source_target_pairs={{0,4},{4,0},{8,12},{12,8},{16,20},{20,16},{24,28},{28,24},{1,5},{5... | collective-permute-start | bytes 3268616 | tf_op jit(solution)/shard_map/ppermute | solution.py:36
  209.7 14.5 %collective-permute-start.33 = (bf16[384,256]{1,0:T(8,128)(2,1)S(1)}, bf16[384,256]{1,0:T(8,128)(2,1)S(1)}, u32[]{:S(2)}, u32[]{:S(2)}) collective-permute-start(bf16[384,256]{1,0:T(8,128)(2,1)S(1)} %add_convert_fusion.5), channel_id=1, source_target_pairs={{0,2},{1,3},{2,0},{3,1},{4,6},{5,7},{6,4},{7,5},{8,10},{9,11},{10,... | collective-permute-start | bytes 589832 | tf_op jit(solution)/shard_map/ppermute | solution.py:36
  244.9 34.5 %collective-permute-start.37 = (bf16[256,2048]{1,0:T(8,128)(2,1)S(1)}, bf16[256,2048]{1,0:T(8,128)(2,1)}, u32[]{:S(2)}, u32[]{:S(2)}) collective-permute-start(bf16[256,2048]{1,0:T(8,128)(2,1)S(1)} %bitcast.225), channel_id=1, source_target_pairs={{0,2},{1,3},{2,0},{3,1},{4,6},{5,7},{6,4},{7,5},{8,10},{9,11},{10,... | collective-permute-start | bytes 3145736 | tf_op jit(solution)/shard_map/ppermute | solution.py:36
  246.7 31.3 %collective-permute-start.38 = (bf16[1,304,896]{2,1,0:T(8,128)(2,1)}, bf16[1,304,896]{2,1,0:T(8,128)(2,1)S(1)}, u32[]{:S(2)}, u32[]{:S(2)}) collective-permute-start(bf16[1,304,896]{2,1,0:T(8,128)(2,1)} %get-tuple-element.99), channel_id=1, source_target_pairs={{0,8},{4,12},{8,0},{12,4},{16,24},{20,28},{24,16},{28,20},{1,9},{5... | collective-permute-start | bytes 1634312 | tf_op jit(solution)/shard_map/ppermute | solution.py:36
  278.8 23.6 %collective-permute-start.39 = (bf16[1,152,896]{2,1,0:T(8,128)(2,1)}, bf16[1,152,896]{2,1,0:T(8,128)(2,1)S(1)}, u32[]{:S(2)}, u32[]{:S(2)}) collective-permute-start(bf16[1,152,896]{2,1,0:T(8,128)(2,1)} %get-tuple-element.101), channel_id=1, source_target_pairs={{0,16},{4,20},{8,24},{12,28},{16,0},{20,4},{24,8},{28,12},{1,17},{... | collective-permute-start | bytes 817160 | tf_op jit(solution)/shard_map/ppermute | solution.py:36
  281.8 82.4 %all-to-all-start = ((bf16[8,32,2048]{2,1,0:T(8,128)(2,1)}), bf16[8,32,2048]{2,1,0:T(8,128)(2,1)}, u32[]{:S(2)}, u32[]{:S(2)}) async-start(bf16[8,32,2048]{2,1,0:T(8,128)(2,1)} %bitcast.51), calls=%async_computation | async-start | bytes 2097152 | tf_op jit(solution)/shard_map/all_to_all | solution.py:1078
  298.0 16.2 %collective-permute-start.45 = (bf16[4,56,640]{2,1,0:T(8,128)(2,1)S(1)}, bf16[4,56,640]{2,1,0:T(8,128)(2,1)S(1)}, u32[]{:S(2)}, u32[]{:S(2)}) collective-permute-start(bf16[4,56,640]{2,1,0:T(8,128)(2,1)S(1)} %bitcast.229), channel_id=1, source_target_pairs={{0,4},{4,0},{8,12},{12,8},{16,20},{20,16},{24,28},{28,24},{1,5},{5... | collective-permute-start | bytes 860168 | tf_op jit(solution)/shard_map/ppermute | solution.py:36
  300.1 34.6 %collective-permute-start.44 = (bf16[4,56,640]{2,1,0:T(8,128)(2,1)S(1)}, bf16[4,56,640]{2,1,0:T(8,128)(2,1)S(1)}, u32[]{:S(2)}, u32[]{:S(2)}) collective-permute-start(bf16[4,56,640]{2,1,0:T(8,128)(2,1)S(1)} %bitcast.227), channel_id=1, source_target_pairs={{0,16},{4,20},{8,24},{12,28},{16,0},{20,4},{24,8},{28,12},{1,17},{... | collective-permute-start | bytes 860168 | tf_op jit(solution)/shard_map/ppermute | solution.py:36
  302.5 37.9 %collective-permute-start.43 = (bf16[1,152,896]{2,1,0:T(8,128)(2,1)S(1)}, bf16[1,152,896]{2,1,0:T(8,128)(2,1)S(1)}, u32[]{:S(2)}, u32[]{:S(2)}) collective-permute-start(bf16[1,152,896]{2,1,0:T(8,128)(2,1)S(1)} %add.281.refs_2_.refs_0_), channel_id=1, source_target_pairs={{0,16},{4,20},{8,24},{12,28},{16,0},{20,4},{24,8},{28,12},{1,17},{... | collective-permute-start | bytes 817160 | tf_op jit(solution)/shard_map/ppermute | solution.py:36
  303.1 55.3 %collective-permute-start.26 = (bf16[384,896]{1,0:T(8,128)(2,1)}, bf16[384,896]{1,0:T(8,128)(2,1)}, u32[]{:S(2)}, u32[]{:S(2)}) collective-permute-start(bf16[384,896]{1,0:T(8,128)(2,1)} %copy-done.49), channel_id=1, source_target_pairs={{0,1},{1,0},{2,3},{3,2},{4,5},{5,4},{6,7},{7,6},{8,9},{9,8},{10,11... | collective-permute-start | bytes 2064392 | tf_op jit(solution)/shard_map/ppermute | solution.py:36
  341.1 53.6 %collective-permute-start.22 = (bf16[384,896]{1,0:T(8,128)(2,1)}, bf16[384,896]{1,0:T(8,128)(2,1)}, u32[]{:S(2)}, u32[]{:S(2)}) collective-permute-start(bf16[384,896]{1,0:T(8,128)(2,1)} %get-tuple-element.64), channel_id=1, source_target_pairs={{0,1},{1,0},{2,3},{3,2},{4,5},{5,4},{6,7},{7,6},{8,9},{9,8},{10,11... | collective-permute-start | bytes 2064392 | tf_op jit(solution)/shard_map/ppermute | solution.py:36
  356.9 46.4 %collective-permute-start.51 = (bf16[2,2,1,152,896]{4,3,2,1,0:T(8,128)(2,1)}, bf16[2,2,1,152,896]{4,3,2,1,0:T(8,128)(2,1)}, u32[]{:S(2)}, u32[]{:S(2)}) collective-permute-start(bf16[2,2,1,152,896]{4,3,2,1,0:T(8,128)(2,1)} %bitcast.74.refs_1_), channel_id=1, source_target_pairs={{0,4},{4,0},{8,12},{12,8},{16,20},{20,16},{24,28},{28,24},{1,5},{5... | collective-permute-start | bytes 3268616 | tf_op jit(solution)/shard_map/ppermute | solution.py:36
  360.5 34.2 %collective-permute-start.27 = (bf16[384,896]{1,0:T(8,128)(2,1)}, bf16[384,896]{1,0:T(8,128)(2,1)}, u32[]{:S(2)}, u32[]{:S(2)}) collective-permute-start(bf16[384,896]{1,0:T(8,128)(2,1)} %add_convert_fusion.3), channel_id=1, source_target_pairs={{0,2},{1,3},{2,0},{3,1},{4,6},{5,7},{6,4},{7,5},{8,10},{9,11},{10,... | collective-permute-start | bytes 2064392 | tf_op jit(solution)/shard_map/ppermute | solution.py:36
  361.9 24.9 %collective-permute-start.47 = (bf16[2,4,56,640]{3,2,1,0:T(8,128)(2,1)S(1)}, bf16[2,4,56,640]{3,2,1,0:T(8,128)(2,1)S(1)}, u32[]{:S(2)}, u32[]{:S(2)}) collective-permute-start(bf16[2,4,56,640]{3,2,1,0:T(8,128)(2,1)S(1)} %place.15.refs_2_), channel_id=1, source_target_pairs={{0,8},{4,12},{8,0},{12,4},{16,24},{20,28},{24,16},{28,20},{1,9},{5... | collective-permute-start | bytes 1720328 | tf_op jit(solution)/shard_map/ppermute | solution.py:36
  362.2 26.9 %collective-permute-start.49 = (bf16[2,4,56,640]{3,2,1,0:T(8,128)(2,1)S(1)}, bf16[2,4,56,640]{3,2,1,0:T(8,128)(2,1)}, u32[]{:S(2)}, u32[]{:S(2)}) collective-permute-start(bf16[2,4,56,640]{3,2,1,0:T(8,128)(2,1)S(1)} %place.14.refs_2_), channel_id=1, source_target_pairs={{0,16},{4,20},{8,24},{12,28},{16,0},{20,4},{24,8},{28,12},{1,17},{... | collective-permute-start | bytes 1720328 | tf_op jit(solution)/shard_map/ppermute | solution.py:36
  394.7 38.6 %collective-permute-start.50 = (bf16[2,2,4,56,640]{4,3,2,1,0:T(8,128)(2,1)}, bf16[2,2,4,56,640]{4,3,2,1,0:T(8,128)(2,1)}, u32[]{:S(2)}, u32[]{:S(2)}) collective-permute-start(bf16[2,2,4,56,640]{4,3,2,1,0:T(8,128)(2,1)} %bitcast.86), channel_id=1, source_target_pairs={{0,8},{4,12},{8,0},{12,4},{16,24},{20,28},{24,16},{28,20},{1,9},{5... | collective-permute-start | bytes 3440648 | tf_op jit(solution)/shard_map/ppermute | solution.py:36
  397.4 50.9 %all-to-all-start.1 = ((bf16[8,32,2048]{2,1,0:T(8,128)(2,1)}), bf16[8,32,2048]{2,1,0:T(8,128)(2,1)S(1)}, u32[]{:S(2)}, u32[]{:S(2)}) async-start(bf16[8,32,2048]{2,1,0:T(8,128)(2,1)} %sum_and_spread.1.refs_2_), calls=%async_computation.2 | async-start | bytes 2097152 | tf_op jit(solution)/shard_map/all_to_all | solution.py:1104
  401.2 36.0 %collective-permute-start.48 = (bf16[2,2,4,56,640]{4,3,2,1,0:T(8,128)(2,1)S(1)}, bf16[2,2,4,56,640]{4,3,2,1,0:T(8,128)(2,1)S(1)}, u32[]{:S(2)}, u32[]{:S(2)}) collective-permute-start(bf16[2,2,4,56,640]{4,3,2,1,0:T(8,128)(2,1)S(1)} %bitcast.202), channel_id=1, source_target_pairs={{0,4},{4,0},{8,12},{12,8},{16,20},{20,16},{24,28},{28,24},{1,5},{5... | collective-permute-start | bytes 3440648 | tf_op jit(solution)/shard_map/ppermute | solution.py:36
  (88 other events, 826.6 us)
Sparse Core Ops, SparseCore 0:
  169.4 107.9 reduce-scatter.1
